TPU v7x, 32 devices: a whole 2x2x4 slice. The times are simulated.
32 devices in a mesh: dp: 8 (over y, x, core), fsdp: 4 (over z).
Axes of the slice: x: 2, y: 2, z: 4, core: 2. Of those that a mesh axis runs over, the one named last changes fastest.
Arguments:
- tokens: bfloat16 [32768, 1024], P(('dp', 'fsdp')), may hold values from -6 to 6
- out_grad: bfloat16 [32768, 1024], P(('dp', 'fsdp')), may hold values from -6 to 6
- domain_ids: int32 [32768], P(('dp', 'fsdp')), may hold values from 0 to 15
- domain_scale: float32 [16], replicated, may hold values from 0.5 to 2
- attn_in: float32 [1024, 1536], P(('dp', 'fsdp')), may hold values from -0.1875 to 0.1875
- latent_expand_weight: float32 [512, 1024], P(('dp', 'fsdp')), may hold values from -0.375 to 0.375
- attn_out: float32 [1024, 1024], P(('dp', 'fsdp')), may hold values from -1.5 to 1.5
- gate_up: float32 [1024, 5632], P(('dp', 'fsdp')), may hold values from -0.1875 to 0.1875
- down_proj: float32 [2816, 1024], P(('dp', 'fsdp')), may hold values from -0.109375 to 0.109375
- norm_gains: float32 [2, 1024], P(None, ('dp', 'fsdp')), may hold values from 0.4 to 3.5
- attn_in_first: float32 [1024, 1536], P(('dp', 'fsdp')), may hold values from -0.00018310547 to 0.00018310547
- attn_in_second: float32 [1024, 1536], P(('dp', 'fsdp')), may hold values from 4.492086e-09 to 1.779883e-08
- latent_up_first: float32 [512, 1024], P(('dp', 'fsdp')), may hold values from -0.00018310547 to 0.00018310547
- latent_up_second: float32 [512, 1024], P(('dp', 'fsdp')), may hold values from 4.492086e-09 to 1.779883e-08
- attn_out_first: float32 [1024, 1024], P(('dp', 'fsdp')), may hold values from -6.1035156e-05 to 6.1035156e-05
- attn_out_second: float32 [1024, 1024], P(('dp', 'fsdp')), may hold values from 2.54269e-10 to 1.017076e-09
- gate_up_first: float32 [1024, 5632], P(('dp', 'fsdp')), may hold values from -0.00018310547 to 0.00018310547
- gate_up_second: float32 [1024, 5632], P(('dp', 'fsdp')), may hold values from 4.492086e-09 to 1.779883e-08
- down_proj_first: float32 [2816, 1024], P(('dp', 'fsdp')), may hold values from -0.00018310547 to 0.00018310547
- down_proj_second: float32 [2816, 1024], P(('dp', 'fsdp')), may hold values from 4.492086e-09 to 1.779883e-08
- gains_first: float32 [2, 1024], P(None, ('dp', 'fsdp')), may hold values from -0.00048828125 to 0.00048828125
- gains_second: float32 [2, 1024], P(None, ('dp', 'fsdp')), may hold values from 2.5426901e-08 to 1.01707606e-07
Outputs:
- mixed: bfloat16 [32768, 1024], P(('dp', 'fsdp'))
- input_grad: bfloat16 [32768, 1024], P(('dp', 'fsdp'))
- grad_norm: float32 [], replicated
- attn_in_new: float32 [1024, 1536], P(('dp', 'fsdp'))
- attn_in_first_new: float32 [1024, 1536], P(('dp', 'fsdp'))
- attn_in_second_new: float32 [1024, 1536], P(('dp', 'fsdp'))
- latent_up_new: float32 [512, 1024], P(('dp', 'fsdp'))
- latent_up_first_new: float32 [512, 1024], P(('dp', 'fsdp'))
- latent_up_second_new: float32 [512, 1024], P(('dp', 'fsdp'))
- attn_out_new: float32 [1024, 1024], P(('dp', 'fsdp'))
- attn_out_first_new: float32 [1024, 1024], P(('dp', 'fsdp'))
- attn_out_second_new: float32 [1024, 1024], P(('dp', 'fsdp'))
- gate_up_new: float32 [1024, 5632], P(('dp', 'fsdp'))
- gate_up_first_new: float32 [1024, 5632], P(('dp', 'fsdp'))
- gate_up_second_new: float32 [1024, 5632], P(('dp', 'fsdp'))
- down_proj_new: float32 [2816, 1024], P(('dp', 'fsdp'))
- down_proj_first_new: float32 [2816, 1024], P(('dp', 'fsdp'))
- down_proj_second_new: float32 [2816, 1024], P(('dp', 'fsdp'))
- norm_gains_new: float32 [2, 1024], P(None, ('dp', 'fsdp'))
- gains_first_new: float32 [2, 1024], P(None, ('dp', 'fsdp'))
- gains_second_new: float32 [2, 1024], P(None, ('dp', 'fsdp'))
All inputs are finite; a program needn't handle non-finite values.
Results may differ from a plain program's by a relative error of at most 0.017.
The roundings to bfloat16 on the way count: a program that leaves them out, or rounds other values in their place, can miss the bound.
Values may be sent and summed in bfloat16 or wider, within the bound.
No kernel may reach another device: no remote copies, remote signals or barrier semaphores. Data moves between devices by JAX's collectives and lax.ppermute only.
A program may use at most 320 MiB of HBM per device.

v0:
```python
import jax
import jax.numpy as jnp
from jax import lax
from jax.sharding import PartitionSpec as P

HQ = 16
HD = 64
LATENT_HEADS = 2
LATENT_WIDTH = 256
FF = 2816
NDOM = 16
STEP = 10
ROPE = 32


MAX_NORM = 1.0
BETA_ONE = 0.9
BETA_TWO = 0.95
RATE_MATRIX = 0.02
RATE_OUTPUT = 0.2
RATE_GAIN = 1.0
DECAY_MATRIX = 0.1
EPSILON_ADAM = 1e-08
EPSILON_NORM = 1e-06
ROPE_BASE = 10000.0


def angles(length):
    half = ROPE // 2
    freqs = ROPE_BASE ** (-jnp.arange(half).astype(jnp.float32) / half)
    theta = jnp.arange(length).astype(jnp.float32)[:, None] * freqs[None, :]
    return (jnp.cos(theta)[:, None, :], jnp.sin(theta)[:, None, :])


def rotate(values, cosine, sine):
    half = ROPE // 2
    first = values[..., :half]
    second = values[..., half:ROPE]
    return jnp.concatenate(
        [first * cosine - second * sine, first * sine + second * cosine, values[..., ROPE:]],
        axis=-1,
    )


def unrotate(values, cosine, sine):
    half = ROPE // 2
    first = values[..., :half]
    second = values[..., half:ROPE]
    return jnp.concatenate(
        [first * cosine + second * sine, second * cosine - first * sine, values[..., ROPE:]],
        axis=-1,
    )


def norm_forward(values, gain):
    inverse = lax.rsqrt(jnp.mean(values * values, axis=-1, keepdims=True) + EPSILON_NORM)
    values_hat = values * inverse
    return (values_hat * gain, values_hat, inverse)


def norm_back(grad_out, values_hat, inverse, gain):
    scaled = grad_out * gain
    grad_in = inverse * (
        scaled - values_hat * jnp.mean(scaled * values_hat, axis=-1, keepdims=True)
    )
    return (grad_in, jnp.sum(grad_out * values_hat, axis=0))


def collect(pieces):
    part_in, part_up, part_out, part_gate, part_down, part_gain = pieces
    return (
        lax.all_gather(part_in, ("dp", "fsdp"), axis=0, tiled=True),
        lax.all_gather(part_up, ("dp", "fsdp"), axis=0, tiled=True),
        lax.all_gather(part_out, ("dp", "fsdp"), axis=0, tiled=True),
        lax.all_gather(part_gate, ("dp", "fsdp"), axis=0, tiled=True),
        lax.all_gather(part_down, ("dp", "fsdp"), axis=0, tiled=True),
        lax.all_gather(part_gain, ("dp", "fsdp"), axis=1, tiled=True),
    )


def spread(grads):
    grad_in, grad_up, grad_out, grad_gate, grad_down, grad_gain = grads
    return (
        lax.psum_scatter(grad_in, ("dp", "fsdp"), scatter_dimension=0, tiled=True),
        lax.psum_scatter(grad_up, ("dp", "fsdp"), scatter_dimension=0, tiled=True),
        lax.psum_scatter(grad_out, ("dp", "fsdp"), scatter_dimension=0, tiled=True),
        lax.psum_scatter(grad_gate, ("dp", "fsdp"), scatter_dimension=0, tiled=True),
        lax.psum_scatter(grad_down, ("dp", "fsdp"), scatter_dimension=0, tiled=True),
        lax.psum_scatter(grad_gain, ("dp", "fsdp"), scatter_dimension=1, tiled=True),
    )


def adamw(master, grad, first, second, rate, decay):
    first_new = BETA_ONE * first + (1.0 - BETA_ONE) * grad
    second_new = BETA_TWO * second + (1.0 - BETA_TWO) * grad * grad
    first_hat = first_new / (1.0 - BETA_ONE**STEP)
    second_hat = second_new / (1.0 - BETA_TWO**STEP)
    master_new = master - rate * (
        first_hat / (jnp.sqrt(second_hat) + EPSILON_ADAM) + decay * master
    )
    return (master_new, first_new, second_new)


def block_scores(query_block, keys_part, start, scale):
    scores = (
        jnp.einsum("qhd,khd->hqk", query_block, keys_part, preferred_element_type=jnp.float32)
        * scale
    )
    rows = start + jnp.arange(query_block.shape[0])
    columns = jnp.arange(keys_part.shape[0])
    allowed = rows[:, None] >= columns[None, :]
    return jnp.where(allowed[None], scores, -1e30)


def shards(
    tokens,
    out_grad,
    domain_ids,
    domain_scale,
    attn_in,
    latent_expand_weight,
    attn_out,
    gate_up,
    down_proj,
    norm_gains,
    attn_in_first,
    attn_in_second,
    latent_up_first,
    latent_up_second,
    attn_out_first,
    attn_out_second,
    gate_up_first,
    gate_up_second,
    down_proj_first,
    down_proj_second,
    gains_first,
    gains_second,
):
    masters = (attn_in, latent_expand_weight, attn_out, gate_up, down_proj, norm_gains)
    lowered = tuple((w.astype(jnp.bfloat16) for w in masters))
    w_in, w_up, w_out, w_gate, w_down, w_gains = collect(lowered)
    length = tokens.shape[0]
    block = min(512, length)
    query_group_width = HQ // LATENT_HEADS * HD
    query_width = HQ * HD
    scale = HD ** (-0.5)
    cosine, sine = angles(length)
    inputs = tokens.astype(jnp.float32)
    gain_one = w_gains[0].astype(jnp.float32)
    gain_two = w_gains[1].astype(jnp.float32)
    normed_one, hat_one, inverse_one = norm_forward(inputs, gain_one)
    first_act = normed_one.astype(jnp.bfloat16)
    joined = jnp.dot(first_act, w_in, preferred_element_type=jnp.float32)
    query_pre = joined[:, :query_width].reshape(length, HQ, HD)
    latent_state = (
        joined[:, query_width:].astype(jnp.bfloat16).reshape(length, LATENT_HEADS, LATENT_WIDTH)
    )
    key_value_rows = jnp.einsum(
        "nph,phy->npy",
        latent_state,
        w_up.reshape(LATENT_HEADS, LATENT_WIDTH, 2 * query_group_width),
        preferred_element_type=jnp.float32,
    )
    key_pre = key_value_rows[..., :query_group_width].reshape(length, HQ, HD)
    values = key_value_rows[..., query_group_width:].reshape(length, HQ, HD).astype(jnp.bfloat16)
    query = rotate(query_pre, cosine, sine).astype(jnp.bfloat16)
    keys = rotate(key_pre, cosine, sine).astype(jnp.bfloat16)
    pieces = []
    log_totals = []
    for start in range(0, length, block):
        stop = start + block
        scores = block_scores(query[start:stop], keys[:stop], start, scale)
        peak = jnp.max(scores, axis=-1, keepdims=True)
        expo = jnp.exp(scores - peak)
        total = jnp.sum(expo, axis=-1, keepdims=True)
        probs = (expo / total).astype(jnp.bfloat16)
        pieces.append(
            jnp.einsum("hqk,khd->qhd", probs, values[:stop], preferred_element_type=jnp.float32)
        )
        log_totals.append(peak + jnp.log(total))
    attended = jnp.concatenate(pieces, axis=0).astype(jnp.bfloat16).reshape(length, query_width)
    hidden_state = inputs + jnp.dot(attended, w_out, preferred_element_type=jnp.float32)
    normed_two, hat_two, inverse_two = norm_forward(hidden_state, gain_two)
    second_act = normed_two.astype(jnp.bfloat16)
    gate_both = jnp.dot(second_act, w_gate, preferred_element_type=jnp.float32)
    gate = gate_both[:, :FF]
    upper = gate_both[:, FF:]
    sigmoid = jax.nn.sigmoid(gate)
    activated = gate * sigmoid
    hidden = (activated * upper).astype(jnp.bfloat16)
    mixed = (hidden_state + jnp.dot(hidden, w_down, preferred_element_type=jnp.float32)).astype(
        jnp.bfloat16
    )
    w_in, w_up, w_out, w_gate, w_down, w_gains = (
        lax.all_gather(lowered[0], ("dp", "fsdp"), axis=0, tiled=True),
        lax.all_gather(lowered[1], ("dp", "fsdp"), axis=0, tiled=True),
        lax.all_gather(lowered[2], ("dp", "fsdp"), axis=0, tiled=True),
        lax.all_gather(lowered[3], ("dp", "fsdp"), axis=0, tiled=True),
        lax.all_gather(lowered[4], ("dp", "fsdp"), axis=0, tiled=True),
        lax.all_gather(lowered[5], ("dp", "fsdp"), axis=1, tiled=True),
    )
    gain_one = w_gains[0].astype(jnp.float32)
    gain_two = w_gains[1].astype(jnp.float32)
    factor = jnp.sum(
        jnp.where(domain_ids[:, None] == jnp.arange(NDOM)[None, :], domain_scale[None, :], 0.0),
        axis=1,
    )
    grad_mixed = out_grad.astype(jnp.float32) * factor[:, None]
    grad_low = grad_mixed.astype(jnp.bfloat16)
    grad_down = jnp.einsum("sf,sd->fd", hidden, grad_low, preferred_element_type=jnp.float32)
    grad_hidden = jnp.einsum("sd,fd->sf", grad_low, w_down, preferred_element_type=jnp.float32)
    grad_gate_pre = grad_hidden * upper * sigmoid * (1.0 + gate * (1.0 - sigmoid))
    grad_upper = grad_hidden * activated
    grad_both = jnp.concatenate([grad_gate_pre, grad_upper], axis=1).astype(jnp.bfloat16)
    grad_gate = jnp.einsum("sd,sc->dc", second_act, grad_both, preferred_element_type=jnp.float32)
    grad_second = jnp.einsum("sc,dc->sd", grad_both, w_gate, preferred_element_type=jnp.float32)
    grad_norm_two, grad_gain_two = norm_back(grad_second, hat_two, inverse_two, gain_two)
    grad_state = grad_mixed + grad_norm_two
    grad_state_low = grad_state.astype(jnp.bfloat16)
    grad_out = jnp.einsum("so,sd->od", attended, grad_state_low, preferred_element_type=jnp.float32)
    grad_attended = (
        jnp.einsum("sd,od->so", grad_state_low, w_out, preferred_element_type=jnp.float32)
        .astype(jnp.bfloat16)
        .reshape(length, HQ, HD)
    )
    grad_query_parts = []
    grad_keys = jnp.zeros((length, HQ, HD), jnp.float32)
    grad_values = jnp.zeros((length, HQ, HD), jnp.float32)
    for number, start in enumerate(range(0, length, block)):
        stop = start + block
        scores = block_scores(query[start:stop], keys[:stop], start, scale)
        probs_full = jnp.exp(scores - log_totals[number])
        probs = probs_full.astype(jnp.bfloat16)
        grad_block = grad_attended[start:stop]
        grad_values = grad_values.at[:stop].add(
            jnp.einsum("hqk,qhd->khd", probs, grad_block, preferred_element_type=jnp.float32)
        )
        grad_probs = jnp.einsum(
            "qhd,khd->hqk", grad_block, values[:stop], preferred_element_type=jnp.float32
        )
        inner_sum = jnp.sum(probs_full * grad_probs, axis=-1, keepdims=True)
        grad_scores = (probs_full * (grad_probs - inner_sum) * scale).astype(jnp.bfloat16)
        grad_query_parts.append(
            jnp.einsum("hqk,khd->qhd", grad_scores, keys[:stop], preferred_element_type=jnp.float32)
        )
        grad_keys = grad_keys.at[:stop].add(
            jnp.einsum(
                "hqk,qhd->khd", grad_scores, query[start:stop], preferred_element_type=jnp.float32
            )
        )
    grad_query = jnp.concatenate(grad_query_parts, axis=0)
    grad_key_pre = unrotate(grad_keys, cosine, sine).reshape(
        length, LATENT_HEADS, query_group_width
    )
    grad_key_value_rows = jnp.concatenate(
        [grad_key_pre, grad_values.reshape(length, LATENT_HEADS, query_group_width)], axis=-1
    ).astype(jnp.bfloat16)
    grad_up = jnp.einsum(
        "xvi,xvh->vih", latent_state, grad_key_value_rows, preferred_element_type=jnp.float32
    ).reshape(LATENT_HEADS * LATENT_WIDTH, 2 * query_group_width)
    grad_latent = jnp.einsum(
        "xmz,mbz->xmb",
        grad_key_value_rows,
        w_up.reshape(LATENT_HEADS, LATENT_WIDTH, 2 * query_group_width),
        preferred_element_type=jnp.float32,
    ).reshape(length, LATENT_HEADS * LATENT_WIDTH)
    grad_query_pre = unrotate(grad_query, cosine, sine).reshape(length, query_width)
    grad_joined = jnp.concatenate([grad_query_pre, grad_latent], axis=1).astype(jnp.bfloat16)
    grad_in = jnp.einsum("sd,sc->dc", first_act, grad_joined, preferred_element_type=jnp.float32)
    grad_first = jnp.einsum("sc,dc->sd", grad_joined, w_in, preferred_element_type=jnp.float32)
    grad_norm_one, grad_gain_one = norm_back(grad_first, hat_one, inverse_one, gain_one)
    input_grad = (grad_state + grad_norm_one).astype(jnp.bfloat16)
    grad_gains = jnp.stack([grad_gain_one, grad_gain_two])
    owned = spread((grad_in, grad_up, grad_out, grad_gate, grad_down, grad_gains))
    local_squares = jnp.float32(0.0)
    for grad in owned:
        local_squares = local_squares + jnp.sum(grad * grad)
    grad_norm = jnp.sqrt(lax.psum(local_squares, ("dp", "fsdp")))
    clip = jnp.minimum(1.0, MAX_NORM / (grad_norm + 1e-06))
    firsts = (
        attn_in_first,
        latent_up_first,
        attn_out_first,
        gate_up_first,
        down_proj_first,
        gains_first,
    )
    seconds = (
        attn_in_second,
        latent_up_second,
        attn_out_second,
        gate_up_second,
        down_proj_second,
        gains_second,
    )
    results = []
    for index in range(6):
        if index == 5:
            rate, decay = (RATE_GAIN, 0.0)
        elif index == 2:
            rate, decay = (RATE_OUTPUT, DECAY_MATRIX)
        else:
            rate, decay = (RATE_MATRIX, DECAY_MATRIX)
        results.extend(
            adamw(masters[index], clip * owned[index], firsts[index], seconds[index], rate, decay)
        )
    return (
        mixed,
        input_grad,
        grad_norm,
        results[0],
        results[1],
        results[2],
        results[3],
        results[4],
        results[5],
        results[6],
        results[7],
        results[8],
        results[9],
        results[10],
        results[11],
        results[12],
        results[13],
        results[14],
        results[15],
        results[16],
        results[17],
    )


def solution(mesh):
    return jax.shard_map(
        shards,
        mesh=mesh,
        in_specs=(
            P(("dp", "fsdp"), None),
            P(("dp", "fsdp"), None),
            P(("dp", "fsdp")),
            P(),
            P(("dp", "fsdp"), None),
            P(("dp", "fsdp"), None),
            P(("dp", "fsdp"), None),
            P(("dp", "fsdp"), None),
            P(("dp", "fsdp"), None),
            P(None, ("dp", "fsdp")),
            P(("dp", "fsdp"), None),
            P(("dp", "fsdp"), None),
            P(("dp", "fsdp"), None),
            P(("dp", "fsdp"), None),
            P(("dp", "fsdp"), None),
            P(("dp", "fsdp"), None),
            P(("dp", "fsdp"), None),
            P(("dp", "fsdp"), None),
            P(("dp", "fsdp"), None),
            P(("dp", "fsdp"), None),
            P(None, ("dp", "fsdp")),
            P(None, ("dp", "fsdp")),
        ),
        out_specs=(
            P(("dp", "fsdp"), None),
            P(("dp", "fsdp"), None),
            P(),
            P(("dp", "fsdp"), None),
            P(("dp", "fsdp"), None),
            P(("dp", "fsdp"), None),
            P(("dp", "fsdp"), None),
            P(("dp", "fsdp"), None),
            P(("dp", "fsdp"), None),
            P(("dp", "fsdp"), None),
            P(("dp", "fsdp"), None),
            P(("dp", "fsdp"), None),
            P(("dp", "fsdp"), None),
            P(("dp", "fsdp"), None),
            P(("dp", "fsdp"), None),
            P(("dp", "fsdp"), None),
            P(("dp", "fsdp"), None),
            P(("dp", "fsdp"), None),
            P(None, ("dp", "fsdp")),
            P(None, ("dp", "fsdp")),
            P(None, ("dp", "fsdp")),
        ),
        check_vma=False,
    )
```

profile of v0, /device:TPU:0, one launch (start us, length us, event | category | flops | bytes accessed | tf_op | source)
XLA Modules:
  0.0 1999.0 jit_solution(11739299925855286108)
XLA Ops:
  16.6 69.4 %all-gather = bf16[32,32,2]{1,2,0:T(2,128)(2,1)S(1)} all-gather(bf16[1,32,2]{1,2,0:T(2,128)(2,1)S(1)} %convert_bitcast_fusion), channel_id=1, replica_groups=mesh['dp'=8,'fsdp'=4] {'dp','fsdp'}, dimensions={0}, use_global_device_ids=true | all-gather | bytes 4224 | tf_op jit(solution)/shard_map/all_gather | solution.py:77
  106.4 23.1 %all-gather.9.cloned.1.call-done = bf16[512,1024]{1,0:T(8,128)(2,1)} async-done(((bf16[16,1024]{1,0:T(8,128)(2,1)}), bf16[512,1024]{1,0:T(8,128)(2,1)}) %all-gather.9.cloned.1.call-update) | async-done | bytes 1048592 | tf_op jit(solution)/shard_map/all_gather | solution.py:73
  148.5 7.4 fusion.151
  155.9 14.0 fusion.4
  169.9 8.6 fusion.37
  178.5 8.6 fusion.92
  187.1 15.3 fusion.3
  202.3 15.7 fusion.94
  226.1 55.8 %all-gather.13.cloned.1.call-done = bf16[1024,5632]{1,0:T(8,128)(2,1)} async-done(((bf16[32,5632]{1,0:T(8,128)(2,1)}), bf16[1024,5632]{1,0:T(8,128)(2,1)}) %all-gather.13.cloned.1.call-update) | async-done | bytes 11534352 | tf_op jit(solution)/shard_map/all_gather | solution.py:75
  281.9 21.2 %fusion.142 = f32[1024,5632]{1,0:T(8,128)} fusion(bf16[1024,5632]{1,0:T(8,128)(2,1)} %all-gather.13.cloned.1.call-done, f32[1024,1024]{0,1:T(8,128)} %get-tuple-element.219, f32[1024]{0:T(1024)S(1)} %bitcast.101, f32[1024]{0:T(1024)S(1)} %add_rsqrt_fusion), kind=kOutput, calls=%fused_computation.199 | convolution fusion | flops 11814305792 | bytes 38805504 | tf_op jit(solution)/shard_map/dot_general | solution.py:185
  303.0 47.8 %all-gather.15.cloned.1.call-done = bf16[2816,1024]{1,0:T(8,128)(2,1)} async-done(((bf16[88,1024]{1,0:T(8,128)(2,1)}), bf16[2816,1024]{1,0:T(8,128)(2,1)}) %all-gather.15.cloned.1.call-update) | async-done | bytes 5767184 | tf_op jit(solution)/shard_map/all_gather | solution.py:76
  350.9 20.1 %multiply_convert_fusion.3 = (bf16[1024,2816]{1,0:T(8,128)(2,1)}, bf16[1024,2816]{1,0:T(8,128)(2,1)}, bf16[1024,2816]{1,0:T(8,128)(2,1)}) fusion(f32[1024,5632]{1,0:T(8,128)} %fusion.142, bf16[2816,1024]{1,0:T(8,128)(2,1)} %all-gather.15.cloned.1.call-done, bf16[1024,1024]{0,1:T(8,128)(2,1)S(1)} %copy-done.6, f32[1024]{0:T(1024)S(1)} %copy-done.42), kind=kOutput, calls=%fused_computation.36 | convolution fusion | flops 5951979520 | bytes 48238592 | tf_op jit(solution)/shard_map/sd,fd->sf/dot_general | solution.py:211
  370.9 20.8 %multiply_reduce_fusion.2 = (f32[1024]{0:T(1024)S(1)}, f32[1024]{0:T(1024)S(1)}, f32[1024,1024]{0,1:T(8,128)}) fusion(f32[1024,1024]{0,1:T(8,128)} %get-tuple-element.219, f32[1024]{0:T(1024)S(1)} %add_rsqrt_fusion, f32[1024]{0:T(1024)S(1)} %bitcast.102, bf16[1024,5632]{1,0:T(8,128)(2,1)} %all-gather.13.cloned.1.call-done, ...), kind=kOutput, calls=%fused_computation.71 | convolution fusion | flops 11840518144 | bytes 31473664 | tf_op jit(solution)/shard_map/sc,dc->sd/dot_general | solution.py:216
  400.1 9.2 fusion.152
  413.9 24.2 %fusion.80 = f32[512,16,64]{0,2,1:T(8,128)} fusion(f32[16,512,512]{1,2,0:T(8,128)} %fusion.152, f32[16,512,512]{1,2,0:T(8,128)} %get-tuple-element.217, f32[16,512]{1,0:T(8,128)} %log_add_fusion.1, bf16[1024,16,32]{0,2,1:T(8,128)(2,1)} %copy-done.23, bf16[1024,16,16]{0,2,1:T(8,128)(2,1)} %copy-done.33, bf16[1024,16,16]{0,2,1:T(8,128)(2,1)} %copy-done.32), kind=kOutput, calls=%fused_computation.100 | convolution fusion | flops 569385472 | bytes 37781504 | tf_op jit(solution)/shard_map/hqk,khd->qhd/dot_general | solution.py:244
  438.1 25.1 %fusion.83 = f32[512,16,64]{0,2,1:T(8,128)} fusion(f32[16,512,512]{1,2,0:T(8,128)} %fusion.152, f32[16,512,512]{1,2,0:T(8,128)} %get-tuple-element.217, f32[16,512]{1,0:T(8,128)S(1)} %copy-done.36, bf16[1024,16,64]{0,2,1:T(8,128)(2,1)} %copy-done.18), kind=kOutput, calls=%fused_computation.101 | convolution fusion | flops 566239744 | bytes 70320128 | tf_op jit(solution)/shard_map/hqk,qhd->khd/dot_general | solution.py:247
  463.3 13.1 fusion.153
  476.4 68.5 %fusion.89 = f32[512,16,64]{0,2,1:T(8,128)} fusion(f32[16,512,1024]{2,1,0:T(8,128)} %fusion.153, f32[16,512,1024]{2,1,0:T(8,128)} %get-tuple-element.215, f32[16,512]{1,0:T(8,128)S(1)} %copy-done.37, pred[512,1024]{1,0:T(8,128)(4,1)} %iota_compare_fusion, bf16[1024,16,32]{0,2,1:T(8,128)(2,1)} %copy-done.23, bf16[1024,16,16]{0,2,1:T(8,128)(2,1)} %copy-done.33, ...), kind=kOutput, calls=%fused_computation.103 | convolution fusion | flops 1172317184 | bytes 71860224 | tf_op jit(solution)/shard_map/hqk,khd->qhd/dot_general | solution.py:244
  545.0 61.6 %bitcast_add_fusion.1 = f32[1024,16,64]{0,2,1:T(8,128)} fusion(f32[512,16,64]{0,2,1:T(8,128)} %fusion.83, f32[16,512,1024]{2,1,0:T(8,128)} %fusion.153, f32[16,512,1024]{2,1,0:T(8,128)} %get-tuple-element.215, f32[16,512]{1,0:T(8,128)S(1)} %copy-done.37, pred[512,1024]{1,0:T(8,128)(4,1)} %iota_compare_fusion, bf16[1024,16,64]{0,2,1:T(8,128)(2,1)} %copy-done.18), kind=kOutput, calls=%fused_computation.70 | convolution fusion | flops 1167074304 | bytes 142671872 | tf_op jit(solution)/shard_map/hqk,qhd->khd/dot_general | solution.py:247
  614.8 15.3 fusion.65
  654.2 7.5 fusion.74
  662.9 6.8 fusion.95
  669.8 12.0 fusion.76
  682.4 21.7 %fusion.45 = f32[1024,5632]{1,0:T(8,128)} fusion(bf16[1024,2816]{1,0:T(8,128)(2,1)} %get-tuple-element.192, bf16[1024,2816]{1,0:T(8,128)(2,1)} %get-tuple-element.191, f32[1024,1024]{0,1:T(8,128)} %get-tuple-element.219, f32[1024]{0:T(1024)S(1)} %bitcast.104, f32[1024]{0:T(1024)S(1)} %copy-done.44), kind=kOutput, calls=%fused_computation.44 | convolution fusion | flops 11837374464 | bytes 38805504 | tf_op jit(solution)/shard_map/sd,sc->dc/dot_general | solution.py:215
  704.2 11.5 add_convert_fusion
  725.6 57.3 %reduce-scatter.19.cloned.1.call-done = f32[32,2]{1,0:T(8,128)} async-done(((f32[1024,2]{1,0:T(8,128)}), f32[32,2]{1,0:T(8,128)}) %reduce-scatter.19.cloned.1.call-update) | async-done | bytes 272
  784.3 135.2 %reduce-scatter.11.cloned.1.call-done = f32[16,1024]{1,0:T(8,128)} async-done(((f32[512,1024]{1,0:T(8,128)}), f32[16,1024]{1,0:T(8,128)}) %reduce-scatter.11.cloned.1.call-update) | async-done | bytes 65552 | tf_op jit(solution)/shard_map/reduce_scatter | solution.py:85
  920.9 116.4 %reduce-scatter.9.cloned.1.call-done = f32[32,1536]{1,0:T(8,128)} async-done(((f32[1024,1536]{1,0:T(8,128)}), f32[32,1536]{1,0:T(8,128)}) %reduce-scatter.9.cloned.1.call-update) | async-done | bytes 196624 | tf_op jit(solution)/shard_map/reduce_scatter | solution.py:84
  1040.3 147.1 %reduce-scatter.13.cloned.1.call-done = f32[32,1024]{1,0:T(8,128)} async-done(((f32[1024,1024]{1,0:T(8,128)}), f32[32,1024]{1,0:T(8,128)}) %reduce-scatter.13.cloned.1.call-update) | async-done | bytes 131088 | tf_op jit(solution)/shard_map/reduce_scatter | solution.py:86
  1189.7 249.6 %reduce-scatter.17.cloned.1.call-done = f32[88,1024]{1,0:T(8,128)} async-done(((f32[2816,1024]{1,0:T(8,128)}), f32[88,1024]{1,0:T(8,128)}) %reduce-scatter.17.cloned.1.call-update) | async-done | bytes 360464 | tf_op jit(solution)/shard_map/reduce_scatter | solution.py:88
  1441.0 492.6 %reduce-scatter.15.cloned.1.call-done = f32[32,5632]{1,0:T(8,128)} async-done(((f32[1024,5632]{1,0:T(8,128)}), f32[32,5632]{1,0:T(8,128)}) %reduce-scatter.15.cloned.1.call-update) | async-done | bytes 720912 | tf_op jit(solution)/shard_map/reduce_scatter | solution.py:87
  1941.6 38.7 %psum.7 = f32[]{:T(128)} all-reduce(f32[]{:T(128)S(6)} %add.251), channel_id=1, replica_groups=mesh['dp'=8,'fsdp'=4] {'dp','fsdp'}, use_global_device_ids=true, to_apply=%region_25.26 | all-reduce | flops 1 | bytes 8 | tf_op jit(solution)/shard_map/psum | solution.py:278
  (215 shorter events, 137.1 us)
Async XLA Ops:
  7.2 88.6 %all-gather.7.cloned.1.call-start = ((), (), s32[]{:S(2)}) async-start(), calls=%async_computation.6 | async-start | bytes 3244032 | tf_op jit(solution)/shard_map/all_gather | solution.py:72
  8.8 120.6 %all-gather.9.cloned.1.call-start = ((), (), s32[]{:S(2)}) async-start(), calls=%async_computation.7 | async-start | bytes 1081344 | tf_op jit(solution)/shard_map/all_gather | solution.py:73
  10.4 207.7 %all-gather.11.cloned.1.call-start = ((), (), s32[]{:S(2)}) async-start(), calls=%async_computation.8 | async-start | bytes 2162688 | tf_op jit(solution)/shard_map/all_gather | solution.py:74
  12.0 269.9 %all-gather.13.cloned.1.call-start = ((), (), s32[]{:S(2)}) async-start(), calls=%async_computation.9 | async-start | bytes 11894784 | tf_op jit(solution)/shard_map/all_gather | solution.py:75
  14.0 336.9 %all-gather.15.cloned.1.call-start = ((), (), s32[]{:S(2)}) async-start(), calls=%async_computation.10 | async-start | bytes 5947392 | tf_op jit(solution)/shard_map/all_gather | solution.py:76
  15.7 767.2 %reduce-scatter.19.cloned.1.call-start = ((), (), s32[]{:S(2)}) async-start(), calls=%async_computation.16 | async-start | bytes 540672
  86.0 305.7 %copy-start.45 = (f32[1,1024]{1,0:T(1,128)}, f32[1,1024]{1,0:T(1,128)S(1)}, u32[]{:S(2)}) copy-start(f32[1,1024]{1,0:T(1,128)S(1)} %get-tuple-element.210) | copy-start | bytes 12292
  90.1 128.0 %copy-start = (bf16[1024,1024]{0,1:T(8,128)(2,1)}, bf16[1024,1024]{0,1:T(8,128)(2,1)S(1)}, u32[]{:S(2)}) copy-start(bf16[1024,1024]{0,1:T(8,128)(2,1)S(1)} %copy.104) | copy-start | bytes 6291460
  95.8 51.2 %copy-start.28 = (f32[1024,16]{0,1:T(8,128)}, f32[1024,16]{0,1:T(8,128)S(1)}, u32[]{:S(2)}) copy-start(f32[1024,16]{0,1:T(8,128)S(1)} %get-tuple-element.208) | copy-start | bytes 196612
  224.8 166.9 %copy-start.43 = (f32[1024]{0:T(1024)}, f32[1024]{0:T(1024)S(1)}, u32[]{:S(2)}) copy-start(f32[1024]{0:T(1024)S(1)} %add_rsqrt_fusion) | copy-start | bytes 12292
  281.9 69.0 %copy-start.6 = (bf16[1024,1024]{0,1:T(8,128)(2,1)S(1)}, bf16[1024,1024]{0,1:T(8,128)(2,1)}, u32[]{:S(2)}) copy-start(bf16[1024,1024]{0,1:T(8,128)(2,1)} %copy.111) | copy-start | bytes 6291460
  281.9 69.0 %copy-start.42 = (f32[1024]{0:T(1024)S(1)}, f32[1024]{0:T(1024)}, u32[]{:S(2)}) copy-start(f32[1024]{0:T(1024)} %select_reduce_fusion) | copy-start | bytes 12292
  545.0 64.4 %copy-start.7 = (f32[512,16,64]{0,2,1:T(8,128)S(1)}, f32[512,16,64]{0,2,1:T(8,128)}, u32[]{:S(2)}) copy-start(f32[512,16,64]{0,2,1:T(8,128)} %fusion.80) | copy-start | bytes 6291460
  545.0 64.4 %copy-start.29 = (f32[1024,16]{0,1:T(8,128)S(1)}, f32[1024,16]{0,1:T(8,128)}, u32[]{:S(2)}) copy-start(f32[1024,16]{0,1:T(8,128)} %copy-done.28) | copy-start | bytes 196612
  545.0 64.4 %copy-start.31 = (f32[1024,16]{0,1:T(8,128)S(1)}, f32[1024,16]{0,1:T(8,128)}, u32[]{:S(2)}) copy-start(f32[1024,16]{0,1:T(8,128)} %copy-done.30) | copy-start | bytes 196612
  649.2 270.2 %reduce-scatter.11.cloned.1.call-start = ((), (), s32[]{:S(2)}) async-start(), calls=%async_computation.12 | async-start | bytes 2162688 | tf_op jit(solution)/shard_map/reduce_scatter | solution.py:85
  654.1 383.2 %reduce-scatter.9.cloned.1.call-start = ((), (), s32[]{:S(2)}) async-start(), calls=%async_computation.11 | async-start | bytes 6488064 | tf_op jit(solution)/shard_map/reduce_scatter | solution.py:84
  661.7 525.7 %reduce-scatter.13.cloned.1.call-start = ((), (), s32[]{:S(2)}) async-start(), calls=%async_computation.13 | async-start | bytes 4325376 | tf_op jit(solution)/shard_map/reduce_scatter | solution.py:86
  669.7 769.6 %reduce-scatter.17.cloned.1.call-start = ((), (), s32[]{:S(2)}) async-start(), calls=%async_computation.15 | async-start | bytes 11894784 | tf_op jit(solution)/shard_map/reduce_scatter | solution.py:88
  681.8 1251.9 %reduce-scatter.15.cloned.1.call-start = ((), (), s32[]{:S(2)}) async-start(), calls=%async_computation.14 | async-start | bytes 23789568 | tf_op jit(solution)/shard_map/reduce_scatter | solution.py:87
  725.5 1255.4 %copy-start.48 = (f32[2,32]{1,0:T(2,128)S(1)}, f32[2,32]{1,0:T(2,128)}, u32[]{:S(2)}) copy-start(f32[2,32]{1,0:T(2,128)} %param.43) | copy-start | bytes 772
  725.5 1255.5 %copy-start.49 = (f32[2,32]{1,0:T(2,128)S(1)}, f32[2,32]{1,0:T(2,128)}, u32[]{:S(2)}) copy-start(f32[2,32]{1,0:T(2,128)} %param.54) | copy-start | bytes 772
  725.5 1255.5 %copy-start.50 = (f32[2,32]{1,0:T(2,128)S(1)}, f32[2,32]{1,0:T(2,128)}, u32[]{:S(2)}) copy-start(f32[2,32]{1,0:T(2,128)} %param.55) | copy-start | bytes 772
  725.5 1257.7 %copy-start.34 = (f32[32,1024]{1,0:T(8,128)S(1)}, f32[32,1024]{1,0:T(8,128)}, u32[]{:S(2)}) copy-start(f32[32,1024]{1,0:T(8,128)} %param.40) | copy-start | bytes 393220
  725.5 1259.5 %copy-start.24 = (f32[32,1536]{1,0:T(8,128)S(1)}, f32[32,1536]{1,0:T(8,128)}, u32[]{:S(2)}) copy-start(f32[32,1536]{1,0:T(8,128)} %param.38) | copy-start | bytes 589828
  920.9 1066.0 %copy-start.20 = (f32[88,1024]{1,0:T(8,128)S(1)}, f32[88,1024]{1,0:T(8,128)}, u32[]{:S(2)}) copy-start(f32[88,1024]{1,0:T(8,128)} %param.42) | copy-start | bytes 1081348
  1037.3 947.7 %copy-start.25 = (f32[32,1536]{1,0:T(8,128)S(1)}, f32[32,1536]{1,0:T(8,128)}, u32[]{:S(2)}) copy-start(f32[32,1536]{1,0:T(8,128)} %reduce-scatter.9.cloned.1.call-done) | copy-start | bytes 589828
  1187.4 795.9 %copy-start.35 = (f32[32,1024]{1,0:T(8,128)S(1)}, f32[32,1024]{1,0:T(8,128)}, u32[]{:S(2)}) copy-start(f32[32,1024]{1,0:T(8,128)} %reduce-scatter.13.cloned.1.call-done) | copy-start | bytes 393220
  1439.3 547.7 %copy-start.21 = (f32[88,1024]{1,0:T(8,128)S(1)}, f32[88,1024]{1,0:T(8,128)}, u32[]{:S(2)}) copy-start(f32[88,1024]{1,0:T(8,128)} %reduce-scatter.17.cloned.1.call-done) | copy-start | bytes 1081348
  1937.5 51.7 %copy-start.15 = (f32[32,5632]{1,0:T(8,128)S(1)}, f32[32,5632]{1,0:T(8,128)}, u32[]{:S(2)}) copy-start(f32[32,5632]{1,0:T(8,128)} %param.41) | copy-start | bytes 2162692
  1937.5 51.7 %copy-start.16 = (f32[32,5632]{1,0:T(8,128)S(1)}, f32[32,5632]{1,0:T(8,128)}, u32[]{:S(2)}) copy-start(f32[32,5632]{1,0:T(8,128)} %reduce-scatter.15.cloned.1.call-done) | copy-start | bytes 2162692
  1937.5 51.7 %copy-start.26 = (f32[32,5632]{1,0:T(8,128)S(1)}, f32[32,5632]{1,0:T(8,128)}, u32[]{:S(2)}) copy-start(f32[32,5632]{1,0:T(8,128)} %param.50) | copy-start | bytes 2162692
  (39 other events, 406.7 us)
Sparse Core Ops, SparseCore 0:
  11.5 61.7 all-gather.6
  76.8 52.5 all-gather.8
  133.0 55.4 all-gather.10
  191.7 90.1 all-gather.12
  285.1 65.6 all-gather.14
  649.4 133.4 reduce-scatter.18
  785.3 134.1 reduce-scatter.10
  925.1 112.2 reduce-scatter.8
  1039.7 147.6 reduce-scatter.12
  1189.7 249.5 reduce-scatter.16
  1441.7 491.8 reduce-scatter.14
where the time goes:
time: 2010 us; the launch traced here: 2000 us
  waiting for transfers between devices  1330 us (66%)
  matrix products  423 us (21%)
  blocking collectives  108 us (5%)
  other arithmetic  75.5 us (4%)
  local copies, waits for them, and re-layouts  45.8 us (2%)
  between operations  20.8 us (1%)
    reduce_scatter x1, waiting for transfers between devices, spread(): lax.psum_scatter(grad_gate, ('dp', 'fsdp'), scatter_dimension=0, tiled=True)  493 us
    reduce_scatter x1, waiting for transfers between devices, spread(): lax.psum_scatter(grad_down, ('dp', 'fsdp'), scatter_dimension=0, tiled=True)  250 us
    reduce_scatter x1, waiting for transfers between devices, spread(): lax.psum_scatter(grad_out, ('dp', 'fsdp'), scatter_dimension=0, tiled=True)  147 us
    reduce_scatter x1, waiting for transfers between devices, spread(): lax.psum_scatter(grad_up, ('dp', 'fsdp'), scatter_dimension=0, tiled=True)  135 us
    reduce_scatter x1, waiting for transfers between devices, spread(): lax.psum_scatter(grad_in, ('dp', 'fsdp'), scatter_dimension=0, tiled=True)  116 us
    dot_general x2, matrix products, shards(): jnp.einsum('hqk,khd->qhd', grad_scores, keys[:stop], preferred_element_ty...  92.7 us
    dot_general x2, matrix products, shards(): jnp.einsum('hqk,qhd->khd', grad_scores, query[start:stop], preferred_elem...  86.7 us
    all_gather x1, blocking collectives, collect(): lax.all_gather(part_gain, ('dp', 'fsdp'), axis=1, tiled=True)  69.4 us
  transfers between devices with their start and end apart: 11, of which 9 were waited for; matrix products, arithmetic and copies ran while one was open for 11% of the time, Pallas kernels for 0%

commit v1 on v0

v1 whole, which is shorter than its diff:
```python
import jax
import jax.numpy as jnp
from jax import lax
from jax.experimental import pallas as pl
from jax.experimental.pallas import tpu as pltpu
from jax.sharding import PartitionSpec as P

HQ = 16
HD = 64
LATENT_HEADS = 2
LATENT_WIDTH = 256
FF = 2816
NDOM = 16
STEP = 10
ROPE = 32
QUERY_WIDTH = HQ * HD
GROUP_WIDTH = QUERY_WIDTH // LATENT_HEADS
LANES = 128
PAIRS = QUERY_WIDTH // LANES
PAIRS_PER_LATENT = PAIRS // LATENT_HEADS

MAX_NORM = 1.0
BETA_ONE = 0.9
BETA_TWO = 0.95
RATE_MATRIX = 0.02
RATE_OUTPUT = 0.2
RATE_GAIN = 1.0
DECAY_MATRIX = 0.1
EPSILON_ADAM = 1e-08
EPSILON_NORM = 1e-06
ROPE_BASE = 10000.0

AXES = ("dp", "fsdp")
BF = jnp.bfloat16
F32 = jnp.float32
LOG2E = 1.4426950408889634
SCALE = HD**-0.5
NN = (((1,), (0,)), ((), ()))
NT = (((1,), (1,)), ((), ()))
TN = (((0,), (0,)), ((), ()))
MIB = 1 << 20


def dot(left, right, dims):
    return lax.dot_general(left, right, dims, preferred_element_type=F32)


def resident(*shape):
    return pl.BlockSpec(shape, lambda *step: (0,) * len(shape), pipeline_mode=pl.Buffered(1))


def rotation_tables(length):
    half = ROPE // 2
    freqs = ROPE_BASE ** (-jnp.arange(half).astype(F32) / half)
    theta = jnp.arange(length).astype(F32)[:, None] * freqs[None, :]
    cosine, sine = jnp.cos(theta), jnp.sin(theta)
    zero = jnp.zeros((length, half), F32)
    rest = jnp.zeros((length, HD - ROPE), F32)
    own = jnp.concatenate([cosine, cosine, rest + 1.0], axis=1)
    ahead = jnp.concatenate([-sine, zero, rest], axis=1)
    behind = jnp.concatenate([zero, sine, rest], axis=1)
    return tuple(jnp.concatenate([t, t], axis=1) for t in (own, ahead, behind))


def rotate(values, own, ahead, behind):
    half = ROPE // 2
    return (
        values * own
        + pltpu.roll(values, LANES - half, 1) * ahead
        + pltpu.roll(values, half, 1) * behind
    )


def unrotate(values, own, ahead, behind):
    half = ROPE // 2
    return (
        values * own
        - pltpu.roll(values, LANES - half, 1) * ahead
        - pltpu.roll(values, half, 1) * behind
    )


def project_kernel(x_ref, gain_ref, win_ref, wup_ref, own_ref, ahead_ref, behind_ref,
                   a1_ref, q_ref, k_ref, v_ref, c_ref):
    tables = (own_ref[...], ahead_ref[...], behind_ref[...])
    x = x_ref[...].astype(F32)
    inverse = lax.rsqrt(jnp.mean(x * x, axis=1, keepdims=True) + EPSILON_NORM)
    a1 = (x * inverse * gain_ref[...].astype(F32)).astype(BF)
    a1_ref[...] = a1
    joined = dot(a1, win_ref[...], NN)
    for pair in range(PAIRS):
        lanes = slice(pair * LANES, (pair + 1) * LANES)
        q_ref[:, lanes] = rotate(joined[:, lanes], *tables).astype(BF)
    c = joined[:, QUERY_WIDTH:].astype(BF)
    c_ref[...] = c
    for head in range(LATENT_HEADS):
        latent = slice(head * LATENT_WIDTH, (head + 1) * LATENT_WIDTH)
        both = dot(c[:, latent], wup_ref[latent, :], NN)
        for pair in range(PAIRS_PER_LATENT):
            lanes = slice(pair * LANES, (pair + 1) * LANES)
            out = slice(head * GROUP_WIDTH + pair * LANES, head * GROUP_WIDTH + (pair + 1) * LANES)
            k_ref[:, out] = rotate(both[:, lanes], *tables).astype(BF)
        out = slice(head * GROUP_WIDTH, (head + 1) * GROUP_WIDTH)
        v_ref[:, out] = both[:, GROUP_WIDTH:].astype(BF)


def project(x, gain, w_in, w_up, tables):
    length, width = x.shape
    tile = min(256, length)
    latents = LATENT_HEADS * LATENT_WIDTH
    rows = lambda columns: pl.BlockSpec((tile, columns), lambda i: (i, 0))
    shape = lambda columns: jax.ShapeDtypeStruct((length, columns), BF)
    return pl.pallas_call(
        project_kernel,
        grid=(length // tile,),
        in_specs=[rows(width), resident(1, width), resident(*w_in.shape), resident(*w_up.shape)]
        + [rows(LANES)] * 3,
        out_specs=[rows(width), rows(QUERY_WIDTH), rows(QUERY_WIDTH), rows(QUERY_WIDTH), rows(latents)],
        out_shape=[shape(width), shape(QUERY_WIDTH), shape(QUERY_WIDTH), shape(QUERY_WIDTH), shape(latents)],
        compiler_params=pltpu.CompilerParams(vmem_limit_bytes=48 * MIB),
        cost_estimate=pl.CostEstimate(
            flops=2 * length * (w_in.size + w_up.size), bytes_accessed=16 * MIB, transcendentals=0
        ),
        name="project",
    )(x, gain, w_in, w_up, *tables)


def halves(pair, axis):
    first = lax.broadcasted_iota(jnp.int32, pair.shape, axis) < HD
    zero = jnp.zeros_like(pair)
    return (jnp.where(first, pair, zero), jnp.where(first, zero, pair))


def not_after(block):
    keys = lax.broadcasted_iota(jnp.int32, (block, block), 0)
    queries = lax.broadcasted_iota(jnp.int32, (block, block), 1)
    return keys <= queries


def attention_kernel(q_ref, k_ref, v_ref, o_ref, log_ref):
    length = q_ref.shape[0]
    block = min(256, length)
    values = halves(v_ref[...].T, 0)
    for start in range(0, length, block):
        stop = start + block
        queries = halves(q_ref[start:stop, :], 1)
        probs = []
        for head in range(2):
            scores = dot(k_ref[:stop, :], queries[head], NT) * (SCALE * LOG2E)
            last = jnp.where(not_after(block), scores[start:, :], -1e30)
            scores = jnp.concatenate([scores[:start, :], last], axis=0) if start else last
            peak = jnp.max(scores, axis=0, keepdims=True)
            expo = jnp.exp2(scores - peak)
            total = jnp.sum(expo, axis=0, keepdims=True)
            log_ref[0, head : head + 1, start:stop] = peak + jnp.log2(total)
            probs.append((expo * (1.0 / total)).astype(BF))
        mixed = dot(values[0][:, :stop], probs[0], NN) + dot(values[1][:, :stop], probs[1], NN)
        o_ref[start:stop, :] = mixed.T.astype(BF)


def attention(q, k, v):
    length, width = q.shape
    spec = pl.BlockSpec((length, LANES), lambda i: (0, i))
    logs = pl.BlockSpec((1, 2, length), lambda i: (i, 0, 0))
    return pl.pallas_call(
        attention_kernel,
        grid=(PAIRS,),
        in_specs=[spec] * 3,
        out_specs=[spec, logs],
        out_shape=[
            jax.ShapeDtypeStruct((length, width), BF),
            jax.ShapeDtypeStruct((PAIRS, 2, length), F32),
        ],
        compiler_params=pltpu.CompilerParams(vmem_limit_bytes=48 * MIB),
        cost_estimate=pl.CostEstimate(
            flops=PAIRS * 8 * LANES * length * length,
            bytes_accessed=8 * length * width,
            transcendentals=PAIRS * length * length,
        ),
        name="attention",
    )(q, k, v)


def attention_back_kernel(q_ref, k_ref, v_ref, o_ref, do_ref, log_ref, own_ref, ahead_ref, behind_ref,
                          dq_ref, dk_ref, dv_ref, total_ref):
    length = q_ref.shape[0]
    block = min(256, length)
    tables = lambda rows: (own_ref[rows, :], ahead_ref[rows, :], behind_ref[rows, :])
    product = (do_ref[...].astype(F32) * o_ref[...].astype(F32)).T
    deltas = (
        jnp.sum(product[:HD], axis=0, keepdims=True),
        jnp.sum(product[HD:], axis=0, keepdims=True),
    )
    keys = halves(k_ref[...].T, 0)
    for start in range(0, length, block):
        stop = start + block
        queries = halves(q_ref[start:, :], 1)
        grads = halves(do_ref[start:, :], 1)
        dk = dv = dq = None
        for head in range(2):
            scores = dot(k_ref[start:stop, :], queries[head], NT) * (SCALE * LOG2E)
            probs = jnp.exp2(scores - log_ref[0, head : head + 1, start:])
            first = jnp.where(not_after(block), probs[:, :block], 0.0)
            probs = jnp.concatenate([first, probs[:, block:]], axis=1) if stop < length else first
            dprobs = dot(v_ref[start:stop, :], grads[head], NT)
            dscores = (probs * (dprobs - deltas[head][:, start:])).astype(BF)
            parts = (
                dot(probs.astype(BF), grads[head], NN),
                dot(dscores, queries[head], NN),
                dot(keys[head][:, start:stop], dscores, NN),
            )
            dv = parts[0] if dv is None else dv + parts[0]
            dk = parts[1] if dk is None else dk + parts[1]
            dq = parts[2] if dq is None else dq + parts[2]
        dv_ref[start:stop, :] = dv.astype(BF)
        dk_ref[start:stop, :] = unrotate(dk * SCALE, *tables(slice(start, stop))).astype(BF)
        if start == 0:
            total_ref[...] = dq
        else:
            total_ref[:, start:] += dq
    dq_ref[...] = unrotate(total_ref[...].T * SCALE, *tables(slice(None))).astype(BF)


def attention_back(q, k, v, o, do, logs, tables):
    length, width = q.shape
    spec = pl.BlockSpec((length, LANES), lambda i: (0, i))
    return pl.pallas_call(
        attention_back_kernel,
        grid=(PAIRS,),
        in_specs=[spec] * 5 + [pl.BlockSpec((1, 2, length), lambda i: (i, 0, 0))] + [resident(length, LANES)] * 3,
        out_specs=[spec] * 3,
        out_shape=[jax.ShapeDtypeStruct((length, width), BF)] * 3,
        scratch_shapes=[pltpu.VMEM((LANES, length), F32)],
        compiler_params=pltpu.CompilerParams(vmem_limit_bytes=48 * MIB),
        cost_estimate=pl.CostEstimate(
            flops=PAIRS * 20 * LANES * length * length,
            bytes_accessed=16 * length * width,
            transcendentals=PAIRS * length * length,
        ),
        name="attention_back",
    )(q, k, v, o, do, logs, *tables)


def feed_forward_kernel(x_ref, o_ref, og_ref, factor_ref, gain_ref, wout_ref, wg_ref, wu_ref, wd_ref,
                        mixed_ref, dh_ref, do_ref, gout_ref, gg_ref, gu_ref, gd_ref, dgain_ref,
                        h_ref, acc_ref, da2_ref, a2_ref, a2t_ref, dyb_ref, hid_ref, dgu_ref):
    step = pl.program_id(0)
    last = pl.num_programs(0) - 1
    length, width = x_ref.shape
    chunk = wg_ref.shape[1]
    tile = min(256, length)
    gain = gain_ref[...].astype(F32)

    @pl.when(step == 0)
    def _():
        for m in range(0, length, tile):
            rows = pl.ds(m, tile)
            h = x_ref[rows, :].astype(F32) + dot(o_ref[rows, :], wout_ref[...], NN)
            h_ref[rows, :] = h
            acc_ref[rows, :] = h
            inverse = lax.rsqrt(jnp.mean(h * h, axis=1, keepdims=True) + EPSILON_NORM)
            a2 = (h * inverse * gain).astype(BF)
            a2_ref[rows, :] = a2
            a2t_ref[:, rows] = a2.T
            dyb_ref[rows, :] = (og_ref[rows, :].astype(F32) * factor_ref[rows, :]).astype(BF)
            da2_ref[rows, :] = jnp.zeros((tile, width), F32)

    for m in range(0, length, tile):
        rows = pl.ds(m, tile)
        gate = dot(a2_ref[rows, :], wg_ref[...], NN)
        up = dot(a2_ref[rows, :], wu_ref[...], NN)
        dhid = dot(dyb_ref[rows, :], wd_ref[...], NT)
        sig = 1.0 / (1.0 + jnp.exp2(gate * -LOG2E))
        act = gate * sig
        hid_ref[rows, :] = (act * up).astype(BF)
        dgu_ref[rows, :chunk] = (dhid * up * (sig + act * (1.0 - sig))).astype(BF)
        dgu_ref[rows, chunk:] = (dhid * act).astype(BF)
    for m in range(0, length, tile):
        rows = pl.ds(m, tile)
        acc_ref[rows, :] += dot(hid_ref[rows, :], wd_ref[...], NN)
        da2_ref[rows, :] += dot(dgu_ref[rows, :chunk], wg_ref[...], NT) + dot(
            dgu_ref[rows, chunk:], wu_ref[...], NT
        )
    gd_ref[...] = dot(hid_ref[...], dyb_ref[...], TN).astype(BF)
    gg_ref[...] = dot(a2t_ref[...], dgu_ref[:, :chunk], NN).astype(BF)
    gu_ref[...] = dot(a2t_ref[...], dgu_ref[:, chunk:], NN).astype(BF)

    @pl.when(step == last)
    def _():
        total = jnp.zeros((1, width), F32)
        for m in range(0, length, tile):
            rows = pl.ds(m, tile)
            mixed_ref[rows, :] = acc_ref[rows, :].astype(BF)
            h = h_ref[rows, :]
            inverse = lax.rsqrt(jnp.mean(h * h, axis=1, keepdims=True) + EPSILON_NORM)
            hat = h * inverse
            da2 = da2_ref[rows, :]
            total = total + jnp.sum(da2 * hat, axis=0, keepdims=True)
            scaled = da2 * gain
            dy = og_ref[rows, :].astype(F32) * factor_ref[rows, :]
            dh = dy + inverse * (scaled - hat * jnp.mean(scaled * hat, axis=1, keepdims=True))
            dh_ref[rows, :] = dh
            low = dh.astype(BF)
            dyb_ref[rows, :] = low
            do_ref[rows, :] = dot(low, wout_ref[...], NT).astype(BF)
        dgain_ref[...] = total
        gout_ref[...] = dot(o_ref[...], dyb_ref[...], TN).astype(BF)


def feed_forward(x, o, out_grad, factor, gain, w_out, w_gate, w_down):
    length, width = x.shape
    chunk = 256
    steps = FF // chunk
    grid = lambda block, index: pl.BlockSpec(block, index)
    columns = lambda shift: pl.BlockSpec((width, chunk), lambda i: (0, i + shift))
    rows = pl.BlockSpec((chunk, width), lambda i: (i, 0))
    shape = jax.ShapeDtypeStruct
    return pl.pallas_call(
        feed_forward_kernel,
        grid=(steps,),
        in_specs=[
            resident(length, width),
            resident(length, QUERY_WIDTH),
            resident(length, width),
            resident(length, 1),
            resident(1, width),
            resident(QUERY_WIDTH, width),
            columns(0),
            columns(steps),
            rows,
        ],
        out_specs=[
            resident(length, width),
            resident(length, width),
            resident(length, QUERY_WIDTH),
            resident(QUERY_WIDTH, width),
            columns(0),
            columns(0),
            rows,
            resident(1, width),
        ],
        out_shape=[
            shape((length, width), BF),
            shape((length, width), F32),
            shape((length, QUERY_WIDTH), BF),
            shape((QUERY_WIDTH, width), BF),
            shape((width, FF), BF),
            shape((width, FF), BF),
            shape((FF, width), BF),
            shape((1, width), F32),
        ],
        scratch_shapes=[
            pltpu.VMEM((length, width), F32),
            pltpu.VMEM((length, width), F32),
            pltpu.VMEM((length, width), F32),
            pltpu.VMEM((length, width), BF),
            pltpu.VMEM((width, length), BF),
            pltpu.VMEM((length, width), BF),
            pltpu.VMEM((length, chunk), BF),
            pltpu.VMEM((length, 2 * chunk), BF),
        ],
        compiler_params=pltpu.CompilerParams(vmem_limit_bytes=58 * MIB),
        cost_estimate=pl.CostEstimate(
            flops=2 * length * width * (9 * FF + 3 * QUERY_WIDTH),
            bytes_accessed=60 * MIB,
            transcendentals=length * FF,
        ),
        name="feed_forward",
    )(x, o, out_grad, factor, gain, w_out, w_gate, w_gate, w_down)


def unproject_kernel(a1_ref, c_ref, dq_ref, dk_ref, dv_ref, wup_ref, dc_ref, ginq_ref, ginc_ref, gup_ref, a1t_ref):
    head = pl.program_id(0)

    @pl.when(head == 0)
    def _():
        a1t_ref[...] = a1_ref[...].T

    dc = (
        dot(dk_ref[...], wup_ref[:, :GROUP_WIDTH], NT) + dot(dv_ref[...], wup_ref[:, GROUP_WIDTH:], NT)
    ).astype(BF)
    dc_ref[...] = dc
    latent = c_ref[...].T
    gup_ref[:, :GROUP_WIDTH] = dot(latent, dk_ref[...], NN).astype(BF)
    gup_ref[:, GROUP_WIDTH:] = dot(latent, dv_ref[...], NN).astype(BF)
    ginc_ref[...] = dot(a1t_ref[...], dc, NN).astype(BF)
    ginq_ref[...] = dot(a1t_ref[...], dq_ref[...], NN).astype(BF)


def unproject(a1, c, dq, dk, dv, w_up):
    length, width = a1.shape
    group = pl.BlockSpec((length, GROUP_WIDTH), lambda g: (0, g))
    latent = pl.BlockSpec((length, LATENT_WIDTH), lambda g: (0, g))
    up = pl.BlockSpec((LATENT_WIDTH, 2 * GROUP_WIDTH), lambda g: (g, 0))
    shape = jax.ShapeDtypeStruct
    latents = LATENT_HEADS * LATENT_WIDTH
    return pl.pallas_call(
        unproject_kernel,
        grid=(LATENT_HEADS,),
        in_specs=[resident(length, width), latent, group, group, group, up],
        out_specs=[
            latent,
            pl.BlockSpec((width, GROUP_WIDTH), lambda g: (0, g)),
            pl.BlockSpec((width, LATENT_WIDTH), lambda g: (0, g)),
            up,
        ],
        out_shape=[
            shape((length, latents), BF),
            shape((width, QUERY_WIDTH), BF),
            shape((width, latents), BF),
            shape((latents, 2 * GROUP_WIDTH), BF),
        ],
        scratch_shapes=[pltpu.VMEM((width, length), BF)],
        compiler_params=pltpu.CompilerParams(vmem_limit_bytes=56 * MIB),
        cost_estimate=pl.CostEstimate(
            flops=2 * length * (width * (QUERY_WIDTH + latents) + 4 * latents * GROUP_WIDTH),
            bytes_accessed=16 * MIB,
            transcendentals=0,
        ),
        name="unproject",
    )(a1, c, dq, dk, dv, w_up)


def input_grad_kernel(x_ref, dh_ref, dq_ref, dc_ref, gain_ref, win_ref, out_ref, dgain_ref):
    x = x_ref[...].astype(F32)
    inverse = lax.rsqrt(jnp.mean(x * x, axis=1, keepdims=True) + EPSILON_NORM)
    hat = x * inverse
    da1 = dot(dq_ref[...], win_ref[:, :QUERY_WIDTH], NT) + dot(dc_ref[...], win_ref[:, QUERY_WIDTH:], NT)
    part = jnp.sum(da1 * hat, axis=0, keepdims=True)
    scaled = da1 * gain_ref[...].astype(F32)
    out_ref[...] = (
        dh_ref[...] + inverse * (scaled - hat * jnp.mean(scaled * hat, axis=1, keepdims=True))
    ).astype(BF)

    @pl.when(pl.program_id(0) == 0)
    def _():
        dgain_ref[...] = part

    @pl.when(pl.program_id(0) > 0)
    def _():
        dgain_ref[...] += part


def input_grad(x, dh, dq, dc, gain, w_in):
    length, width = x.shape
    tile = min(256, length)
    rows = lambda columns: pl.BlockSpec((tile, columns), lambda i: (i, 0))
    return pl.pallas_call(
        input_grad_kernel,
        grid=(length // tile,),
        in_specs=[rows(width), rows(width), rows(QUERY_WIDTH), rows(dc.shape[1]), resident(1, width), resident(*w_in.shape)],
        out_specs=[rows(width), resident(1, width)],
        out_shape=[jax.ShapeDtypeStruct((length, width), BF), jax.ShapeDtypeStruct((1, width), F32)],
        compiler_params=pltpu.CompilerParams(vmem_limit_bytes=48 * MIB),
        cost_estimate=pl.CostEstimate(flops=2 * length * w_in.size, bytes_accessed=16 * MIB, transcendentals=0),
        name="input_grad",
    )(x, dh, dq, dc, gain, w_in)


class Ring:
    def __init__(self, data, line):
        self.cores = 2 if data % 2 == 0 else 1
        self.plane, self.line = data // self.cores, line
        place = lax.axis_index("dp")
        self.core, self.at, self.z = place % self.cores, place // self.cores, lax.axis_index("fsdp")

    def partner(self, index, shift, count):
        if count & (count - 1) == 0:
            return index ^ shift
        return (index + shift) % count

    def send_core(self, value):
        swap = [(i, i ^ 1) for i in range(self.plane * 2)]
        return lax.ppermute(value, "dp", swap)

    def send_plane(self, value, shift):
        pairs = [
            (p * self.cores + c, self.partner(p, shift, self.plane) * self.cores + c)
            for p in range(self.plane)
            for c in range(self.cores)
        ]
        return lax.ppermute(value, "dp", pairs)

    def send_line(self, value, shift):
        return lax.ppermute(value, "fsdp", [(i, (i + shift) % self.line) for i in range(self.line)])


def take(array, index, axis):
    return lax.dynamic_index_in_dim(array, index, axis, keepdims=False)


def sum_core(ring, grad):
    columns = grad.shape[1]
    rows = grad.shape[0] // (ring.plane * ring.cores * ring.line)
    grad = grad.reshape(ring.plane, ring.cores, ring.line, rows, columns)
    if ring.cores == 1:
        return grad[:, 0]
    received = ring.send_core(take(grad, 1 - ring.core, 1))
    return (take(grad, ring.core, 1).astype(F32) + received.astype(F32)).astype(BF)


def sum_plane(ring, grad):
    total = take(grad, ring.at, 0).astype(F32)
    for shift in range(1, ring.plane):
        total += ring.send_plane(take(grad, ring.partner(ring.at, shift, ring.plane), 0), shift).astype(F32)
    return total


def sum_line(ring, grad, axis):
    total = take(grad, ring.z, axis).astype(F32)
    for shift in range(1, ring.line):
        total += ring.send_line(take(grad, (ring.z + shift) % ring.line, axis), shift).astype(F32)
    return total


def plane_first(ring, grad):
    return sum_line(ring, sum_plane(ring, sum_core(ring, grad)).astype(BF), 0)


def line_first(ring, grad):
    return sum_plane(ring, sum_line(ring, sum_core(ring, grad), 1).astype(BF))


def sum_all(ring, value):
    if ring.cores == 2:
        value = value + ring.send_core(value)
    for count, send in ((ring.plane, ring.send_plane), (ring.line, None)):
        if count & (count - 1):
            return lax.psum(value, AXES)
    shift = 1
    while shift < ring.plane:
        value = value + ring.send_plane(value, shift)
        shift *= 2
    shift = 1
    while shift < ring.line:
        swap = [(i, i ^ shift) for i in range(ring.line)]
        value = value + lax.ppermute(value, "fsdp", swap)
        shift *= 2
    return value


def adamw(master, grad, first, second, rate, decay):
    first_new = BETA_ONE * first + (1.0 - BETA_ONE) * grad
    second_new = BETA_TWO * second + (1.0 - BETA_TWO) * grad * grad
    first_hat = first_new / (1.0 - BETA_ONE**STEP)
    second_hat = second_new / (1.0 - BETA_TWO**STEP)
    master_new = master - rate * (
        first_hat / (jnp.sqrt(second_hat) + EPSILON_ADAM) + decay * master
    )
    return (master_new, first_new, second_new)


def gather(piece, axis=0):
    return lax.all_gather(piece, AXES, axis=axis, tiled=True)


def shards(data, line, tokens, out_grad, domain_ids, domain_scale, *state):
    masters, moments = state[:6], state[6:]
    firsts, seconds = moments[0::2], moments[1::2]
    ring = Ring(data, line)
    length, width = tokens.shape
    lowered = tuple(w.astype(BF) for w in masters)
    w_in = gather(lowered[0])
    gains = gather(lowered[5], 1)
    w_up = gather(lowered[1])
    w_out = gather(lowered[2])
    w_gate = gather(lowered[3])
    w_down = gather(lowered[4])
    tables = rotation_tables(length)
    factor = jnp.sum(
        jnp.where(domain_ids[:, None] == jnp.arange(NDOM)[None, :], domain_scale[None, :], 0.0),
        axis=1,
        keepdims=True,
    )
    a1, q, k, v, c = project(tokens, gains[:1], w_in, w_up, tables)
    o, logs = attention(q, k, v)
    mixed, dh, do, g_out, g_gate, g_upper, g_down, dgain_two = feed_forward(
        tokens, o, out_grad, factor, gains[1:], w_out, w_gate, w_down
    )
    sum_down = line_first(ring, g_down)
    sum_gate = plane_first(ring, g_gate)
    sum_upper = plane_first(ring, g_upper)
    sum_out = line_first(ring, g_out)
    dq, dk, dv = attention_back(q, k, v, o, do, logs, tables)
    dc, g_query, g_latent_in, g_up = unproject(a1, c, dq, dk, dv, w_up)
    sum_query = plane_first(ring, g_query)
    sum_latent_in = plane_first(ring, g_latent_in)
    sum_up = line_first(ring, g_up)
    given, dgain_one = input_grad(tokens, dh, dq, dc, gains[:1], w_in)
    owned = [
        jnp.concatenate([sum_query, sum_latent_in], axis=1),
        sum_up,
        sum_out,
        jnp.concatenate([sum_gate, sum_upper], axis=1),
        sum_down,
    ]
    squares = sum(jnp.sum(grad * grad) for grad in owned)
    dgains = jnp.concatenate([dgain_one, dgain_two], axis=0)
    message = jnp.concatenate(
        [dgains.reshape(-1, LANES), jnp.full((8, LANES), squares, F32)], axis=0
    )
    message = sum_all(ring, message)
    dgains = message[:-8].reshape(2, width)
    grad_norm = jnp.sqrt(message[-1, 0] + jnp.sum(dgains * dgains))
    clip = jnp.minimum(1.0, MAX_NORM / (grad_norm + 1e-06))
    share = masters[5].shape[1]
    place = lax.axis_index("dp") * line + lax.axis_index("fsdp")
    owned.append(lax.dynamic_slice_in_dim(dgains, place * share, share, 1))
    results = []
    for index in range(6):
        if index == 5:
            rate, decay = (RATE_GAIN, 0.0)
        elif index == 2:
            rate, decay = (RATE_OUTPUT, DECAY_MATRIX)
        else:
            rate, decay = (RATE_MATRIX, DECAY_MATRIX)
        results.extend(
            adamw(masters[index], clip * owned[index], firsts[index], seconds[index], rate, decay)
        )
    return (mixed, given, grad_norm, *results)


def solution(mesh):
    data, line = mesh.shape["dp"], mesh.shape["fsdp"]
    rows, flat, columns = P(AXES, None), P(AXES), P(None, AXES)

    def run(*arrays):
        return shards(data, line, *arrays)

    return jax.shard_map(
        run,
        mesh=mesh,
        in_specs=(rows, rows, flat, P()) + (rows,) * 5 + (columns,) + (rows,) * 10 + (columns,) * 2,
        out_specs=(rows, rows, P()) + (rows,) * 15 + (columns,) * 3,
        check_vma=False,
    )
```

time: 2010 us -> 757 us (0.38)
  waiting for transfers between devices: 1330 us -> 358 us
  matrix products: 423 us -> 0 us
  Pallas kernels: 0 us -> 163 us
  starting transfers between devices: 0.67 us -> 71.4 us
  blocking collectives: 108 us -> 69.3 us
  other arithmetic: 75.5 us -> 38.1 us
    reduce_scatter x5 -> x0, waiting for transfers between devices: 1140 us -> none  [the longest x1 493 us: spread(): lax.psum_scatter(grad_gate, ('dp', 'fsdp'), scatter_dimension=0, tiled=True)]
    dot_general x27 -> x0, matrix products: 423 us -> none  [the longest x2 92.7 us: shards(): jnp.einsum('hqk,khd->qhd', grad_scores, keys[:stop], preferred_element_ty...]
    pallas_call x0 -> x6, Pallas kernels: none -> 163 us  [the longest x1 75.9 us: feed_forward(): pl.pallas_call(feed_forward_kernel, grid=(steps,), in_specs=[resident(len...]
    ppermute x0 -> x54, waiting for transfers between devices: none -> 140 us  [the longest x21 69.3 us: send_line(): lax.ppermute(value, 'fsdp', [(i, (i + shift) % self.line) for i in range(...]
    all_gather x5, waiting for transfers between devices: 127 us -> 218 us  [gather(): return lax.all_gather(piece, AXES, axis=axis, tiled=True)]
    ppermute x0 -> x54, starting transfers between devices: none -> 71.1 us  [the longest x21 39.7 us: send_line(): lax.ppermute(value, 'fsdp', [(i, (i + shift) % self.line) for i in range(...]
    unnamed x12 -> x5, waiting for transfers between devices: 57.5 us -> 0.08 us
    psum x1 -> x0, blocking collectives: 38.7 us -> none  [shards(): grad_norm = jnp.sqrt(lax.psum(local_squares, ('dp', 'fsdp')))]
  transfers between devices with their start and end apart: 11 -> 59, of which waited for: 9 -> 34; matrix products, arithmetic and copies ran while one was open for 11% -> 6% of each run, Pallas kernels for 0% -> 5%
where the time goes in v1:
time: 757 us; the launch traced here: 749 us
  waiting for transfers between devices  358 us (47%)
  Pallas kernels  163 us (22%)
  starting transfers between devices  71.4 us (9%)
  blocking collectives  69.3 us (9%)
  other arithmetic  38.1 us (5%)
  local copies, waits for them, and re-layouts  29.1 us (4%)
  between operations  20.6 us (3%)
    all_gather x5, waiting for transfers between devices, gather(): return lax.all_gather(piece, AXES, axis=axis, tiled=True)  218 us
    pallas_call x1, Pallas kernels, feed_forward(): pl.pallas_call(feed_forward_kernel, grid=(steps,), in_specs=[resident(len...  75.9 us
    ppermute x21, waiting for transfers between devices, send_line(): lax.ppermute(value, 'fsdp', [(i, (i + shift) % self.line) for i in range(...  69.3 us
    all_gather x1, blocking collectives, gather(): return lax.all_gather(piece, AXES, axis=axis, tiled=True)  69.3 us
    ppermute x23, waiting for transfers between devices, send_plane(): return lax.ppermute(value, 'dp', pairs)  63.8 us
    ppermute x21, starting transfers between devices, send_line(): lax.ppermute(value, 'fsdp', [(i, (i + shift) % self.line) for i in range(...  39.7 us
    pallas_call x1, Pallas kernels, attention_back(): pl.pallas_call(attention_back_kernel, grid=(PAIRS,), in_specs=[spec] * 5...  32.8 us
    ppermute x23, starting transfers between devices, send_plane(): return lax.ppermute(value, 'dp', pairs)  27.6 us
  transfers between devices with their start and end apart: 59, of which 34 were waited for; matrix products, arithmetic and copies ran while one was open for 6% of the time, Pallas kernels for 5%

profile of v1, /device:TPU:0, one launch (start us, length us, event | category | flops | bytes accessed | tf_op | source)
XLA Modules:
  0.0 749.4 jit_solution(14836585597210937509)
XLA Ops:
  15.8 69.3 %all-gather = bf16[32,32,2]{1,2,0:T(2,128)(2,1)S(1)} all-gather(bf16[1,32,2]{1,2,0:T(2,128)(2,1)S(1)} %convert_bitcast_fusion), channel_id=1, replica_groups=mesh['dp'=8,'fsdp'=4] {'dp','fsdp'}, dimensions={0}, use_global_device_ids=true | all-gather | bytes 4224 | tf_op jit(solution)/shard_map/all_gather | solution.py:554
  92.8 36.8 %all-gather.7.cloned.1.call-done.win_ref = bf16[1024,1536]{1,0:T(8,128)(2,1)} async-done(((bf16[32,1536]{1,0:T(8,128)(2,1)}), bf16[1024,1536]{1,0:T(8,128)(2,1)}) %all-gather.7.cloned.1.call-update) | async-done | bytes 3145744 | tf_op jit(solution)/shard_map/all_gather | solution.py:554
  130.8 10.3 %project.1 = (bf16[1024,1024]{1,0:T(8,128)(2,1)S(1)}, bf16[1024,1024]{1,0:T(8,128)(2,1)}, bf16[1024,1024]{1,0:T(8,128)(2,1)}, bf16[1024,1024]{1,0:T(8,128)(2,1)}, bf16[1024,512]{1,0:T(8,128)(2,1)S(1)}) custom-call(bf16[1024,1024]{1,0:T(8,128)(2,1)} %x_ref.5, bf16[1,1024]{1,0:T(2,128)(2,1)S(1)} %get-tuple-element.147.gain_ref, ...), custom_call_target="tpu_custom_call" | custom-call | flops 4294967296 | bytes 16777216 | tf_op jit(solution)/shard_map/project/pallas_call | solution.py:113
  145.1 24.3 %attention.1 = (bf16[1024,1024]{1,0:T(8,128)(2,1)S(1)}, f32[8,2,1024]{2,1,0:T(2,128)S(1)}) custom-call(bf16[1024,1024]{1,0:T(8,128)(2,1)S(1)} %copy-done.6, bf16[1024,1024]{1,0:T(8,128)(2,1)} %get-tuple-element.46.k_ref, bf16[1024,1024]{1,0:T(8,128)(2,1)} %get-tuple-element.47.v_ref), custom_call_target="tpu_custom_call" | custom-call | flops 8589934592 | bytes 8388608 | tf_op jit(solution)/shard_map/attention/pallas_call | solution.py:165
  170.7 17.8 %all-gather.11.cloned.1.call-done.wout_ref = bf16[1024,1024]{1,0:T(8,128)(2,1)} async-done(((bf16[32,1024]{1,0:T(8,128)(2,1)}), bf16[1024,1024]{1,0:T(8,128)(2,1)}) %all-gather.11.cloned.1.call-update) | async-done | bytes 2097168 | tf_op jit(solution)/shard_map/all_gather | solution.py:554
  188.4 69.5 %all-gather.15.cloned.1.call-done.wd_ref = bf16[2816,1024]{1,0:T(8,128)(2,1)} async-done(((bf16[88,1024]{1,0:T(8,128)(2,1)}), bf16[2816,1024]{1,0:T(8,128)(2,1)}) %all-gather.15.cloned.1.call-update) | async-done | bytes 5767184 | tf_op jit(solution)/shard_map/all_gather | solution.py:554
  257.9 93.5 %all-gather.13.cloned.1.call-done.wg_ref.wu_ref = bf16[1024,5632]{1,0:T(8,128)(2,1)} async-done(((bf16[32,5632]{1,0:T(8,128)(2,1)}), bf16[1024,5632]{1,0:T(8,128)(2,1)}) %all-gather.13.cloned.1.call-update) | async-done | bytes 11534352 | tf_op jit(solution)/shard_map/all_gather | solution.py:554
  351.4 75.9 %feed_forward.1 = (bf16[1024,1024]{1,0:T(8,128)(2,1)}, f32[1024,1024]{1,0:T(8,128)}, bf16[1024,1024]{1,0:T(8,128)(2,1)}, bf16[1024,1024]{1,0:T(8,128)(2,1)}, bf1...) custom-call(bf16[1024,1024]{1,0:T(8,128)(2,1)} %x_ref.5, ...), custom_call_target="tpu_custom_call" | custom-call | flops 59592671232 | bytes 62914560 | tf_op jit(solution)/shard_map/feed_forward/pallas_call | solution.py:318
  427.3 32.8 %attention_back.1 = (bf16[1024,1024]{1,0:T(8,128)(2,1)S(1)}, bf16[1024,1024]{1,0:T(8,128)(2,1)S(1)}, bf16[1024,1024]{1,0:T(8,128)(2,1)}) custom-call(bf16[1024,1024]{1,0:T(8,128)(2,1)} %get-tuple-element.45.q_ref, bf16[1024,1024]{1,0:T(8,128)(2,1)} %get-tuple-element.46.k_ref, bf16[1024,1024]{1,0:T(8,128)(2,1)} %get-tuple-element.47.v_ref, ...), custom_call_target="tpu_custom_call" | custom-call | flops 21474836480 | bytes 16777216 | tf_op jit(solution)/shard_map/attention_back/pallas_call | solution.py:227
  462.7 11.6 %unproject.1 = (bf16[1024,512]{1,0:T(8,128)(2,1)}, bf16[1024,1024]{1,0:T(8,128)(2,1)}, bf16[1024,512]{1,0:T(8,128)(2,1)}, bf16[512,1024]{1,0:T(8,128)(2,1)}) custom-call(bf16[1024,1024]{1,0:T(8,128)(2,1)} %copy-done.5, bf16[1024,512]{1,0:T(8,128)(2,1)} %copy-done.8, bf16[1024,1024]{1,0:T(8,128)(2,1)} %copy-done.1, bf16[1024,1024]{1,0:T(8,128)(2,1)} %copy-done.7, ...), custom_call_target="tpu_custom_call" | custom-call | flops 5368709120 | bytes 16777216 | tf_op jit(solution)/shard_map/unproject/pallas_call | solution.py:397
  475.5 8.3 %input_grad.1 = (bf16[1024,1024]{1,0:T(8,128)(2,1)}, f32[1,1024]{1,0:T(1,128)S(1)}) custom-call(bf16[1024,1024]{1,0:T(8,128)(2,1)S(1)} %copy-done, f32[1024,1024]{1,0:T(8,128)} %get-tuple-element.50.dh_ref, bf16[1024,1024]{1,0:T(8,128)(2,1)S(1)} %copy-done.2, bf16[1024,512]{1,0:T(8,128)(2,1)S(1)} %copy-done.3, ...), custom_call_target="tpu_custom_call" | custom-call | flops 3221225472 | bytes 16777216 | tf_op jit(solution)/shard_map/input_grad/pallas_call | solution.py:448
  487.3 4.0 dynamic-slice_bitcast_fusion
  500.5 3.5 collective-permute-done.10
  509.0 9.4 %collective-permute-done.16 = bf16[4,16,1024]{2,1,0:T(8,128)(2,1)S(1)} collective-permute-done((bf16[4,16,1024]{2,1,0:T(8,128)(2,1)S(1)}, bf16[4,16,1024]{2,1,0:T(8,128)(2,1)S(1)}, u32[]{:S(2)}, u32[]{:S(2)}) %collective-permute-start.16) | collective-permute-done | bytes 131104 | tf_op jit(solution)/shard_map/ppermute | solution.py:485
  525.7 5.1 collective-permute-done.11
  531.0 3.0 collective-permute-start.24
  541.3 14.3 %collective-permute-done.23 = bf16[4,32,1024]{2,1,0:T(8,128)(2,1)S(1)} collective-permute-done((bf16[4,32,1024]{2,1,0:T(8,128)(2,1)S(1)}, bf16[4,32,1024]{2,1,0:T(8,128)(2,1)S(1)}, u32[]{:S(2)}, u32[]{:S(2)}) %collective-permute-start.23) | collective-permute-done | bytes 262176 | tf_op jit(solution)/shard_map/ppermute | solution.py:485
  574.2 3.4 fusion.1
  581.4 3.4 fusion.2
  587.7 3.2 fusion
  591.1 6.7 collective-permute-done.38
  599.0 25.3 %collective-permute-done.37 = bf16[4,32,2816]{2,1,0:T(8,128)(2,1)S(1)} collective-permute-done((bf16[4,32,2816]{2,1,0:T(8,128)(2,1)S(1)}, bf16[4,32,2816]{2,1,0:T(8,128)(2,1)S(1)}, u32[]{:S(2)}, u32[]{:S(2)}) %collective-permute-start.37) | collective-permute-done | bytes 720928 | tf_op jit(solution)/shard_map/ppermute | solution.py:482
  624.7 4.0 collective-permute-done.31
  629.3 12.2 %collective-permute-done.30 = bf16[4,32,2816]{2,1,0:T(8,128)(2,1)S(1)} collective-permute-done((bf16[4,32,2816]{2,1,0:T(8,128)(2,1)S(1)}, bf16[4,32,2816]{2,1,0:T(8,128)(2,1)S(1)}, u32[]{:S(2)}, u32[]{:S(2)}) %collective-permute-start.30) | collective-permute-done | bytes 720928 | tf_op jit(solution)/shard_map/ppermute | solution.py:482
  643.6 19.0 %collective-permute-start.39 = (bf16[32,2816]{1,0:T(8,128)(2,1)S(1)}, bf16[32,2816]{1,0:T(8,128)(2,1)S(1)}, u32[]{:S(2)}, u32[]{:S(2)}) collective-permute-start(bf16[32,2816]{1,0:T(8,128)(2,1)S(1)} %get-tuple-element.120), channel_id=1, source_target_pairs={{0,1},{1,2},{2,3},{3,0},{4,5},{5,6},{6,7},{7,4},{8,9},{9,10},{10,1... | collective-permute-start | bytes 540680 | tf_op jit(solution)/shard_map/ppermute | solution.py:485
  662.6 23.9 %collective-permute-done.44 = bf16[4,88,1024]{2,1,0:T(8,128)(2,1)S(1)} collective-permute-done((bf16[4,88,1024]{2,1,0:T(8,128)(2,1)S(1)}, bf16[4,88,1024]{2,1,0:T(8,128)(2,1)S(1)}, u32[]{:S(2)}, u32[]{:S(2)}) %collective-permute-start.44) | collective-permute-done | bytes 720928 | tf_op jit(solution)/shard_map/ppermute | solution.py:485
  686.5 3.8 collective-permute-start.33
  692.8 9.2 %collective-permute-done.40 = bf16[32,2816]{1,0:T(8,128)(2,1)S(1)} collective-permute-done((bf16[32,2816]{1,0:T(8,128)(2,1)S(1)}, bf16[32,2816]{1,0:T(8,128)(2,1)S(1)}, u32[]{:S(2)}, u32[]{:S(2)}) %collective-permute-start.40) | collective-permute-done | bytes 180256 | tf_op jit(solution)/shard_map/ppermute | solution.py:485
  705.6 2.8 collective-permute-done.33
  723.3 2.7 collective-permute-done.52
  727.4 3.1 collective-permute-done.53
  735.1 3.1 multiply_subtract_fusion
  (260 shorter events, 113.5 us)
Async XLA Ops:
  7.2 85.6 %all-gather.9.cloned.1.call-start = ((), (), s32[]{:S(2)}) async-start(), calls=%async_computation.1 | async-start | bytes 1081344 | tf_op jit(solution)/shard_map/all_gather | solution.py:554
  8.7 120.9 %all-gather.7.cloned.1.call-start = ((), (), s32[]{:S(2)}) async-start(), calls=%async_computation | async-start | bytes 3244032 | tf_op jit(solution)/shard_map/all_gather | solution.py:554
  10.4 178.1 %all-gather.11.cloned.1.call-start = ((), (), s32[]{:S(2)}) async-start(), calls=%async_computation.2 | async-start | bytes 2162688 | tf_op jit(solution)/shard_map/all_gather | solution.py:554
  12.0 245.9 %all-gather.15.cloned.1.call-start = ((), (), s32[]{:S(2)}) async-start(), calls=%async_computation.4 | async-start | bytes 5947392 | tf_op jit(solution)/shard_map/all_gather | solution.py:554
  13.8 337.7 %all-gather.13.cloned.1.call-start = ((), (), s32[]{:S(2)}) async-start(), calls=%async_computation.3 | async-start | bytes 11894784 | tf_op jit(solution)/shard_map/all_gather | solution.py:554
  484.0 12.5 %collective-permute-start.7 = (bf16[4,4,32,512]{3,2,1,0:T(8,128)(2,1)S(1)}, bf16[4,4,32,512]{3,2,1,0:T(8,128)(2,1)S(1)}, u32[]{:S(2)}, u32[]{:S(2)}) collective-permute-start(bf16[4,4,32,512]{3,2,1,0:T(8,128)(2,1)S(1)} %dynamic-slice_bitcast_fusion.12), channel_id=1, source_target_pairs={{0,4},{4,0},{8,12},{12,8},{16,20},{20,16},{24,28},{28,24},{1,5},{5... | collective-permute-start | bytes 1572872 | tf_op jit(solution)/shard_map/ppermute | solution.py:474
  485.8 34.5 %collective-permute-start = (bf16[4,4,32,1024]{3,2,1,0:T(8,128)(2,1)S(1)}, bf16[4,4,32,1024]{3,2,1,0:T(8,128)(2,1)S(1)}, u32[]{:S(2)}, u32[]{:S(2)}) collective-permute-start(bf16[4,4,32,1024]{3,2,1,0:T(8,128)(2,1)S(1)} %dynamic-slice_bitcast_fusion.2), channel_id=1, source_target_pairs={{0,4},{4,0},{8,12},{12,8},{16,20},{20,16},{24,28},{28,24},{1,5},{5... | collective-permute-start | bytes 3145736 | tf_op jit(solution)/shard_map/ppermute | solution.py:474
  486.3 13.6 %collective-permute-start.14 = (bf16[4,4,16,1024]{3,2,0,1:T(8,128)(2,1)S(1)}, bf16[4,4,16,1024]{3,2,0,1:T(8,128)(2,1)S(1)}, u32[]{:S(2)}, u32[]{:S(2)}) collective-permute-start(bf16[4,4,16,1024]{3,2,0,1:T(8,128)(2,1)S(1)} %bitcast.213), channel_id=1, source_target_pairs={{0,4},{4,0},{8,12},{12,8},{16,20},{20,16},{24,28},{28,24},{1,5},{5... | collective-permute-start | bytes 1572872 | tf_op jit(solution)/shard_map/ppermute | solution.py:474
  487.0 37.2 %collective-permute-start.21 = (bf16[4,4,32,1024]{3,2,0,1:T(8,128)(2,1)S(1)}, bf16[4,4,32,1024]{3,2,0,1:T(8,128)(2,1)S(1)}, u32[]{:S(2)}, u32[]{:S(2)}) collective-permute-start(bf16[4,4,32,1024]{3,2,0,1:T(8,128)(2,1)S(1)} %bitcast.209), channel_id=1, source_target_pairs={{0,4},{4,0},{8,12},{12,8},{16,20},{20,16},{24,28},{28,24},{1,5},{5... | collective-permute-start | bytes 3145736 | tf_op jit(solution)/shard_map/ppermute | solution.py:474
  509.0 65.2 %collective-permute-start.35 = (bf16[4,4,32,2816]{3,2,1,0:T(8,128)(2,1)}, bf16[4,4,32,2816]{3,2,1,0:T(8,128)(2,1)}, u32[]{:S(2)}, u32[]{:S(2)}) collective-permute-start(bf16[4,4,32,2816]{3,2,1,0:T(8,128)(2,1)} %dynamic-slice_bitcast_fusion), channel_id=1, source_target_pairs={{0,4},{4,0},{8,12},{12,8},{16,20},{20,16},{24,28},{28,24},{1,5},{5... | collective-permute-start | bytes 8650760 | tf_op jit(solution)/shard_map/ppermute | solution.py:474
  522.7 12.6 %collective-permute-start.2 = (bf16[4,32,1024]{2,1,0:T(8,128)(2,1)S(1)}, bf16[4,32,1024]{2,1,0:T(8,128)(2,1)S(1)}, u32[]{:S(2)}, u32[]{:S(2)}) collective-permute-start(bf16[4,32,1024]{2,1,0:T(8,128)(2,1)S(1)} %get-tuple-element.113), channel_id=1, source_target_pairs={{0,16},{4,20},{8,24},{12,28},{16,0},{20,4},{24,8},{28,12},{1,17},{... | collective-permute-start | bytes 786440 | tf_op jit(solution)/shard_map/ppermute | solution.py:482
  524.1 12.5 %collective-permute-start.1 = (bf16[4,32,1024]{2,1,0:T(8,128)(2,1)S(1)}, bf16[4,32,1024]{2,1,0:T(8,128)(2,1)S(1)}, u32[]{:S(2)}, u32[]{:S(2)}) collective-permute-start(bf16[4,32,1024]{2,1,0:T(8,128)(2,1)S(1)} %get-tuple-element.111), channel_id=1, source_target_pairs={{0,8},{4,12},{8,0},{12,4},{16,24},{20,28},{24,16},{28,20},{1,9},{5... | collective-permute-start | bytes 786440 | tf_op jit(solution)/shard_map/ppermute | solution.py:482
  530.8 50.5 %collective-permute-start.28 = (bf16[4,4,32,2816]{3,2,1,0:T(8,128)(2,1)}, bf16[4,4,32,2816]{3,2,1,0:T(8,128)(2,1)}, u32[]{:S(2)}, u32[]{:S(2)}) collective-permute-start(bf16[4,4,32,2816]{3,2,1,0:T(8,128)(2,1)} %dynamic-slice_bitcast_fusion.1), channel_id=1, source_target_pairs={{0,4},{4,0},{8,12},{12,8},{16,20},{20,16},{24,28},{28,24},{1,5},{5... | collective-permute-start | bytes 8650760 | tf_op jit(solution)/shard_map/ppermute | solution.py:474
  535.4 20.2 %collective-permute-start.23 = (bf16[4,32,1024]{2,1,0:T(8,128)(2,1)S(1)}, bf16[4,32,1024]{2,1,0:T(8,128)(2,1)S(1)}, u32[]{:S(2)}, u32[]{:S(2)}) collective-permute-start(bf16[4,32,1024]{2,1,0:T(8,128)(2,1)S(1)} %get-tuple-element.108), channel_id=1, source_target_pairs={{0,2},{1,3},{2,0},{3,1},{4,6},{5,7},{6,4},{7,5},{8,10},{9,11},{10,... | collective-permute-start | bytes 786440 | tf_op jit(solution)/shard_map/ppermute | solution.py:485
  536.6 20.1 %collective-permute-start.22 = (bf16[4,32,1024]{2,1,0:T(8,128)(2,1)S(1)}, bf16[4,32,1024]{2,1,0:T(8,128)(2,1)S(1)}, u32[]{:S(2)}, u32[]{:S(2)}) collective-permute-start(bf16[4,32,1024]{2,1,0:T(8,128)(2,1)S(1)} %get-tuple-element.106), channel_id=1, source_target_pairs={{0,1},{1,2},{2,3},{3,0},{4,5},{5,6},{6,7},{7,4},{8,9},{9,10},{10,1... | collective-permute-start | bytes 786440 | tf_op jit(solution)/shard_map/ppermute | solution.py:485
  539.7 18.0 %collective-permute-start.20 = (bf16[16,1024]{1,0:T(8,128)(2,1)S(1)}, bf16[16,1024]{1,0:T(8,128)(2,1)S(1)}, u32[]{:S(2)}, u32[]{:S(2)}) collective-permute-start(bf16[16,1024]{1,0:T(8,128)(2,1)S(1)} %get-tuple-element.136), channel_id=1, source_target_pairs={{0,24},{4,28},{8,16},{12,20},{16,8},{20,12},{24,0},{28,4},{1,25},{... | collective-permute-start | bytes 98312 | tf_op jit(solution)/shard_map/ppermute | solution.py:482
  565.8 20.7 %collective-permute-start.42 = (bf16[4,4,88,1024]{3,2,0,1:T(8,128)(2,1)}, bf16[4,4,88,1024]{3,2,0,1:T(8,128)(2,1)}, u32[]{:S(2)}, u32[]{:S(2)}) collective-permute-start(bf16[4,4,88,1024]{3,2,0,1:T(8,128)(2,1)} %bitcast.194), channel_id=1, source_target_pairs={{0,4},{4,0},{8,12},{12,8},{16,20},{20,16},{24,28},{28,24},{1,5},{5... | collective-permute-start | bytes 8650760 | tf_op jit(solution)/shard_map/ppermute | solution.py:474
  577.8 20.0 %collective-permute-start.38 = (bf16[4,32,2816]{2,1,0:T(8,128)(2,1)S(1)}, bf16[4,32,2816]{2,1,0:T(8,128)(2,1)S(1)}, u32[]{:S(2)}, u32[]{:S(2)}) collective-permute-start(bf16[4,32,2816]{2,1,0:T(8,128)(2,1)S(1)} %get-tuple-element.102), channel_id=1, source_target_pairs={{0,24},{4,28},{8,16},{12,20},{16,8},{20,12},{24,0},{28,4},{1,25},{... | collective-permute-start | bytes 2162696 | tf_op jit(solution)/shard_map/ppermute | solution.py:482
  579.4 44.9 %collective-permute-start.37 = (bf16[4,32,2816]{2,1,0:T(8,128)(2,1)S(1)}, bf16[4,32,2816]{2,1,0:T(8,128)(2,1)S(1)}, u32[]{:S(2)}, u32[]{:S(2)}) collective-permute-start(bf16[4,32,2816]{2,1,0:T(8,128)(2,1)S(1)} %get-tuple-element.103), channel_id=1, source_target_pairs={{0,16},{4,20},{8,24},{12,28},{16,0},{20,4},{24,8},{28,12},{1,17},{... | collective-permute-start | bytes 2162696 | tf_op jit(solution)/shard_map/ppermute | solution.py:482
  580.5 43.8 %collective-permute-start.36 = (bf16[4,32,2816]{2,1,0:T(8,128)(2,1)S(1)}, bf16[4,32,2816]{2,1,0:T(8,128)(2,1)S(1)}, u32[]{:S(2)}, u32[]{:S(2)}) collective-permute-start(bf16[4,32,2816]{2,1,0:T(8,128)(2,1)S(1)} %get-tuple-element.101), channel_id=1, source_target_pairs={{0,8},{4,12},{8,0},{12,4},{16,24},{20,28},{24,16},{28,20},{1,9},{5... | collective-permute-start | bytes 2162696 | tf_op jit(solution)/shard_map/ppermute | solution.py:482
  585.0 43.8 %collective-permute-start.31 = (bf16[4,32,2816]{2,1,0:T(8,128)(2,1)S(1)}, bf16[4,32,2816]{2,1,0:T(8,128)(2,1)S(1)}, u32[]{:S(2)}, u32[]{:S(2)}) collective-permute-start(bf16[4,32,2816]{2,1,0:T(8,128)(2,1)S(1)} %get-tuple-element.99), channel_id=1, source_target_pairs={{0,24},{4,28},{8,16},{12,20},{16,8},{20,12},{24,0},{28,4},{1,25},{... | collective-permute-start | bytes 2162696 | tf_op jit(solution)/shard_map/ppermute | solution.py:482
  586.6 55.0 %collective-permute-start.30 = (bf16[4,32,2816]{2,1,0:T(8,128)(2,1)S(1)}, bf16[4,32,2816]{2,1,0:T(8,128)(2,1)S(1)}, u32[]{:S(2)}, u32[]{:S(2)}) collective-permute-start(bf16[4,32,2816]{2,1,0:T(8,128)(2,1)S(1)} %get-tuple-element.100), channel_id=1, source_target_pairs={{0,16},{4,20},{8,24},{12,28},{16,0},{20,4},{24,8},{28,12},{1,17},{... | collective-permute-start | bytes 2162696 | tf_op jit(solution)/shard_map/ppermute | solution.py:482
  597.8 45.3 %collective-permute-start.29 = (bf16[4,32,2816]{2,1,0:T(8,128)(2,1)S(1)}, bf16[4,32,2816]{2,1,0:T(8,128)(2,1)S(1)}, u32[]{:S(2)}, u32[]{:S(2)}) collective-permute-start(bf16[4,32,2816]{2,1,0:T(8,128)(2,1)S(1)} %get-tuple-element.98), channel_id=1, source_target_pairs={{0,8},{4,12},{8,0},{12,4},{16,24},{20,28},{24,16},{28,20},{1,9},{5... | collective-permute-start | bytes 2162696 | tf_op jit(solution)/shard_map/ppermute | solution.py:482
  624.3 19.3 %collective-permute-start.45 = (bf16[4,88,1024]{2,1,0:T(8,128)(2,1)S(1)}, bf16[4,88,1024]{2,1,0:T(8,128)(2,1)S(1)}, u32[]{:S(2)}, u32[]{:S(2)}) collective-permute-start(bf16[4,88,1024]{2,1,0:T(8,128)(2,1)S(1)} %get-tuple-element.96), channel_id=1, source_target_pairs={{0,3},{1,0},{2,1},{3,2},{4,7},{5,4},{6,5},{7,6},{8,11},{9,8},{10,9... | collective-permute-start | bytes 2162696 | tf_op jit(solution)/shard_map/ppermute | solution.py:485
  624.3 62.2 %collective-permute-start.44 = (bf16[4,88,1024]{2,1,0:T(8,128)(2,1)S(1)}, bf16[4,88,1024]{2,1,0:T(8,128)(2,1)S(1)}, u32[]{:S(2)}, u32[]{:S(2)}) collective-permute-start(bf16[4,88,1024]{2,1,0:T(8,128)(2,1)S(1)} %get-tuple-element.97), channel_id=1, source_target_pairs={{0,2},{1,3},{2,0},{3,1},{4,6},{5,7},{6,4},{7,5},{8,10},{9,11},{10,... | collective-permute-start | bytes 2162696 | tf_op jit(solution)/shard_map/ppermute | solution.py:485
  628.8 57.7 %collective-permute-start.43 = (bf16[4,88,1024]{2,1,0:T(8,128)(2,1)S(1)}, bf16[4,88,1024]{2,1,0:T(8,128)(2,1)S(1)}, u32[]{:S(2)}, u32[]{:S(2)}) collective-permute-start(bf16[4,88,1024]{2,1,0:T(8,128)(2,1)S(1)} %get-tuple-element.95), channel_id=1, source_target_pairs={{0,1},{1,2},{2,3},{3,0},{4,5},{5,6},{6,7},{7,4},{8,9},{9,10},{10,1... | collective-permute-start | bytes 2162696 | tf_op jit(solution)/shard_map/ppermute | solution.py:485
  641.6 50.1 %collective-permute-start.41 = (bf16[32,2816]{1,0:T(8,128)(2,1)S(1)}, bf16[32,2816]{1,0:T(8,128)(2,1)S(1)}, u32[]{:S(2)}, u32[]{:S(2)}) collective-permute-start(bf16[32,2816]{1,0:T(8,128)(2,1)S(1)} %get-tuple-element.121), channel_id=1, source_target_pairs={{0,3},{1,0},{2,1},{3,2},{4,7},{5,4},{6,5},{7,6},{8,11},{9,8},{10,9... | collective-permute-start | bytes 540680 | tf_op jit(solution)/shard_map/ppermute | solution.py:485
  643.1 58.8 %collective-permute-start.40 = (bf16[32,2816]{1,0:T(8,128)(2,1)S(1)}, bf16[32,2816]{1,0:T(8,128)(2,1)S(1)}, u32[]{:S(2)}, u32[]{:S(2)}) collective-permute-start(bf16[32,2816]{1,0:T(8,128)(2,1)S(1)} %get-tuple-element.122), channel_id=1, source_target_pairs={{0,2},{1,3},{2,0},{3,1},{4,6},{5,7},{6,4},{7,5},{8,10},{9,11},{10,... | collective-permute-start | bytes 540680 | tf_op jit(solution)/shard_map/ppermute | solution.py:485
  643.6 60.4 %collective-permute-start.39 = (bf16[32,2816]{1,0:T(8,128)(2,1)S(1)}, bf16[32,2816]{1,0:T(8,128)(2,1)S(1)}, u32[]{:S(2)}, u32[]{:S(2)}) collective-permute-start(bf16[32,2816]{1,0:T(8,128)(2,1)S(1)} %get-tuple-element.120), channel_id=1, source_target_pairs={{0,1},{1,2},{2,3},{3,0},{4,5},{5,6},{6,7},{7,4},{8,9},{9,10},{10,1... | collective-permute-start | bytes 540680 | tf_op jit(solution)/shard_map/ppermute | solution.py:485
  686.5 18.2 %collective-permute-start.34 = (bf16[32,2816]{1,0:T(8,128)(2,1)S(1)}, bf16[32,2816]{1,0:T(8,128)(2,1)S(1)}, u32[]{:S(2)}, u32[]{:S(2)}) collective-permute-start(bf16[32,2816]{1,0:T(8,128)(2,1)S(1)} %get-tuple-element.118), channel_id=1, source_target_pairs={{0,3},{1,0},{2,1},{3,2},{4,7},{5,4},{6,5},{7,6},{8,11},{9,8},{10,9... | collective-permute-start | bytes 540680 | tf_op jit(solution)/shard_map/ppermute | solution.py:485
  686.5 21.9 %collective-permute-start.33 = (bf16[32,2816]{1,0:T(8,128)(2,1)S(1)}, bf16[32,2816]{1,0:T(8,128)(2,1)S(1)}, u32[]{:S(2)}, u32[]{:S(2)}) collective-permute-start(bf16[32,2816]{1,0:T(8,128)(2,1)S(1)} %get-tuple-element.119), channel_id=1, source_target_pairs={{0,2},{1,3},{2,0},{3,1},{4,6},{5,7},{6,4},{7,5},{8,10},{9,11},{10,... | collective-permute-start | bytes 540680 | tf_op jit(solution)/shard_map/ppermute | solution.py:485
  691.7 16.8 %collective-permute-start.32 = (bf16[32,2816]{1,0:T(8,128)(2,1)S(1)}, bf16[32,2816]{1,0:T(8,128)(2,1)S(1)}, u32[]{:S(2)}, u32[]{:S(2)}) collective-permute-start(bf16[32,2816]{1,0:T(8,128)(2,1)S(1)} %get-tuple-element.117), channel_id=1, source_target_pairs={{0,1},{1,2},{2,3},{3,0},{4,5},{5,6},{6,7},{7,4},{8,9},{9,10},{10,1... | collective-permute-start | bytes 540680 | tf_op jit(solution)/shard_map/ppermute | solution.py:485
  (65 other events, 455.3 us)
Sparse Core Ops, SparseCore 0:
  11.6 56.4 all-gather.8
  71.5 58.0 all-gather.6
  133.1 55.3 all-gather.10
  191.7 66.1 all-gather.14
  261.2 90.2 all-gather.12

commit v2 on v1

--- a/solution.py
+++ b/solution.py
@@ -1,3 +1,5 @@
+import functools
+
 import jax
 import jax.numpy as jnp
 from jax import lax
@@ -39,6 +41,8 @@
 NT = (((1,), (1,)), ((), ()))
 TN = (((0,), (0,)), ((), ()))
 MIB = 1 << 20
+CHUNK = 256
+TILE = 2 * CHUNK
 
 
 def dot(left, right, dims):
@@ -221,71 +225,101 @@
     dq_ref[...] = unrotate(total_ref[...].T * SCALE, *tables(slice(None))).astype(BF)
 
 
-def attention_back(q, k, v, o, do, logs, tables):
-    length, width = q.shape
-    spec = pl.BlockSpec((length, LANES), lambda i: (0, i))
+def attention_back(start, count, q, k, v, o, do, logs, tables):
+    length = q.shape[0]
+    spec = pl.BlockSpec((length, LANES), lambda i: (0, i + start))
+    out = pl.BlockSpec((length, LANES), lambda i: (0, i))
+    log = pl.BlockSpec((1, 2, length), lambda i: (i + start, 0, 0))
     return pl.pallas_call(
         attention_back_kernel,
-        grid=(PAIRS,),
-        in_specs=[spec] * 5 + [pl.BlockSpec((1, 2, length), lambda i: (i, 0, 0))] + [resident(length, LANES)] * 3,
-        out_specs=[spec] * 3,
-        out_shape=[jax.ShapeDtypeStruct((length, width), BF)] * 3,
+        grid=(count,),
+        in_specs=[spec] * 5 + [log] + [resident(length, LANES)] * 3,
+        out_specs=[out] * 3,
+        out_shape=[jax.ShapeDtypeStruct((length, count * LANES), BF)] * 3,
         scratch_shapes=[pltpu.VMEM((LANES, length), F32)],
         compiler_params=pltpu.CompilerParams(vmem_limit_bytes=48 * MIB),
         cost_estimate=pl.CostEstimate(
-            flops=PAIRS * 20 * LANES * length * length,
-            bytes_accessed=16 * length * width,
-            transcendentals=PAIRS * length * length,
+            flops=count * 20 * LANES * length * length,
+            bytes_accessed=16 * length * count * LANES,
+            transcendentals=count * length * length,
         ),
         name="attention_back",
     )(q, k, v, o, do, logs, *tables)
 
 
-def feed_forward_kernel(x_ref, o_ref, og_ref, factor_ref, gain_ref, wout_ref, wg_ref, wu_ref, wd_ref,
-                        mixed_ref, dh_ref, do_ref, gout_ref, gg_ref, gu_ref, gd_ref, dgain_ref,
-                        h_ref, acc_ref, da2_ref, a2_ref, a2t_ref, dyb_ref, hid_ref, dgu_ref):
+def place_rows(target_ref, columns, values, order_ref):
+    blocks = order_ref.shape[0]
+    size = values.shape[1] // blocks
+    for block in range(blocks):
+        start = pl.multiple_of(order_ref[block] * size, size)
+        target_ref[pl.ds(start, size), columns] = values[:, block * size : (block + 1) * size].T
+
+
+def feed_forward_kernel(first, last, order_ref, *refs):
+    x_ref, o_ref, og_ref, factor_ref, gain_ref, out_low_ref, out_high_ref, wgu_ref, wd_ref = refs[:9]
+    refs = refs[9:]
+    if first:
+        (h_ref, acc_ref, da2_ref, own_ref, send_ref, gd_ref, a2_ref, a2t_ref, dyb_ref, hid_ref, dgu_ref) = refs
+    else:
+        h_ref, acc_in_ref, da2_in_ref = refs[:3]
+        (mixed_ref, dh_ref, do_ref, own_ref, send_ref, gd_ref, dgain_ref) = refs[4:11]
+        (acc_ref, da2_ref, a2_ref, a2t_ref, dyb_ref, hid_ref, dgu_ref) = refs[11:]
     step = pl.program_id(0)
-    last = pl.num_programs(0) - 1
     length, width = x_ref.shape
-    chunk = wg_ref.shape[1]
+    chunk = wd_ref.shape[0]
+    side = width // 2
     tile = min(256, length)
     gain = gain_ref[...].astype(F32)
+    matrix = lambda ref: ref[...].reshape(-1, ref.shape[-1])
 
     @pl.when(step == 0)
     def _():
         for m in range(0, length, tile):
             rows = pl.ds(m, tile)
-            h = x_ref[rows, :].astype(F32) + dot(o_ref[rows, :], wout_ref[...], NN)
-            h_ref[rows, :] = h
-            acc_ref[rows, :] = h
+            if first:
+                o = o_ref[rows, :]
+                added = [dot(o, matrix(ref), NN) for ref in (out_low_ref, out_high_ref)]
+                h = x_ref[rows, :].astype(F32) + jnp.concatenate(added, axis=1)
+                h_ref[rows, :] = h
+                acc_ref[rows, :] = h
+                da2_ref[rows, :] = jnp.zeros((tile, width), F32)
+            else:
+                h = h_ref[rows, :]
+                acc_ref[rows, :] = acc_in_ref[rows, :]
+                da2_ref[rows, :] = da2_in_ref[rows, :]
             inverse = lax.rsqrt(jnp.mean(h * h, axis=1, keepdims=True) + EPSILON_NORM)
             a2 = (h * inverse * gain).astype(BF)
             a2_ref[rows, :] = a2
-            a2t_ref[:, rows] = a2.T
+            place_rows(a2t_ref, rows, a2, order_ref)
             dyb_ref[rows, :] = (og_ref[rows, :].astype(F32) * factor_ref[rows, :]).astype(BF)
-            da2_ref[rows, :] = jnp.zeros((tile, width), F32)
-
-    for m in range(0, length, tile):
-        rows = pl.ds(m, tile)
-        gate = dot(a2_ref[rows, :], wg_ref[...], NN)
-        up = dot(a2_ref[rows, :], wu_ref[...], NN)
-        dhid = dot(dyb_ref[rows, :], wd_ref[...], NT)
-        sig = 1.0 / (1.0 + jnp.exp2(gate * -LOG2E))
-        act = gate * sig
-        hid_ref[rows, :] = (act * up).astype(BF)
-        dgu_ref[rows, :chunk] = (dhid * up * (sig + act * (1.0 - sig))).astype(BF)
-        dgu_ref[rows, chunk:] = (dhid * act).astype(BF)
-    for m in range(0, length, tile):
-        rows = pl.ds(m, tile)
-        acc_ref[rows, :] += dot(hid_ref[rows, :], wd_ref[...], NN)
-        da2_ref[rows, :] += dot(dgu_ref[rows, :chunk], wg_ref[...], NT) + dot(
-            dgu_ref[rows, chunk:], wu_ref[...], NT
-        )
-    gd_ref[...] = dot(hid_ref[...], dyb_ref[...], TN).astype(BF)
-    gg_ref[...] = dot(a2t_ref[...], dgu_ref[:, :chunk], NN).astype(BF)
-    gu_ref[...] = dot(a2t_ref[...], dgu_ref[:, chunk:], NN).astype(BF)
-
-    @pl.when(step == last)
+
+    def one_chunk():
+        weights = matrix(wgu_ref)
+        for m in range(0, length, tile):
+            rows = pl.ds(m, tile)
+            gate = dot(a2_ref[rows, :], weights[:, :chunk], NN)
+            up = dot(a2_ref[rows, :], weights[:, chunk:], NN)
+            dhid = dot(dyb_ref[rows, :], wd_ref[...], NT)
+            sig = 1.0 / (1.0 + jnp.exp2(gate * -LOG2E))
+            act = gate * sig
+            hid_ref[rows, :] = (act * up).astype(BF)
+            dgu_ref[rows, :chunk] = (dhid * up * (sig + act * (1.0 - sig))).astype(BF)
+            dgu_ref[rows, chunk:] = (dhid * act).astype(BF)
+        for m in range(0, length, tile):
+            rows = pl.ds(m, tile)
+            acc_ref[rows, :] += dot(hid_ref[rows, :], wd_ref[...], NN)
+            da2_ref[rows, :] += dot(dgu_ref[rows, :], weights, NT)
+        gd_ref[...] = dot(hid_ref[...], dyb_ref[...], TN).astype(BF)
+        own_ref[...] = dot(a2t_ref[:side, :], dgu_ref[...], NN).astype(BF)
+        send_ref[...] = dot(a2t_ref[side:, :], dgu_ref[...], NN).astype(BF)
+
+    if first:
+        one_chunk()
+        return
+    tail = pl.num_programs(0) - 2
+    pl.when(step < tail)(one_chunk)
+
+    @pl.when(step == tail)
     def _():
         total = jnp.zeros((1, width), F32)
         for m in range(0, length, tile):
@@ -302,115 +336,108 @@
             dh_ref[rows, :] = dh
             low = dh.astype(BF)
             dyb_ref[rows, :] = low
-            do_ref[rows, :] = dot(low, wout_ref[...], NT).astype(BF)
+            half = width // 2
+            do_ref[rows, :] = (
+                dot(low[:, :half], matrix(out_low_ref), NT) + dot(low[:, half:], matrix(out_high_ref), NT)
+            ).astype(BF)
+            place_rows(a2t_ref, rows, o_ref[rows, :], order_ref)
         dgain_ref[...] = total
-        gout_ref[...] = dot(o_ref[...], dyb_ref[...], TN).astype(BF)
-
-
-def feed_forward(x, o, out_grad, factor, gain, w_out, w_gate, w_down):
+
+    for tile_number in range(2):
+
+        @pl.when(step == tail + tile_number)
+        def _():
+            half = width // 2
+            grads = dyb_ref[:, tile_number * half : (tile_number + 1) * half]
+            own_ref[...] = dot(a2t_ref[:side, :], grads, NN).astype(BF)
+            send_ref[...] = dot(a2t_ref[side:, :], grads, NN).astype(BF)
+
+
+def feed_forward(order, start, count, state, x, o, out_grad, factor, gain, weights, w_down):
     length, width = x.shape
-    chunk = 256
-    steps = FF // chunk
-    grid = lambda block, index: pl.BlockSpec(block, index)
-    columns = lambda shift: pl.BlockSpec((width, chunk), lambda i: (0, i + shift))
-    rows = pl.BlockSpec((chunk, width), lambda i: (i, 0))
+    chunk = CHUNK
+    first = state is None
+    chunks = FF // chunk
+    steps = count if first else count + 2
+    parts, per, tile = weights.shape[0], width // weights.shape[0], weights.shape[2]
+    within = lambda i: start + jnp.minimum(i, count - 1)
+    weight = lambda index: pl.BlockSpec((parts, per, tile), lambda i, order: (0, index(i), 0))
+    kept = lambda index: pl.BlockSpec(
+        (parts, per, tile), lambda i, order: (0, index, 0), pipeline_mode=pl.Buffered(1)
+    )
+    rows = pl.BlockSpec((chunk, width), lambda i, order: (within(i), 0))
+    columns = pl.BlockSpec((width // 2, tile), lambda i, order: (0, i))
     shape = jax.ShapeDtypeStruct
+    scratch = [
+        pltpu.VMEM((length, width), BF),
+        pltpu.VMEM((width, length), BF),
+        pltpu.VMEM((length, width), BF),
+        pltpu.VMEM((length, chunk), BF),
+        pltpu.VMEM((length, 2 * chunk), BF),
+    ]
+    big = resident(length, width)
+    in_specs = [big, big, big, resident(length, 1), resident(1, width), kept(chunks), kept(chunks + 1), weight(within), rows]
+    operands = [x, o, out_grad, factor, gain, weights, weights, weights, w_down]
+    halves_out = [shape((width // 2, steps * tile), BF)] * 2
+    aliases = {}
+    if first:
+        out_specs = [big, big, big, columns, columns, rows]
+        out_shape = [shape((length, width), F32)] * 3 + halves_out + [shape((FF, width), BF)]
+    else:
+        in_specs += [big] * 3 + [pl.BlockSpec(memory_space=pl.ANY)]
+        operands += list(state)
+        out_specs = [big, big, big, columns, columns, rows, resident(1, width)]
+        out_shape = [shape((length, width), BF), shape((length, width), F32), shape((length, width), BF)]
+        out_shape += halves_out + [shape((FF, width), BF), shape((1, width), F32)]
+        scratch = [pltpu.VMEM((length, width), F32)] * 2 + scratch
+        aliases = {len(operands): 5}
     return pl.pallas_call(
-        feed_forward_kernel,
-        grid=(steps,),
-        in_specs=[
-            resident(length, width),
-            resident(length, QUERY_WIDTH),
-            resident(length, width),
-            resident(length, 1),
-            resident(1, width),
-            resident(QUERY_WIDTH, width),
-            columns(0),
-            columns(steps),
-            rows,
-        ],
-        out_specs=[
-            resident(length, width),
-            resident(length, width),
-            resident(length, QUERY_WIDTH),
-            resident(QUERY_WIDTH, width),
-            columns(0),
-            columns(0),
-            rows,
-            resident(1, width),
-        ],
-        out_shape=[
-            shape((length, width), BF),
-            shape((length, width), F32),
-            shape((length, QUERY_WIDTH), BF),
-            shape((QUERY_WIDTH, width), BF),
-            shape((width, FF), BF),
-            shape((width, FF), BF),
-            shape((FF, width), BF),
-            shape((1, width), F32),
-        ],
-        scratch_shapes=[
-            pltpu.VMEM((length, width), F32),
-            pltpu.VMEM((length, width), F32),
-            pltpu.VMEM((length, width), F32),
-            pltpu.VMEM((length, width), BF),
-            pltpu.VMEM((width, length), BF),
-            pltpu.VMEM((length, width), BF),
-            pltpu.VMEM((length, chunk), BF),
-            pltpu.VMEM((length, 2 * chunk), BF),
-        ],
-        compiler_params=pltpu.CompilerParams(vmem_limit_bytes=58 * MIB),
+        functools.partial(feed_forward_kernel, first, not first),
+        grid_spec=pltpu.PrefetchScalarGridSpec(
+            num_scalar_prefetch=1, grid=(steps,), in_specs=in_specs, out_specs=out_specs, scratch_shapes=scratch
+        ),
+        out_shape=out_shape,
+        input_output_aliases=aliases,
+        compiler_params=pltpu.CompilerParams(vmem_limit_bytes=60 * MIB),
         cost_estimate=pl.CostEstimate(
-            flops=2 * length * width * (9 * FF + 3 * QUERY_WIDTH),
-            bytes_accessed=60 * MIB,
-            transcendentals=length * FF,
+            flops=2 * length * width * (9 * chunk * count + 2 * QUERY_WIDTH),
+            bytes_accessed=40 * MIB,
+            transcendentals=length * chunk * count,
         ),
         name="feed_forward",
-    )(x, o, out_grad, factor, gain, w_out, w_gate, w_gate, w_down)
-
-
-def unproject_kernel(a1_ref, c_ref, dq_ref, dk_ref, dv_ref, wup_ref, dc_ref, ginq_ref, ginc_ref, gup_ref, a1t_ref):
-    head = pl.program_id(0)
-
-    @pl.when(head == 0)
-    def _():
-        a1t_ref[...] = a1_ref[...].T
-
-    dc = (
-        dot(dk_ref[...], wup_ref[:, :GROUP_WIDTH], NT) + dot(dv_ref[...], wup_ref[:, GROUP_WIDTH:], NT)
-    ).astype(BF)
-    dc_ref[...] = dc
-    latent = c_ref[...].T
-    gup_ref[:, :GROUP_WIDTH] = dot(latent, dk_ref[...], NN).astype(BF)
-    gup_ref[:, GROUP_WIDTH:] = dot(latent, dv_ref[...], NN).astype(BF)
-    ginc_ref[...] = dot(a1t_ref[...], dc, NN).astype(BF)
-    ginq_ref[...] = dot(a1t_ref[...], dq_ref[...], NN).astype(BF)
-
-
-def unproject(a1, c, dq, dk, dv, w_up):
+    )(order, *operands)
+
+
+def unproject_kernel(a1_ref, c_ref, dq0_ref, dk0_ref, dv0_ref, dq1_ref, dk1_ref, dv1_ref, wup_ref, dql_ref, gin_ref, gup_ref):
+    a1t = a1_ref[...].T
+    for head, (dq_ref, dk_ref, dv_ref) in enumerate(((dq0_ref, dk0_ref, dv0_ref), (dq1_ref, dk1_ref, dv1_ref))):
+        latent = slice(head * LATENT_WIDTH, (head + 1) * LATENT_WIDTH)
+        dc = (
+            dot(dk_ref[...], wup_ref[latent, :GROUP_WIDTH], NT) + dot(dv_ref[...], wup_ref[latent, GROUP_WIDTH:], NT)
+        ).astype(BF)
+        mine = slice(QUERY_WIDTH + head * LATENT_WIDTH, QUERY_WIDTH + (head + 1) * LATENT_WIDTH)
+        group = slice(head * GROUP_WIDTH, (head + 1) * GROUP_WIDTH)
+        dql_ref[:, mine] = dc
+        dql_ref[:, group] = dq_ref[...]
+        gin_ref[:, mine] = dot(a1t, dc, NN).astype(BF)
+        gin_ref[:, group] = dot(a1t, dq_ref[...], NN).astype(BF)
+        turned = c_ref[:, latent].T
+        gup_ref[latent, :GROUP_WIDTH] = dot(turned, dk_ref[...], NN).astype(BF)
+        gup_ref[latent, GROUP_WIDTH:] = dot(turned, dv_ref[...], NN).astype(BF)
+
+
+def unproject(a1, c, one, two, w_up):
     length, width = a1.shape
-    group = pl.BlockSpec((length, GROUP_WIDTH), lambda g: (0, g))
-    latent = pl.BlockSpec((length, LATENT_WIDTH), lambda g: (0, g))
-    up = pl.BlockSpec((LATENT_WIDTH, 2 * GROUP_WIDTH), lambda g: (g, 0))
     shape = jax.ShapeDtypeStruct
     latents = LATENT_HEADS * LATENT_WIDTH
+    operands = (a1, c, *one, *two, w_up)
+    outs = ((length, QUERY_WIDTH + latents), (width, QUERY_WIDTH + latents), (latents, 2 * GROUP_WIDTH))
     return pl.pallas_call(
         unproject_kernel,
-        grid=(LATENT_HEADS,),
-        in_specs=[resident(length, width), latent, group, group, group, up],
-        out_specs=[
-            latent,
-            pl.BlockSpec((width, GROUP_WIDTH), lambda g: (0, g)),
-            pl.BlockSpec((width, LATENT_WIDTH), lambda g: (0, g)),
-            up,
-        ],
-        out_shape=[
-            shape((length, latents), BF),
-            shape((width, QUERY_WIDTH), BF),
-            shape((width, latents), BF),
-            shape((latents, 2 * GROUP_WIDTH), BF),
-        ],
-        scratch_shapes=[pltpu.VMEM((width, length), BF)],
+        grid=(1,),
+        in_specs=[resident(*a.shape) for a in operands],
+        out_specs=[resident(*s) for s in outs],
+        out_shape=[shape(s, BF) for s in outs],
         compiler_params=pltpu.CompilerParams(vmem_limit_bytes=56 * MIB),
         cost_estimate=pl.CostEstimate(
             flops=2 * length * (width * (QUERY_WIDTH + latents) + 4 * latents * GROUP_WIDTH),
@@ -418,14 +445,14 @@
             transcendentals=0,
         ),
         name="unproject",
-    )(a1, c, dq, dk, dv, w_up)
-
-
-def input_grad_kernel(x_ref, dh_ref, dq_ref, dc_ref, gain_ref, win_ref, out_ref, dgain_ref):
+    )(*operands)
+
+
+def input_grad_kernel(x_ref, dh_ref, dql_ref, gain_ref, win_ref, out_ref, dgain_ref):
     x = x_ref[...].astype(F32)
     inverse = lax.rsqrt(jnp.mean(x * x, axis=1, keepdims=True) + EPSILON_NORM)
     hat = x * inverse
-    da1 = dot(dq_ref[...], win_ref[:, :QUERY_WIDTH], NT) + dot(dc_ref[...], win_ref[:, QUERY_WIDTH:], NT)
+    da1 = dot(dql_ref[...], win_ref[...], NT)
     part = jnp.sum(da1 * hat, axis=0, keepdims=True)
     scaled = da1 * gain_ref[...].astype(F32)
     out_ref[...] = (
@@ -441,20 +468,20 @@
         dgain_ref[...] += part
 
 
-def input_grad(x, dh, dq, dc, gain, w_in):
+def input_grad(x, dh, dql, gain, w_in):
     length, width = x.shape
     tile = min(256, length)
     rows = lambda columns: pl.BlockSpec((tile, columns), lambda i: (i, 0))
     return pl.pallas_call(
         input_grad_kernel,
         grid=(length // tile,),
-        in_specs=[rows(width), rows(width), rows(QUERY_WIDTH), rows(dc.shape[1]), resident(1, width), resident(*w_in.shape)],
+        in_specs=[rows(width), rows(width), rows(dql.shape[1]), resident(1, width), resident(*w_in.shape)],
         out_specs=[rows(width), resident(1, width)],
         out_shape=[jax.ShapeDtypeStruct((length, width), BF), jax.ShapeDtypeStruct((1, width), F32)],
         compiler_params=pltpu.CompilerParams(vmem_limit_bytes=48 * MIB),
         cost_estimate=pl.CostEstimate(flops=2 * length * w_in.size, bytes_accessed=16 * MIB, transcendentals=0),
         name="input_grad",
-    )(x, dh, dq, dc, gain, w_in)
+    )(x, dh, dql, gain, w_in)
 
 
 class Ring:
@@ -489,36 +516,68 @@
     return lax.dynamic_index_in_dim(array, index, axis, keepdims=False)
 
 
-def sum_core(ring, grad):
-    columns = grad.shape[1]
+def split_core(ring, grad):
     rows = grad.shape[0] // (ring.plane * ring.cores * ring.line)
-    grad = grad.reshape(ring.plane, ring.cores, ring.line, rows, columns)
+    grad = grad.reshape(ring.plane, ring.cores, ring.line, rows, grad.shape[1])
     if ring.cores == 1:
-        return grad[:, 0]
-    received = ring.send_core(take(grad, 1 - ring.core, 1))
-    return (take(grad, ring.core, 1).astype(F32) + received.astype(F32)).astype(BF)
-
-
-def sum_plane(ring, grad):
-    total = take(grad, ring.at, 0).astype(F32)
-    for shift in range(1, ring.plane):
-        total += ring.send_plane(take(grad, ring.partner(ring.at, shift, ring.plane), 0), shift).astype(F32)
-    return total
+        return grad[:, 0], None
+    return take(grad, ring.core, 1), take(grad, 1 - ring.core, 1)
+
+
+def sum_core(ring, own, other):
+    if ring.cores == 1:
+        return own.astype(F32)
+    return own.astype(F32) + ring.send_core(other).astype(F32)
+
+
+def sum_plane(ring, grad, relative):
+    block = lambda shift: grad[shift] if relative else take(grad, ring.partner(ring.at, shift, ring.plane), 0)
+    received = [ring.send_plane(block(shift).astype(BF), shift) for shift in range(1, ring.plane)]
+    return sum((r.astype(F32) for r in received), block(0).astype(F32))
 
 
 def sum_line(ring, grad, axis):
-    total = take(grad, ring.z, axis).astype(F32)
-    for shift in range(1, ring.line):
-        total += ring.send_line(take(grad, (ring.z + shift) % ring.line, axis), shift).astype(F32)
-    return total
-
-
-def plane_first(ring, grad):
-    return sum_line(ring, sum_plane(ring, sum_core(ring, grad)).astype(BF), 0)
-
-
-def line_first(ring, grad):
-    return sum_plane(ring, sum_line(ring, sum_core(ring, grad), 1).astype(BF))
+    received = [
+        ring.send_line(take(grad, (ring.z + shift) % ring.line, axis).astype(BF), shift)
+        for shift in range(1, ring.line)
+    ]
+    return sum((r.astype(F32) for r in received), take(grad, ring.z, axis).astype(F32))
+
+
+def halves_order(ring):
+    blocks = jnp.arange(ring.plane * ring.cores)
+    plane, core = blocks // ring.cores, blocks % ring.cores
+    if ring.plane & (ring.plane - 1) == 0:
+        shift = plane ^ ring.at
+    else:
+        shift = (plane - ring.at) % ring.plane
+    return (((core - ring.core) % ring.cores) * ring.plane + shift).astype(jnp.int32)
+
+
+def gather_first(ring, piece):
+    pieces = [piece] + [ring.send_line(piece, shift) for shift in range(1, ring.line)]
+    around = jnp.stack(pieces[:0:-1] + [piece] + pieces[:0:-1])
+    line = lax.dynamic_slice_in_dim(around, ring.line - 1 - ring.z, ring.line, 0)
+    blocks = [line] + [ring.send_plane(line, shift) for shift in range(1, ring.plane)]
+    if ring.plane & (ring.plane - 1) == 0:
+        shifts = [ring.at ^ at for at in range(ring.plane)]
+    else:
+        shifts = [(ring.at - at) % ring.plane for at in range(ring.plane)]
+    plane = jnp.stack([choose(shift, blocks) for shift in shifts])
+    if ring.cores == 1:
+        return plane
+    other = ring.send_core(plane)
+    low = jnp.where(ring.core == 0, plane, other)
+    high = jnp.where(ring.core == 0, other, plane)
+    both = jnp.stack([low, high], axis=1)
+    return both.reshape(ring.plane * 2, *both.shape[2:])
+
+
+def choose(index, options):
+    result = options[0]
+    for number, option in enumerate(options[1:], 1):
+        result = jnp.where(index == number, option, result)
+    return result
 
 
 def sum_all(ring, value):
@@ -550,22 +609,33 @@
     return (master_new, first_new, second_new)
 
 
-def gather(piece, axis=0):
-    return lax.all_gather(piece, AXES, axis=axis, tiled=True)
+def after(values, *done):
+    return lax.optimization_barrier((values, done))[0]
 
 
 def shards(data, line, tokens, out_grad, domain_ids, domain_scale, *state):
     masters, moments = state[:6], state[6:]
     firsts, seconds = moments[0::2], moments[1::2]
     ring = Ring(data, line)
+    devices = data * line
     length, width = tokens.shape
-    lowered = tuple(w.astype(BF) for w in masters)
-    w_in = gather(lowered[0])
-    gains = gather(lowered[5], 1)
-    w_up = gather(lowered[1])
-    w_out = gather(lowered[2])
-    w_gate = gather(lowered[3])
-    w_down = gather(lowered[4])
+    p_in, p_up, p_out, p_gate, p_down, p_gains = (w.astype(BF) for w in masters)
+    latents = LATENT_HEADS * LATENT_WIDTH
+    rows = width // devices
+    chunks = FF // CHUNK
+    columns = lambda a: a.reshape(a.shape[0], -1, TILE).transpose(1, 0, 2).reshape(-1, TILE)
+
+    gate_tiles = p_gate.reshape(rows, 2, chunks, CHUNK).transpose(2, 0, 1, 3).reshape(-1, TILE)
+    bundle = jnp.concatenate([gate_tiles, columns(p_out), columns(p_down)], axis=0)
+    bundle = lax.all_gather(bundle, AXES, axis=0, tiled=True).reshape(devices, -1, TILE)
+
+    first = jnp.concatenate([p_in, columns(p_up).reshape(rows, -1), lane_pad(p_gains, rows)], axis=1)
+    first = gather_first(ring, first).reshape(devices, rows, -1)
+    w_in = first[:, :, : p_in.shape[1]].reshape(width, -1)
+    w_up = first[:, :, p_in.shape[1] : p_in.shape[1] + p_up.size // rows]
+    w_up = w_up.reshape(devices, 2 * GROUP_WIDTH // TILE, p_up.shape[0], TILE).transpose(0, 2, 1, 3).reshape(latents, -1)
+    gains = first[:, :2, -LANES:][:, :, : p_gains.shape[1]].transpose(1, 0, 2).reshape(2, width)
+
     tables = rotation_tables(length)
     factor = jnp.sum(
         jnp.where(domain_ids[:, None] == jnp.arange(NDOM)[None, :], domain_scale[None, :], 0.0),
@@ -574,27 +644,50 @@
     )
     a1, q, k, v, c = project(tokens, gains[:1], w_in, w_up, tables)
     o, logs = attention(q, k, v)
-    mixed, dh, do, g_out, g_gate, g_upper, g_down, dgain_two = feed_forward(
-        tokens, o, out_grad, factor, gains[1:], w_out, w_gate, w_down
-    )
-    sum_down = line_first(ring, g_down)
-    sum_gate = plane_first(ring, g_gate)
-    sum_upper = plane_first(ring, g_upper)
-    sum_out = line_first(ring, g_out)
-    dq, dk, dv = attention_back(q, k, v, o, do, logs, tables)
-    dc, g_query, g_latent_in, g_up = unproject(a1, c, dq, dk, dv, w_up)
-    sum_query = plane_first(ring, g_query)
-    sum_latent_in = plane_first(ring, g_latent_in)
-    sum_up = line_first(ring, g_up)
-    given, dgain_one = input_grad(tokens, dh, dq, dc, gains[:1], w_in)
+
+    split = rows * (chunks + width // TILE)
+    w_down = bundle[:, split:].reshape(devices, -1, p_down.shape[0], TILE).transpose(0, 2, 1, 3).reshape(FF, width)
+    if rows % 16:
+        bundle = bundle[:, :split].reshape(devices, -1, rows, TILE).transpose(1, 0, 2, 3).reshape(1, -1, TILE)
+    order = halves_order(ring)
+    half = chunks // 2 + 1
+    common = (tokens, o, out_grad, factor, gains[1:], bundle, w_down)
+    h, acc, da2, own_a, send_a, g_down = feed_forward(order, 0, half, None, *common)
+    blocks = lambda a: a.reshape(ring.plane, ring.line, rows, -1)
+    sum_a = sum_core(ring, blocks(own_a), blocks(send_a)).astype(BF)
+    mixed, dh, do, own_b, send_b, g_down, dgain_two = feed_forward(
+        order, half, chunks - half, (h, acc, da2, g_down), *common
+    )
+    do = after(do, sum_a)
+    part_a = sum_plane(ring, sum_a, True).astype(BF)
+    sum_b = sum_core(ring, blocks(own_b), blocks(send_b)).astype(BF)
+    sum_d = sum_core(ring, *split_core(ring, g_down)).astype(BF)
+    one = attention_back(0, PAIRS_PER_LATENT, q, k, v, o, do, logs, tables)
+    do = after(do, sum_b, sum_d, one)
+    part_d = sum_line(ring, sum_d, 1).astype(BF)
+    part_b = sum_plane(ring, sum_b, True).astype(BF)
+    two = attention_back(PAIRS_PER_LATENT, PAIRS_PER_LATENT, q, k, v, o, do, logs, tables)
+    two = after(two, part_a)
+    total_a = sum_line(ring, part_a, 0)
+    dql, g_in, g_up = unproject(a1, c, one, two, w_up)
+    g_up = g_up.reshape(devices, -1, 2 * GROUP_WIDTH // TILE, TILE).transpose(0, 2, 1, 3).reshape(width, -1)
+    sum_c = sum_core(ring, *split_core(ring, jnp.concatenate([g_in, g_up], axis=1))).astype(BF)
+    part_c = sum_plane(ring, sum_c, False).astype(BF)
+    given, dgain_one = input_grad(tokens, dh, after(dql, sum_c), gains[:1], w_in)
+    total_b = sum_line(ring, part_b, 0)
+    total_d = sum_plane(ring, part_d, False)
+    total_c = sum_line(ring, part_c, 0)
+
+    gated = jnp.concatenate([total_a, total_b[:, : (chunks - half) * TILE]], axis=1)
+    gated = gated.reshape(rows, chunks, 2, CHUNK).transpose(0, 2, 1, 3).reshape(rows, -1)
     owned = [
-        jnp.concatenate([sum_query, sum_latent_in], axis=1),
-        sum_up,
-        sum_out,
-        jnp.concatenate([sum_gate, sum_upper], axis=1),
-        sum_down,
+        total_c[:, : p_in.shape[1]],
+        total_c[:, p_in.shape[1] :].reshape(-1, *p_up.shape[:1], TILE).transpose(1, 0, 2).reshape(p_up.shape),
+        total_b[:, (chunks - half) * TILE :],
+        gated,
+        total_d,
     ]
-    squares = sum(jnp.sum(grad * grad) for grad in owned)
+    squares = sum(jnp.sum(grad * grad) for grad in (total_a, total_b, total_c, total_d))
     dgains = jnp.concatenate([dgain_one, dgain_two], axis=0)
     message = jnp.concatenate(
         [dgains.reshape(-1, LANES), jnp.full((8, LANES), squares, F32)], axis=0
@@ -620,6 +713,10 @@
     return (mixed, given, grad_norm, *results)
 
 
+def lane_pad(gains, rows):
+    return jnp.pad(gains, ((0, rows - gains.shape[0]), (0, LANES - gains.shape[1])))
+
+
 def solution(mesh):
     data, line = mesh.shape["dp"], mesh.shape["fsdp"]
     rows, flat, columns = P(AXES, None), P(AXES), P(None, AXES)

time: 757 us -> 474 us (0.63)
  waiting for transfers between devices: 358 us -> 122 us
  blocking collectives: 69.3 us -> 0 us
  local copies, waits for them, and re-layouts: 29.1 us -> 54.2 us
  starting transfers between devices: 71.4 us -> 48.3 us
  Pallas kernels: 163 us -> 181 us
    all_gather x5 -> x1, waiting for transfers between devices: 218 us -> 37.6 us  [shards(): lax.all_gather(bundle, AXES, axis=0, tiled=True).reshape(devices, -1, TILE)]
    all_gather x1 -> x0, blocking collectives: 69.3 us -> none  [gather(): return lax.all_gather(piece, AXES, axis=axis, tiled=True)]
    ppermute x21 -> x15, waiting for transfers between devices: 69.3 us -> 26.9 us  [send_line(): lax.ppermute(value, 'fsdp', [(i, (i + shift) % self.line) for i in range(...]
    ppermute x23 -> x17, waiting for transfers between devices: 63.8 us -> 44.5 us  [send_plane(): return lax.ppermute(value, 'dp', pairs)]
    pallas_call x3 -> x5, Pallas kernels: 120 us -> 138 us  [the longest x2 89.1 us: feed_forward(): pl.pallas_call(functools.partial(feed_forward_kernel, first, not first),...]
    reshape x0 -> x8, local copies, waits for them, and re-layouts: none -> 14.6 us  [the longest x1 9.07 us: shards(): bundle[:, split:].reshape(devices, -1, p_down.shape[0], TILE)]
    ppermute x21 -> x15, starting transfers between devices: 39.7 us -> 25.8 us  [send_line(): lax.ppermute(value, 'fsdp', [(i, (i + shift) % self.line) for i in range(...]
    ppermute x23 -> x17, starting transfers between devices: 27.6 us -> 20.8 us  [send_plane(): return lax.ppermute(value, 'dp', pairs)]
  transfers between devices with their start and end apart: 59 -> 41, of which waited for: 34 -> 15; matrix products, arithmetic and copies ran while one was open for 6% -> 11% of each run, Pallas kernels for 5% -> 19%
where the time goes in v2:
time: 474 us; the launch traced here: 471 us
  Pallas kernels  181 us (38%)
  waiting for transfers between devices  122 us (26%)
  local copies, waits for them, and re-layouts  54.2 us (11%)
  starting transfers between devices  48.3 us (10%)
  other arithmetic  45.5 us (10%)
  between operations  20.5 us (4%)
    pallas_call x2, Pallas kernels, feed_forward(): pl.pallas_call(functools.partial(feed_forward_kernel, first, not first),...  89.1 us
    ppermute x17, waiting for transfers between devices, send_plane(): return lax.ppermute(value, 'dp', pairs)  44.5 us
    all_gather x1, waiting for transfers between devices, shards(): lax.all_gather(bundle, AXES, axis=0, tiled=True).reshape(devices, -1, TILE)  37.6 us
    pallas_call x2, Pallas kernels, attention_back(): pl.pallas_call(attention_back_kernel, grid=(count,), in_specs=[spec] * 5...  34.8 us
    ppermute x15, waiting for transfers between devices, send_line(): lax.ppermute(value, 'fsdp', [(i, (i + shift) % self.line) for i in range(...  26.9 us
    ppermute x15, starting transfers between devices, send_line(): lax.ppermute(value, 'fsdp', [(i, (i + shift) % self.line) for i in range(...  25.8 us
    pallas_call x1, Pallas kernels, attention(): pl.pallas_call(attention_kernel, grid=(PAIRS,), in_specs=[spec] * 3, out_...  24.3 us
    ppermute x17, starting transfers between devices, send_plane(): return lax.ppermute(value, 'dp', pairs)  20.8 us
  transfers between devices with their start and end apart: 41, of which 15 were waited for; matrix products, arithmetic and copies ran while one was open for 11% of the time, Pallas kernels for 19%

profile of v2, /device:TPU:0, one launch (start us, length us, event | category | flops | bytes accessed | tf_op | source)
XLA Modules:
  0.0 471.1 jit_solution(1017407417687342033)
XLA Ops:
  10.2 5.1 %collective-permute-start = (bf16[32,2176]{1,0:T(8,128)(2,1)S(1)}, bf16[32,2176]{1,0:T(8,128)(2,1)S(1)}, u32[]{:S(2)}, u32[]{:S(2)}) collective-permute-start(bf16[32,2176]{1,0:T(8,128)(2,1)S(1)} %fusion.33), channel_id=1, source_target_pairs={{0,3},{1,0},{2,1},{3,2},{4,7},{5,4},{6,5},{7,6},{8,11},{9,8},{10,9... | collective-permute-start | bytes 417800 | tf_op jit(solution)/shard_map/ppermute | solution.py:512
  16.4 3.1 collective-permute-done
  19.5 7.9 %collective-permute-done.1 = bf16[32,2176]{1,0:T(8,128)(2,1)S(1)} collective-permute-done((bf16[32,2176]{1,0:T(8,128)(2,1)S(1)}, bf16[32,2176]{1,0:T(8,128)(2,1)S(1)}, u32[]{:S(2)}, u32[]{:S(2)}) %collective-permute-start.1) | collective-permute-done | bytes 139296 | tf_op jit(solution)/shard_map/ppermute | solution.py:512
  31.1 13.0 %collective-permute-done.3 = bf16[4,32,2176]{2,1,0:T(8,128)(2,1)S(1)} collective-permute-done((bf16[4,32,2176]{2,1,0:T(8,128)(2,1)S(1)}, bf16[4,32,2176]{2,1,0:T(8,128)(2,1)S(1)}, u32[]{:S(2)}, u32[]{:S(2)}) %collective-permute-start.3) | collective-permute-done | bytes 557088 | tf_op jit(solution)/shard_map/ppermute | solution.py:509
  44.1 10.5 %collective-permute-done.4 = bf16[4,32,2176]{2,1,0:T(8,128)(2,1)S(1)} collective-permute-done((bf16[4,32,2176]{2,1,0:T(8,128)(2,1)S(1)}, bf16[4,32,2176]{2,1,0:T(8,128)(2,1)S(1)}, u32[]{:S(2)}, u32[]{:S(2)}) %collective-permute-start.4) | collective-permute-done | bytes 557088 | tf_op jit(solution)/shard_map/ppermute | solution.py:509
  57.6 3.1 multiply_sine_fusion
  75.9 10.4 %project.1 = (bf16[1024,1024]{1,0:T(8,128)(2,1)S(1)}, bf16[1024,1024]{1,0:T(8,128)(2,1)}, bf16[1024,1024]{1,0:T(8,128)(2,1)}, bf16[1024,1024]{1,0:T(8,128)(2,1)}, bf16[1024,512]{1,0:T(8,128)(2,1)S(1)}) custom-call(bf16[1024,1024]{1,0:T(8,128)(2,1)} %x_ref.3, bf16[1,1024]{1,0:T(2,128)(2,1)S(1)} %slice.71.gain_ref, bf16[1024,1536]{1,0:T(8,128)(2,1)} %bitcast.191, ...), custom_call_target="tpu_custom_call" | custom-call | flops 4294967296 | bytes 16777216 | tf_op jit(solution)/shard_map/project/pallas_call | solution.py:117
  90.2 24.3 %attention.1 = (bf16[1024,1024]{1,0:T(8,128)(2,1)S(1)}, f32[8,2,1024]{2,1,0:T(2,128)S(1)}) custom-call(bf16[1024,1024]{1,0:T(8,128)(2,1)S(1)} %copy-done.4, bf16[1024,1024]{1,0:T(8,128)(2,1)} %get-tuple-element.59.k_ref, bf16[1024,1024]{1,0:T(8,128)(2,1)} %get-tuple-element.60.v_ref), custom_call_target="tpu_custom_call" | custom-call | flops 8589934592 | bytes 8388608 | tf_op jit(solution)/shard_map/attention/pallas_call | solution.py:169
  115.8 37.6 %all-gather.2.cloned.1.call-done = bf16[18944,512]{1,0:T(8,128)(2,1)} async-done(((bf16[592,512]{1,0:T(8,128)(2,1)}), bf16[18944,512]{1,0:T(8,128)(2,1)}) %all-gather.2.cloned.1.call-update) | async-done | bytes 19398672 | tf_op jit(solution)/shard_map/all_gather | solution.py:630
  153.4 3.0 slice.96
  156.4 9.1 %copy.92 = bf16[32,2,88,512]{3,1,2,0:T(2,128)(2,1)S(1)} copy(bf16[32,2,88,512]{3,2,1,0:T(8,128)(2,1)S(1)} %bitcast.185) | data formatting | bytes 11534336 | tf_op jit(solution)/shard_map/reshape | solution.py:649
  165.5 4.3 copy.111
  169.8 41.5 %feed_forward.2 = (f32[1024,1024]{1,0:T(8,128)}, f32[1024,1024]{1,0:T(8,128)}, f32[1024,1024]{1,0:T(8,128)}, bf16[512,3072]{1,0:T(8,128)(2,1)}, bf16[512,3072]{1,0:T(8,128)(2,1)}, /*index=5*/bf16[2816,1024]{1,0:T(8,128)(2,1)}) custom-call(s32[8]{0:T(128)} %fusion.40.order_ref, bf16[1024,1024]{1,0:T(8,128)(2,1)} %x_ref.3, bf16[1024,1024]{1,0:T(8,128)(2,1)} %copy-done.12, ...), custom_call_target="tpu_custom_call" | custom-call | flops 33285996544 | bytes 41943040 | tf_op jit(solution)/shard_map/feed_forward/pallas_call | solution.py:394
  211.3 47.6 %feed_forward.3 = (bf16[1024,1024]{1,0:T(8,128)(2,1)}, f32[1024,1024]{1,0:T(8,128)}, bf16[1024,1024]{1,0:T(8,128)(2,1)}, bf16[512,3584]{1,0:T(8,128)(2,1)}, bf16...) custom-call(s32[8]{0:T(128)} %fusion.40.order_ref, ...), custom_call_target="tpu_custom_call", output_to_operand_aliasing={{5}: (13, {})} | custom-call | flops 28454158336 | bytes 41943040 | tf_op jit(solution)/shard_map/feed_forward/pallas_call | solution.py:394
  259.0 5.1 %constant_dynamic-slice_fusion.2 = (bf16[4,1,4,88,1024]{4,3,2,1,0:T(8,128)(2,1)}, bf16[4,1,4,88,1024]{4,3,2,1,0:T(8,128)(2,1)S(1)}) fusion(bf16[4,2,4,88,1024]{4,3,2,1,0:T(8,128)(2,1)} %bitcast.197, s32[]{:T(128)S(6)} %select_n.242, s32[]{:T(128)S(6)} %select_n.243), kind=kLoop, calls=%fused_computation.134 | loop fusion | bytes 11534344 | tf_op jit(solution)/shard_map/jit(dynamic_index_in_dim)/dynamic_slice | solution.py:516
  266.8 4.8 %collective-permute-done.9 = bf16[4,4,88,1024]{3,2,0,1:T(8,128)(2,1)} collective-permute-done((bf16[4,4,88,1024]{3,2,0,1:T(8,128)(2,1)}, bf16[4,4,88,1024]{3,2,0,1:T(8,128)(2,1)}, u32[]{:S(2)}, u32[]{:S(2)}) %collective-permute-start.9) | collective-permute-done | bytes 2883616 | tf_op jit(solution)/shard_map/ppermute | solution.py:501
  271.7 4.1 fusion.2
  279.5 3.1 fusion.1
  284.8 16.9 %attention_back.2 = (bf16[1024,512]{1,0:T(8,128)(2,1)S(1)}, bf16[1024,512]{1,0:T(8,128)(2,1)S(1)}, bf16[1024,512]{1,0:T(8,128)(2,1)S(1)}) custom-call(bf16[1024,1024]{1,0:T(8,128)(2,1)} %get-tuple-element.58.q_ref, bf16[1024,1024]{1,0:T(8,128)(2,1)} %get-tuple-element.59.k_ref, bf16[1024,1024]{1,0:T(8,128)(2,1)} %get-tuple-element.60.v_ref, ...), custom_call_target="tpu_custom_call" | custom-call | flops 10737418240 | bytes 8388608 | tf_op jit(solution)/shard_map/attention_back/pallas_call | solution.py:233
  303.2 4.2 fusion
  307.5 18.0 %attention_back.3 = (bf16[1024,512]{1,0:T(8,128)(2,1)S(1)}, bf16[1024,512]{1,0:T(8,128)(2,1)S(1)}, bf16[1024,512]{1,0:T(8,128)(2,1)S(1)}) custom-call(bf16[1024,1024]{1,0:T(8,128)(2,1)} %get-tuple-element.58.q_ref, bf16[1024,1024]{1,0:T(8,128)(2,1)} %get-tuple-element.59.k_ref, bf16[1024,1024]{1,0:T(8,128)(2,1)} %get-tuple-element.60.v_ref, ...), custom_call_target="tpu_custom_call" | custom-call | flops 10737418240 | bytes 8388608 | tf_op jit(solution)/shard_map/attention_back/pallas_call | solution.py:233
  333.0 13.9 %unproject.1 = (bf16[1024,1536]{1,0:T(8,128)(2,1)}, bf16[1024,1536]{1,0:T(8,128)(2,1)}, bf16[512,1024]{1,0:T(8,128)(2,1)}) custom-call(bf16[1024,1024]{1,0:T(8,128)(2,1)} %copy-done.3, bf16[1024,512]{1,0:T(8,128)(2,1)} %copy-done.5, bf16[1024,512]{1,0:T(8,128)(2,1)} %copy-done.6, bf16[1024,512]{1,0:T(8,128)(2,1)} %copy-done.7, bf16[1024,512]{1,0:T(8,128)(2,1)} %copy-done.8, ...), custom_call_target="tpu_custom_call" | custom-call | flops 5368709120 | bytes 16777216 | tf_op jit(solution)/shard_map/unproject/pallas_call | solution.py:435
  346.9 2.8 reshape.178
  359.2 16.5 %collective-permute-done.19 = bf16[4,32,3584]{2,1,0:T(8,128)(2,1)S(1)} collective-permute-done((bf16[4,32,3584]{2,1,0:T(8,128)(2,1)}, bf16[4,32,3584]{2,1,0:T(8,128)(2,1)S(1)}, u32[]{:S(2)}, u32[]{:S(2)}) %collective-permute-start.19) | collective-permute-done | bytes 917536 | tf_op jit(solution)/shard_map/ppermute | solution.py:509
  381.5 2.9 collective-permute-start.16
  386.6 10.8 %collective-permute-done.15 = bf16[32,3072]{1,0:T(8,128)(2,1)S(1)} collective-permute-done((bf16[32,3072]{1,0:T(8,128)(2,1)S(1)}, bf16[32,3072]{1,0:T(8,128)(2,1)S(1)}, u32[]{:S(2)}, u32[]{:S(2)}) %collective-permute-start.15) | collective-permute-done | bytes 196640 | tf_op jit(solution)/shard_map/ppermute | solution.py:512
  400.8 3.5 collective-permute-start.22
  405.1 4.7 collective-permute-done.21
  415.8 4.2 collective-permute-start.26
  422.6 8.3 %input_grad.1 = (bf16[1024,1024]{1,0:T(8,128)(2,1)}, f32[1,1024]{1,0:T(1,128)S(1)}) custom-call(bf16[1024,1024]{1,0:T(8,128)(2,1)S(1)} %copy-done.1, f32[1024,1024]{1,0:T(8,128)} %get-tuple-element.67.dh_ref, bf16[1024,1536]{1,0:T(8,128)(2,1)S(1)} %copy-done, bf16[1,1024]{1,0:T(2,128)(2,1)S(1)} %slice.71.gain_ref, bf16[1024,1536]{1,0:T(8,128)(2,1)} %bitcast.192), custom_call_target="tpu_custom_call" | custom-call | flops 3221225472 | bytes 16777216 | tf_op jit(solution)/shard_map/input_grad/pallas_call | solution.py:475
  442.8 3.7 collective-permute-done.38
  448.2 2.9 collective-permute-done.39
  (252 shorter events, 99.5 us)
Async XLA Ops:
  7.2 146.2 %all-gather.2.cloned.1.call-start = ((), (), s32[]{:S(2)}) async-start(), calls=%async_computation | async-start | bytes 20004864 | tf_op jit(solution)/shard_map/all_gather | solution.py:630
  15.3 12.0 %collective-permute-start.1 = (bf16[32,2176]{1,0:T(8,128)(2,1)S(1)}, bf16[32,2176]{1,0:T(8,128)(2,1)S(1)}, u32[]{:S(2)}, u32[]{:S(2)}) collective-permute-start(bf16[32,2176]{1,0:T(8,128)(2,1)S(1)} %fusion.33), channel_id=1, source_target_pairs={{0,2},{1,3},{2,0},{3,1},{4,6},{5,7},{6,4},{7,5},{8,10},{9,11},{10,... | collective-permute-start | bytes 417800 | tf_op jit(solution)/shard_map/ppermute | solution.py:512
  15.3 12.1 %collective-permute-start.2 = (bf16[32,2176]{1,0:T(8,128)(2,1)S(1)}, bf16[32,2176]{1,0:T(8,128)(2,1)S(1)}, u32[]{:S(2)}, u32[]{:S(2)}) collective-permute-start(bf16[32,2176]{1,0:T(8,128)(2,1)S(1)} %fusion.33), channel_id=1, source_target_pairs={{0,1},{1,2},{2,3},{3,0},{4,5},{5,6},{6,7},{7,4},{8,9},{9,10},{10,1... | collective-permute-start | bytes 417800 | tf_op jit(solution)/shard_map/ppermute | solution.py:512
  27.6 16.6 %collective-permute-start.3 = (bf16[4,32,2176]{2,1,0:T(8,128)(2,1)S(1)}, bf16[4,32,2176]{2,1,0:T(8,128)(2,1)S(1)}, u32[]{:S(2)}, u32[]{:S(2)}) collective-permute-start(bf16[4,32,2176]{2,1,0:T(8,128)(2,1)S(1)} %constant_dynamic-slice_fusion.3), channel_id=1, source_target_pairs={{0,24},{4,28},{8,16},{12,20},{16,8},{20,12},{24,0},{28,4},{1,25},{... | collective-permute-start | bytes 1671176 | tf_op jit(solution)/shard_map/ppermute | solution.py:509
  30.3 24.3 %collective-permute-start.4 = (bf16[4,32,2176]{2,1,0:T(8,128)(2,1)S(1)}, bf16[4,32,2176]{2,1,0:T(8,128)(2,1)S(1)}, u32[]{:S(2)}, u32[]{:S(2)}) collective-permute-start(bf16[4,32,2176]{2,1,0:T(8,128)(2,1)S(1)} %constant_dynamic-slice_fusion.3), channel_id=1, source_target_pairs={{0,16},{4,20},{8,24},{12,28},{16,0},{20,4},{24,8},{28,12},{1,17},{... | collective-permute-start | bytes 1671176 | tf_op jit(solution)/shard_map/ppermute | solution.py:509
  30.6 24.0 %collective-permute-start.5 = (bf16[4,32,2176]{2,1,0:T(8,128)(2,1)S(1)}, bf16[4,32,2176]{2,1,0:T(8,128)(2,1)S(1)}, u32[]{:S(2)}, u32[]{:S(2)}) collective-permute-start(bf16[4,32,2176]{2,1,0:T(8,128)(2,1)S(1)} %constant_dynamic-slice_fusion.3), channel_id=1, source_target_pairs={{0,8},{4,12},{8,0},{12,4},{16,24},{20,28},{24,16},{28,20},{1,9},{5... | collective-permute-start | bytes 1671176 | tf_op jit(solution)/shard_map/ppermute | solution.py:509
  57.5 11.1 %collective-permute-start.6 = (bf16[4,4,32,2176]{3,2,1,0:T(8,128)(2,1)}, bf16[4,4,32,2176]{3,2,1,0:T(8,128)(2,1)}, u32[]{:S(2)}, u32[]{:S(2)}) collective-permute-start(bf16[4,4,32,2176]{3,2,1,0:T(8,128)(2,1)} %pad_maximum_fusion.1), channel_id=1, source_target_pairs={{0,4},{4,0},{8,12},{12,8},{16,20},{20,16},{24,28},{28,24},{1,5},{5... | collective-permute-start | bytes 6684680 | tf_op jit(solution)/shard_map/ppermute | solution.py:501
  266.3 12.8 %collective-permute-start.7 = (bf16[4,4,32,3072]{3,2,1,0:T(8,128)(2,1)}, bf16[4,4,32,3072]{3,2,1,0:T(8,128)(2,1)}, u32[]{:S(2)}, u32[]{:S(2)}) collective-permute-start(bf16[4,4,32,3072]{3,2,1,0:T(8,128)(2,1)} %bitcast.28), channel_id=1, source_target_pairs={{0,4},{4,0},{8,12},{12,8},{16,20},{20,16},{24,28},{28,24},{1,5},{5... | collective-permute-start | bytes 9437192 | tf_op jit(solution)/shard_map/ppermute | solution.py:501
  266.6 35.1 %collective-permute-start.8 = (bf16[4,4,32,3584]{3,2,1,0:T(8,128)(2,1)}, bf16[4,4,32,3584]{3,2,1,0:T(8,128)(2,1)}, u32[]{:S(2)}, u32[]{:S(2)}) collective-permute-start(bf16[4,4,32,3584]{3,2,1,0:T(8,128)(2,1)} %bitcast.30), channel_id=1, source_target_pairs={{0,4},{4,0},{8,12},{12,8},{16,20},{20,16},{24,28},{28,24},{1,5},{5... | collective-permute-start | bytes 11010056 | tf_op jit(solution)/shard_map/ppermute | solution.py:501
  277.2 74.0 %collective-permute-start.29 = (bf16[4,88,1024]{2,1,0:T(8,128)(2,1)}, bf16[4,88,1024]{2,1,0:T(8,128)(2,1)}, u32[]{:S(2)}, u32[]{:S(2)}) collective-permute-start(bf16[4,88,1024]{2,1,0:T(8,128)(2,1)} %get-tuple-element.133), channel_id=1, source_target_pairs={{0,1},{1,2},{2,3},{3,0},{4,5},{5,6},{6,7},{7,4},{8,9},{9,10},{10,1... | collective-permute-start | bytes 2162696 | tf_op jit(solution)/shard_map/ppermute | solution.py:512
  277.3 75.7 %collective-permute-start.30 = (bf16[4,88,1024]{2,1,0:T(8,128)(2,1)}, bf16[4,88,1024]{2,1,0:T(8,128)(2,1)}, u32[]{:S(2)}, u32[]{:S(2)}) collective-permute-start(bf16[4,88,1024]{2,1,0:T(8,128)(2,1)} %get-tuple-element.135), channel_id=1, source_target_pairs={{0,2},{1,3},{2,0},{3,1},{4,6},{5,7},{6,4},{7,5},{8,10},{9,11},{10,... | collective-permute-start | bytes 2162696 | tf_op jit(solution)/shard_map/ppermute | solution.py:512
  282.7 44.5 %collective-permute-start.10 = (bf16[4,32,3072]{2,1,0:T(8,128)(2,1)S(1)}, bf16[4,32,3072]{2,1,0:T(8,128)(2,1)S(1)}, u32[]{:S(2)}, u32[]{:S(2)}) collective-permute-start(bf16[4,32,3072]{2,1,0:T(8,128)(2,1)S(1)} %get-tuple-element.130), channel_id=1, source_target_pairs={{0,8},{4,12},{8,0},{12,4},{16,24},{20,28},{24,16},{28,20},{1,9},{5... | collective-permute-start | bytes 2359304 | tf_op jit(solution)/shard_map/ppermute | solution.py:509
  284.2 45.3 %collective-permute-start.11 = (bf16[4,32,3072]{2,1,0:T(8,128)(2,1)S(1)}, bf16[4,32,3072]{2,1,0:T(8,128)(2,1)S(1)}, u32[]{:S(2)}, u32[]{:S(2)}) collective-permute-start(bf16[4,32,3072]{2,1,0:T(8,128)(2,1)S(1)} %get-tuple-element.132), channel_id=1, source_target_pairs={{0,16},{4,20},{8,24},{12,28},{16,0},{20,4},{24,8},{28,12},{1,17},{... | collective-permute-start | bytes 2359304 | tf_op jit(solution)/shard_map/ppermute | solution.py:509
  301.7 29.3 %collective-permute-start.12 = (bf16[4,32,3072]{2,1,0:T(8,128)(2,1)S(1)}, bf16[4,32,3072]{2,1,0:T(8,128)(2,1)S(1)}, u32[]{:S(2)}, u32[]{:S(2)}) collective-permute-start(bf16[4,32,3072]{2,1,0:T(8,128)(2,1)S(1)} %get-tuple-element.131), channel_id=1, source_target_pairs={{0,24},{4,28},{8,16},{12,20},{16,8},{20,12},{24,0},{28,4},{1,25},{... | collective-permute-start | bytes 2359304 | tf_op jit(solution)/shard_map/ppermute | solution.py:509
  327.2 25.9 %collective-permute-start.31 = (bf16[4,88,1024]{2,1,0:T(8,128)(2,1)}, bf16[4,88,1024]{2,1,0:T(8,128)(2,1)}, u32[]{:S(2)}, u32[]{:S(2)}) collective-permute-start(bf16[4,88,1024]{2,1,0:T(8,128)(2,1)} %get-tuple-element.134), channel_id=1, source_target_pairs={{0,3},{1,0},{2,1},{3,2},{4,7},{5,4},{6,5},{7,6},{8,11},{9,8},{10,9... | collective-permute-start | bytes 2162696 | tf_op jit(solution)/shard_map/ppermute | solution.py:512
  329.5 27.5 %collective-permute-start.17 = (bf16[4,32,3584]{2,1,0:T(8,128)(2,1)}, bf16[4,32,3584]{2,1,0:T(8,128)(2,1)}, u32[]{:S(2)}, u32[]{:S(2)}) collective-permute-start(bf16[4,32,3584]{2,1,0:T(8,128)(2,1)} %get-tuple-element.127), channel_id=1, source_target_pairs={{0,8},{4,12},{8,0},{12,4},{16,24},{20,28},{24,16},{28,20},{1,9},{5... | collective-permute-start | bytes 2752520 | tf_op jit(solution)/shard_map/ppermute | solution.py:509
  331.0 26.8 %collective-permute-start.18 = (bf16[4,32,3584]{2,1,0:T(8,128)(2,1)}, bf16[4,32,3584]{2,1,0:T(8,128)(2,1)}, u32[]{:S(2)}, u32[]{:S(2)}) collective-permute-start(bf16[4,32,3584]{2,1,0:T(8,128)(2,1)} %get-tuple-element.129), channel_id=1, source_target_pairs={{0,16},{4,20},{8,24},{12,28},{16,0},{20,4},{24,8},{28,12},{1,17},{... | collective-permute-start | bytes 2752520 | tf_op jit(solution)/shard_map/ppermute | solution.py:509
  351.2 24.6 %collective-permute-start.19 = (bf16[4,32,3584]{2,1,0:T(8,128)(2,1)}, bf16[4,32,3584]{2,1,0:T(8,128)(2,1)S(1)}, u32[]{:S(2)}, u32[]{:S(2)}) collective-permute-start(bf16[4,32,3584]{2,1,0:T(8,128)(2,1)} %get-tuple-element.128), channel_id=1, source_target_pairs={{0,24},{4,28},{8,16},{12,20},{16,8},{20,12},{24,0},{28,4},{1,25},{... | collective-permute-start | bytes 2752520 | tf_op jit(solution)/shard_map/ppermute | solution.py:509
  353.0 25.0 %collective-permute-start.13 = (bf16[4,4,32,2048]{3,2,1,0:T(8,128)(2,1)S(1)}, bf16[4,4,32,2048]{3,2,1,0:T(8,128)(2,1)S(1)}, u32[]{:S(2)}, u32[]{:S(2)}) collective-permute-start(bf16[4,4,32,2048]{3,2,1,0:T(8,128)(2,1)S(1)} %fusion.5), channel_id=1, source_target_pairs={{0,4},{4,0},{8,12},{12,8},{16,20},{20,16},{24,28},{28,24},{1,5},{5... | collective-permute-start | bytes 6291464 | tf_op jit(solution)/shard_map/ppermute | solution.py:501
  355.5 26.0 %collective-permute-start.32 = (bf16[88,1024]{1,0:T(8,128)(2,1)S(1)}, bf16[88,1024]{1,0:T(8,128)(2,1)S(1)}, u32[]{:S(2)}, u32[]{:S(2)}) collective-permute-start(bf16[88,1024]{1,0:T(8,128)(2,1)S(1)} %get-tuple-element.149), channel_id=1, source_target_pairs={{0,8},{4,12},{8,0},{12,4},{16,24},{20,28},{24,16},{28,20},{1,9},{5... | collective-permute-start | bytes 540680 | tf_op jit(solution)/shard_map/ppermute | solution.py:509
  357.1 27.4 %collective-permute-start.33 = (bf16[88,1024]{1,0:T(8,128)(2,1)S(1)}, bf16[88,1024]{1,0:T(8,128)(2,1)S(1)}, u32[]{:S(2)}, u32[]{:S(2)}) collective-permute-start(bf16[88,1024]{1,0:T(8,128)(2,1)S(1)} %get-tuple-element.151), channel_id=1, source_target_pairs={{0,16},{4,20},{8,24},{12,28},{16,0},{20,4},{24,8},{28,12},{1,17},{... | collective-permute-start | bytes 540680 | tf_op jit(solution)/shard_map/ppermute | solution.py:509
  357.7 26.8 %collective-permute-start.34 = (bf16[88,1024]{1,0:T(8,128)(2,1)S(1)}, bf16[88,1024]{1,0:T(8,128)(2,1)S(1)}, u32[]{:S(2)}, u32[]{:S(2)}) collective-permute-start(bf16[88,1024]{1,0:T(8,128)(2,1)S(1)} %get-tuple-element.150), channel_id=1, source_target_pairs={{0,24},{4,28},{8,16},{12,20},{16,8},{20,12},{24,0},{28,4},{1,25},{... | collective-permute-start | bytes 540680 | tf_op jit(solution)/shard_map/ppermute | solution.py:509
  375.7 10.3 %collective-permute-start.14 = (bf16[32,3072]{1,0:T(8,128)(2,1)S(1)}, bf16[32,3072]{1,0:T(8,128)(2,1)S(1)}, u32[]{:S(2)}, u32[]{:S(2)}) collective-permute-start(bf16[32,3072]{1,0:T(8,128)(2,1)S(1)} %get-tuple-element.146), channel_id=1, source_target_pairs={{0,1},{1,2},{2,3},{3,0},{4,5},{5,6},{6,7},{7,4},{8,9},{9,10},{10,1... | collective-permute-start | bytes 589832 | tf_op jit(solution)/shard_map/ppermute | solution.py:512
  378.0 19.3 %collective-permute-start.15 = (bf16[32,3072]{1,0:T(8,128)(2,1)S(1)}, bf16[32,3072]{1,0:T(8,128)(2,1)S(1)}, u32[]{:S(2)}, u32[]{:S(2)}) collective-permute-start(bf16[32,3072]{1,0:T(8,128)(2,1)S(1)} %get-tuple-element.148), channel_id=1, source_target_pairs={{0,2},{1,3},{2,0},{3,1},{4,6},{5,7},{6,4},{7,5},{8,10},{9,11},{10,... | collective-permute-start | bytes 589832 | tf_op jit(solution)/shard_map/ppermute | solution.py:512
  381.5 18.7 %collective-permute-start.16 = (bf16[32,3072]{1,0:T(8,128)(2,1)S(1)}, bf16[32,3072]{1,0:T(8,128)(2,1)S(1)}, u32[]{:S(2)}, u32[]{:S(2)}) collective-permute-start(bf16[32,3072]{1,0:T(8,128)(2,1)S(1)} %get-tuple-element.147), channel_id=1, source_target_pairs={{0,3},{1,0},{2,1},{3,2},{4,7},{5,4},{6,5},{7,6},{8,11},{9,8},{10,9... | collective-permute-start | bytes 589832 | tf_op jit(solution)/shard_map/ppermute | solution.py:512
  384.5 16.4 %collective-permute-start.20 = (bf16[32,3584]{1,0:T(8,128)(2,1)S(1)}, bf16[32,3584]{1,0:T(8,128)(2,1)S(1)}, u32[]{:S(2)}, u32[]{:S(2)}) collective-permute-start(bf16[32,3584]{1,0:T(8,128)(2,1)S(1)} %get-tuple-element.143), channel_id=1, source_target_pairs={{0,1},{1,2},{2,3},{3,0},{4,5},{5,6},{6,7},{7,4},{8,9},{9,10},{10,1... | collective-permute-start | bytes 688136 | tf_op jit(solution)/shard_map/ppermute | solution.py:512
  384.5 28.4 %collective-permute-start.23 = (bf16[4,32,2048]{2,1,0:T(8,128)(2,1)}, bf16[4,32,2048]{2,1,0:T(8,128)(2,1)}, u32[]{:S(2)}, u32[]{:S(2)}) collective-permute-start(bf16[4,32,2048]{2,1,0:T(8,128)(2,1)} %get-tuple-element.140), channel_id=1, source_target_pairs={{0,8},{4,12},{8,0},{12,4},{16,24},{20,28},{24,16},{28,20},{1,9},{5... | collective-permute-start | bytes 1572872 | tf_op jit(solution)/shard_map/ppermute | solution.py:509
  386.0 26.9 %collective-permute-start.24 = (bf16[4,32,2048]{2,1,0:T(8,128)(2,1)}, bf16[4,32,2048]{2,1,0:T(8,128)(2,1)}, u32[]{:S(2)}, u32[]{:S(2)}) collective-permute-start(bf16[4,32,2048]{2,1,0:T(8,128)(2,1)} %get-tuple-element.142), channel_id=1, source_target_pairs={{0,16},{4,20},{8,24},{12,28},{16,0},{20,4},{24,8},{28,12},{1,17},{... | collective-permute-start | bytes 1572872 | tf_op jit(solution)/shard_map/ppermute | solution.py:509
  397.4 15.6 %collective-permute-start.25 = (bf16[4,32,2048]{2,1,0:T(8,128)(2,1)}, bf16[4,32,2048]{2,1,0:T(8,128)(2,1)}, u32[]{:S(2)}, u32[]{:S(2)}) collective-permute-start(bf16[4,32,2048]{2,1,0:T(8,128)(2,1)} %get-tuple-element.141), channel_id=1, source_target_pairs={{0,24},{4,28},{8,16},{12,20},{16,8},{20,12},{24,0},{28,4},{1,25},{... | collective-permute-start | bytes 1572872 | tf_op jit(solution)/shard_map/ppermute | solution.py:509
  415.8 15.2 %collective-permute-start.26 = (bf16[32,2048]{1,0:T(8,128)(2,1)}, bf16[32,2048]{1,0:T(8,128)(2,1)}, u32[]{:S(2)}, u32[]{:S(2)}) collective-permute-start(bf16[32,2048]{1,0:T(8,128)(2,1)} %get-tuple-element.152), channel_id=1, source_target_pairs={{0,1},{1,2},{2,3},{3,0},{4,5},{5,6},{6,7},{7,4},{8,9},{9,10},{10,1... | collective-permute-start | bytes 393224 | tf_op jit(solution)/shard_map/ppermute | solution.py:512
  420.0 11.0 %collective-permute-start.27 = (bf16[32,2048]{1,0:T(8,128)(2,1)}, bf16[32,2048]{1,0:T(8,128)(2,1)}, u32[]{:S(2)}, u32[]{:S(2)}) collective-permute-start(bf16[32,2048]{1,0:T(8,128)(2,1)} %get-tuple-element.154), channel_id=1, source_target_pairs={{0,2},{1,3},{2,0},{3,1},{4,6},{5,7},{6,4},{7,5},{8,10},{9,11},{10,... | collective-permute-start | bytes 393224 | tf_op jit(solution)/shard_map/ppermute | solution.py:512
  420.0 11.0 %collective-permute-start.28 = (bf16[32,2048]{1,0:T(8,128)(2,1)}, bf16[32,2048]{1,0:T(8,128)(2,1)}, u32[]{:S(2)}, u32[]{:S(2)}) collective-permute-start(bf16[32,2048]{1,0:T(8,128)(2,1)} %get-tuple-element.153), channel_id=1, source_target_pairs={{0,3},{1,0},{2,1},{3,2},{4,7},{5,4},{6,5},{7,6},{8,11},{9,8},{10,9... | collective-permute-start | bytes 393224 | tf_op jit(solution)/shard_map/ppermute | solution.py:512
  (56 other events, 295.7 us)
Sparse Core Ops, SparseCore 0:
  11.5 141.9 all-gather.1

commit v3 on v2

v3 whole, which is shorter than its diff:
```python
import functools
import math

import jax
import jax.numpy as jnp
from jax import lax
from jax.experimental import pallas as pl
from jax.experimental.pallas import tpu as pltpu
from jax.sharding import PartitionSpec as P

HQ = 16
HD = 64
LATENT_HEADS = 2
LATENT_WIDTH = 256
FF = 2816
NDOM = 16
STEP = 10
ROPE = 32
QUERY_WIDTH = HQ * HD
GROUP_WIDTH = QUERY_WIDTH // LATENT_HEADS
LANES = 128
PAIRS = QUERY_WIDTH // LANES
PAIRS_PER_LATENT = PAIRS // LATENT_HEADS

MAX_NORM = 1.0
BETA_ONE = 0.9
BETA_TWO = 0.95
RATE_MATRIX = 0.02
RATE_OUTPUT = 0.2
RATE_GAIN = 1.0
DECAY_MATRIX = 0.1
EPSILON_ADAM = 1e-08
EPSILON_NORM = 1e-06
ROPE_BASE = 10000.0

AXES = ("dp", "fsdp")
BF = jnp.bfloat16
F32 = jnp.float32
LOG2E = 1.4426950408889634
SCALE = HD**-0.5
NN = (((1,), (0,)), ((), ()))
NT = (((1,), (1,)), ((), ()))
TN = (((0,), (0,)), ((), ()))
MIB = 1 << 20
CHUNK = 256
TILE = 2 * CHUNK
FIRST_CHUNKS = 7


def dot(left, right, dims):
    return lax.dot_general(left, right, dims, preferred_element_type=F32)


def cost(microseconds):
    return pl.CostEstimate(flops=int(microseconds * 1e9), bytes_accessed=1 << 20, transcendentals=0)


def resident(*shape):
    return pl.BlockSpec(shape, lambda *step: (0,) * len(shape), pipeline_mode=pl.Buffered(1))


def rotation_tables(length):
    half = ROPE // 2
    lane = jnp.arange(LANES) % HD
    freqs = jnp.where(lane < ROPE, ROPE_BASE ** (-(lane % half).astype(F32) / half), 0.0)
    theta = jnp.arange(length).astype(F32)[:, None] * freqs[None, :]
    sine = jnp.sin(theta)
    ahead = jnp.where(lane < half, -sine, 0.0)
    behind = jnp.where((lane >= half) & (lane < ROPE), sine, 0.0)
    return jnp.cos(theta), ahead, behind


def rotate(values, own, ahead, behind):
    half = ROPE // 2
    return (
        values * own
        + pltpu.roll(values, LANES - half, 1) * ahead
        + pltpu.roll(values, half, 1) * behind
    )


def unrotate(values, own, ahead, behind):
    half = ROPE // 2
    return (
        values * own
        - pltpu.roll(values, LANES - half, 1) * ahead
        - pltpu.roll(values, half, 1) * behind
    )


def lay_out(devices, inverse_ref, mine_ref, other_ref, win_ref, wup_ref, gains_ref):
    plane, size = mine_ref.shape[:2]
    width, side = win_ref.shape
    rows, ups, pieces = width // devices, wup_ref.shape[0] // devices, wup_ref.shape[1] // TILE
    line = size // rows
    gains = [jnp.zeros((1, width), F32)] * 2
    source = lambda rows, columns: lax.broadcasted_iota(jnp.int32, (rows, columns), 0)
    target = lambda rows, columns: lax.broadcasted_iota(jnp.int32, (rows, columns), 1)
    share = width // devices
    spread = (source(LANES, width) == target(LANES, width) % share).astype(BF)
    for place in range(inverse_ref.shape[0]):
        ref = mine_ref if place < plane else other_ref
        block = ref[place % plane]
        index = inverse_ref[place]
        win_ref[pl.ds(pl.multiple_of(index * size, size), size), :] = block[:, :side]
        for z in range(line):
            start = pl.multiple_of((index * line + z) * ups, ups)
            for piece in range(pieces):
                row = z * rows + piece * ups
                columns = slice(piece * TILE, (piece + 1) * TILE)
                wup_ref[pl.ds(start, ups), columns] = block[row : row + ups, side : side + TILE]
        spots = block[:, side + TILE :]
        for which in range(2):
            pick = (target(line, size) == source(line, size) * rows + which).astype(BF)
            found = dot(dot(pick, spots, NN).astype(BF), spread, NN)
            here = target(line, width) // share == source(line, width) + index * line
            gains[which] += jnp.sum(jnp.where(here, found, 0.0), axis=0, keepdims=True)
    gains_ref[...] = jnp.concatenate(gains, axis=0)


def project_kernel(devices, *refs):
    if devices:
        inverse_ref, x_ref, mine_ref, other_ref = refs[:4]
        own_ref, ahead_ref, behind_ref, a1_ref, q_ref, k_ref, v_ref, c_ref, win_ref, wup_ref, gains_ref = refs[4:]

        @pl.when(pl.program_id(0) == 0)
        def _():
            lay_out(devices, inverse_ref, mine_ref, other_ref, win_ref, wup_ref, gains_ref)
    else:
        x_ref, win_ref, wup_ref, gains_ref = refs[1:5]
        own_ref, ahead_ref, behind_ref, a1_ref, q_ref, k_ref, v_ref, c_ref = refs[5:]
    tables = (own_ref[...], ahead_ref[...], behind_ref[...])
    x = x_ref[...].astype(F32)
    inverse = lax.rsqrt(jnp.mean(x * x, axis=1, keepdims=True) + EPSILON_NORM)
    a1 = (x * inverse * gains_ref[:1, :]).astype(BF)
    a1_ref[...] = a1
    joined = dot(a1, win_ref[...], NN)
    for pair in range(PAIRS):
        lanes = slice(pair * LANES, (pair + 1) * LANES)
        q_ref[:, lanes] = rotate(joined[:, lanes], *tables).astype(BF)
    c = joined[:, QUERY_WIDTH:].astype(BF)
    c_ref[...] = c
    for head in range(LATENT_HEADS):
        latent = slice(head * LATENT_WIDTH, (head + 1) * LATENT_WIDTH)
        both = dot(c[:, latent], wup_ref[latent, :], NN)
        for pair in range(PAIRS_PER_LATENT):
            lanes = slice(pair * LANES, (pair + 1) * LANES)
            out = slice(head * GROUP_WIDTH + pair * LANES, head * GROUP_WIDTH + (pair + 1) * LANES)
            k_ref[:, out] = rotate(both[:, lanes], *tables).astype(BF)
        out = slice(head * GROUP_WIDTH, (head + 1) * GROUP_WIDTH)
        v_ref[:, out] = both[:, GROUP_WIDTH:].astype(BF)


def project(devices, inverse, x, tables, *weights):
    length, width = x.shape
    tile = min(256, length)
    latents = LATENT_HEADS * LATENT_WIDTH
    rows = lambda columns: pl.BlockSpec((tile, columns), lambda i, *_: (i, 0))
    shape = lambda columns: jax.ShapeDtypeStruct((length, columns), BF)
    out_specs = [rows(width), rows(QUERY_WIDTH), rows(QUERY_WIDTH), rows(QUERY_WIDTH), rows(latents)]
    out_shape = [shape(width), shape(QUERY_WIDTH), shape(QUERY_WIDTH), shape(QUERY_WIDTH), shape(latents)]
    if devices:
        more = [((width, QUERY_WIDTH + latents), BF), ((latents, 2 * GROUP_WIDTH), BF), ((2, width), F32)]
        out_specs += [resident(*s) for s, _ in more]
        out_shape += [jax.ShapeDtypeStruct(*s) for s in more]
    return pl.pallas_call(
        functools.partial(project_kernel, devices),
        grid_spec=pltpu.PrefetchScalarGridSpec(
            num_scalar_prefetch=1,
            grid=(length // tile,),
            in_specs=[rows(width)] + [resident(*w.shape) for w in weights] + [rows(LANES)] * 3,
            out_specs=out_specs,
        ),
        out_shape=out_shape,
        compiler_params=pltpu.CompilerParams(vmem_limit_bytes=60 * MIB),
        cost_estimate=cost(20),
        name="project",
    )(inverse, x, *weights, *tables)


def halves(pair, axis):
    first = lax.broadcasted_iota(jnp.int32, pair.shape, axis) < HD
    zero = jnp.zeros_like(pair)
    return (jnp.where(first, pair, zero), jnp.where(first, zero, pair))


def not_after(block):
    keys = lax.broadcasted_iota(jnp.int32, (block, block), 0)
    queries = lax.broadcasted_iota(jnp.int32, (block, block), 1)
    return keys <= queries


def attention_kernel(q_ref, k_ref, v_ref, o_ref, log_ref):
    length = q_ref.shape[0]
    block = min(256, length)
    values = halves(v_ref[...].T, 0)
    for start in range(0, length, block):
        stop = start + block
        queries = halves(q_ref[start:stop, :], 1)
        probs = []
        for head in range(2):
            scores = dot(k_ref[:stop, :], queries[head], NT) * (SCALE * LOG2E)
            last = jnp.where(not_after(block), scores[start:, :], -1e30)
            scores = jnp.concatenate([scores[:start, :], last], axis=0) if start else last
            peak = jnp.max(scores, axis=0, keepdims=True)
            expo = jnp.exp2(scores - peak)
            total = jnp.sum(expo, axis=0, keepdims=True)
            log_ref[0, head : head + 1, start:stop] = peak + jnp.log2(total)
            probs.append((expo * (1.0 / total)).astype(BF))
        mixed = dot(values[0][:, :stop], probs[0], NN) + dot(values[1][:, :stop], probs[1], NN)
        o_ref[start:stop, :] = mixed.T.astype(BF)


def attention(q, k, v):
    length, width = q.shape
    spec = pl.BlockSpec((length, LANES), lambda i: (0, i))
    logs = pl.BlockSpec((1, 2, length), lambda i: (i, 0, 0))
    return pl.pallas_call(
        attention_kernel,
        grid=(PAIRS,),
        in_specs=[spec] * 3,
        out_specs=[spec, logs],
        out_shape=[
            jax.ShapeDtypeStruct((length, width), BF),
            jax.ShapeDtypeStruct((PAIRS, 2, length), F32),
        ],
        compiler_params=pltpu.CompilerParams(vmem_limit_bytes=60 * MIB),
        cost_estimate=cost(1),
        name="attention",
    )(q, k, v)


def attention_back_kernel(q_ref, k_ref, v_ref, o_ref, do_ref, log_ref, own_ref, ahead_ref, behind_ref,
                          dq_ref, dk_ref, dv_ref, total_ref):
    length = q_ref.shape[0]
    block = min(256, length)
    tables = lambda rows: (own_ref[rows, :], ahead_ref[rows, :], behind_ref[rows, :])
    product = (do_ref[...].astype(F32) * o_ref[...].astype(F32)).T
    deltas = (
        jnp.sum(product[:HD], axis=0, keepdims=True),
        jnp.sum(product[HD:], axis=0, keepdims=True),
    )
    keys = halves(k_ref[...].T, 0)
    for start in range(0, length, block):
        stop = start + block
        queries = halves(q_ref[start:, :], 1)
        grads = halves(do_ref[start:, :], 1)
        dk = dv = dq = None
        for head in range(2):
            scores = dot(k_ref[start:stop, :], queries[head], NT) * (SCALE * LOG2E)
            probs = jnp.exp2(scores - log_ref[0, head : head + 1, start:])
            first = jnp.where(not_after(block), probs[:, :block], 0.0)
            probs = jnp.concatenate([first, probs[:, block:]], axis=1) if stop < length else first
            dprobs = dot(v_ref[start:stop, :], grads[head], NT)
            dscores = (probs * (dprobs - deltas[head][:, start:])).astype(BF)
            parts = (
                dot(probs.astype(BF), grads[head], NN),
                dot(dscores, queries[head], NN),
                dot(keys[head][:, start:stop], dscores, NN),
            )
            dv = parts[0] if dv is None else dv + parts[0]
            dk = parts[1] if dk is None else dk + parts[1]
            dq = parts[2] if dq is None else dq + parts[2]
        dv_ref[start:stop, :] = dv.astype(BF)
        dk_ref[start:stop, :] = unrotate(dk * SCALE, *tables(slice(start, stop))).astype(BF)
        if start == 0:
            total_ref[...] = dq
        else:
            total_ref[:, start:] += dq
    dq_ref[...] = unrotate(total_ref[...].T * SCALE, *tables(slice(None))).astype(BF)


def attention_back(weight, start, count, q, k, v, o, do, logs, tables):
    length = q.shape[0]
    spec = pl.BlockSpec((length, LANES), lambda i: (0, i + start))
    out = pl.BlockSpec((length, LANES), lambda i: (0, i))
    log = pl.BlockSpec((1, 2, length), lambda i: (i + start, 0, 0))
    return pl.pallas_call(
        attention_back_kernel,
        grid=(count,),
        in_specs=[spec] * 5 + [log] + [resident(length, LANES)] * 3,
        out_specs=[out] * 3,
        out_shape=[jax.ShapeDtypeStruct((length, count * LANES), BF)] * 3,
        scratch_shapes=[pltpu.VMEM((LANES, length), F32)],
        compiler_params=pltpu.CompilerParams(vmem_limit_bytes=60 * MIB),
        cost_estimate=cost(weight),
        name="attention_back",
    )(q, k, v, o, do, logs, *tables)


def place_rows(target_ref, columns, values, order_ref):
    blocks = order_ref.shape[0]
    size = values.shape[1] // blocks
    for block in range(blocks):
        start = pl.multiple_of(order_ref[block] * size, size)
        target_ref[pl.ds(start, size), columns] = values[:, block * size : (block + 1) * size].T


def natural_rows(target_ref, piece_refs, places, inverse_ref):
    size = target_ref.shape[0] // inverse_ref.shape[0]
    for ref, (_, entries) in zip(piece_refs, places):
        for number, (place, row) in enumerate(entries):
            start = pl.multiple_of(inverse_ref[place] * size + row, math.gcd(size, row or size))
            target_ref[pl.ds(start, ref.shape[1]), :] = ref[number]


def natural_copies(target_ref, piece_refs, places, inverse_ref, sems, first, last):
    size = target_ref.shape[0] // inverse_ref.shape[0]
    starts = sorted({column for column, _ in places})
    copy = lambda ref, number, column, block: pltpu.make_async_copy(
        ref.at[number],
        target_ref.at[pl.ds(block * size, size), pl.ds(column, ref.shape[2])],
        sems.at[block, starts.index(column)],
    )

    def start():
        for ref, (column, entries) in zip(piece_refs, places):
            for number, (place, _) in enumerate(entries):
                block = inverse_ref[place]

                @pl.when((block >= first) & (block <= last))
                def _():
                    copy(ref, number, column, block).start()

    def wait(block):
        for column in starts:
            ref = next(ref for ref, (at, _) in zip(piece_refs, places) if at == column)
            copy(ref, 0, column, block).wait()

    return start, wait


def feed_forward_kernel(first, start, count, places, order_ref, inverse_ref, *refs):
    out_places, w_places, d_places = places
    out_refs, refs = refs[: len(out_places)], refs[len(out_places) :]
    w_refs, refs = refs[: len(w_places)], refs[len(w_places) :]
    d_refs, refs = refs[: len(d_places)], refs[len(d_places) :]
    og_ref, factor_ref, gain_ref, o_ref = refs[:4]
    if first:
        x_ref, h_out, acc_ref, da2_ref, own_ref, send_ref, gd_ref, h_ref = refs[4:12]
        refs = refs[12:]
    else:
        h_ref, acc_in, da2_in = refs[4:7]
        mixed_out, dh_out, do_out, own_ref, send_ref, gd_ref, dgain_ref = refs[8:15]
        acc_ref, da2_ref, acc_old_ref, da2_old_ref, mixed_ref, do_ref = refs[15:21]
        refs = refs[21:]
    wout_ref, w_ref, wd_ref, a2_ref, a2t_ref, dyb_ref, hid_ref, dgu_ref, sems, more_sems = refs
    step = pl.program_id(0)
    steps = pl.num_programs(0)
    length, width = og_ref.shape
    chunk = gd_ref.shape[0]
    side = width // 2
    tile, big = min(256, length), min(1024, length)
    gain = gain_ref[...]
    copy = lambda source, target, number: pltpu.make_async_copy(source, target, more_sems.at[number])
    block_size = wd_ref.shape[0] // inverse_ref.shape[0]
    block_first, block_last = start * chunk // block_size, ((start + count) * chunk - 1) // block_size
    fetch, arrived = natural_copies(wd_ref, d_refs, d_places, inverse_ref, sems, block_first, block_last)

    @pl.when(step == 0)
    def _():
        fetch()
        if not first:
            copy(acc_in, acc_old_ref, 0).start()
            copy(da2_in, da2_old_ref, 1).start()
        natural_rows(wout_ref, out_refs, out_places, inverse_ref)
        for m in range(0, length, tile):
            rows = pl.ds(m, tile)
            if first:
                h = x_ref[rows, :].astype(F32) + dot(o_ref[rows, :], wout_ref[...], NN)
                h_ref[rows, :] = h
                acc_ref[rows, :] = h
            else:
                h = h_ref[rows, :]
                acc_ref[rows, :] = jnp.zeros((tile, width), F32)
            da2_ref[rows, :] = jnp.zeros((tile, width), F32)
            inverse = lax.rsqrt(jnp.mean(h * h, axis=1, keepdims=True) + EPSILON_NORM)
            a2 = (h * inverse * gain).astype(BF)
            a2_ref[rows, :] = a2
            place_rows(a2t_ref, rows, a2, order_ref)
            dyb_ref[rows, :] = (og_ref[rows, :].astype(F32) * factor_ref[rows, :]).astype(BF)
        if first:
            copy(h_ref, h_out, 0).start()

    for block in range(block_first, block_last + 1):

        @pl.when(step == max(0, block * block_size // chunk - start))
        def _():
            arrived(block)

    def one_chunk():
        natural_rows(w_ref, w_refs, w_places, inverse_ref)
        down = wd_ref[pl.ds(pl.multiple_of((start + step) * chunk, chunk), chunk), :]
        for m in range(0, length, big):
            rows = pl.ds(m, big)
            gate = dot(a2_ref[rows, :], w_ref[:, :chunk], NN)
            up = dot(a2_ref[rows, :], w_ref[:, chunk:], NN)
            dhid = dot(dyb_ref[rows, :], down, NT)
            sig = 1.0 / (1.0 + jnp.exp2(gate * -LOG2E))
            act = gate * sig
            hid_ref[rows, :] = (act * up).astype(BF)
            dgu_ref[rows, :chunk] = (dhid * up * (sig + act * (1.0 - sig))).astype(BF)
            dgu_ref[rows, chunk:] = (dhid * act).astype(BF)
        for m in range(0, length, big):
            rows = pl.ds(m, big)
            acc_ref[rows, :] += dot(hid_ref[rows, :], down, NN)
            da2_ref[rows, :] += dot(dgu_ref[rows, :], w_ref[...], NT)
        gd_ref[...] = dot(hid_ref[...], dyb_ref[...], TN).astype(BF)
        own_ref[...] = dot(a2t_ref[:side, :], dgu_ref[...], NN).astype(BF)
        send_ref[...] = dot(a2t_ref[side:, :], dgu_ref[...], NN).astype(BF)

    if first:
        one_chunk()

        @pl.when(step == steps - 1)
        def _():
            copy(h_ref, h_out, 0).wait()

        return
    tail = steps - 2
    pl.when(step < tail)(one_chunk)

    @pl.when(step == tail)
    def _():
        copy(acc_in, acc_old_ref, 0).wait()
        copy(da2_in, da2_old_ref, 1).wait()
        total = jnp.zeros((1, width), F32)
        for m in range(0, length, tile):
            rows = pl.ds(m, tile)
            mixed_ref[rows, :] = (acc_old_ref[rows, :] + acc_ref[rows, :]).astype(BF)
            h = h_ref[rows, :]
            inverse = lax.rsqrt(jnp.mean(h * h, axis=1, keepdims=True) + EPSILON_NORM)
            hat = h * inverse
            da2 = da2_old_ref[rows, :] + da2_ref[rows, :]
            total = total + jnp.sum(da2 * hat, axis=0, keepdims=True)
            scaled = da2 * gain
            dy = og_ref[rows, :].astype(F32) * factor_ref[rows, :]
            dh = dy + inverse * (scaled - hat * jnp.mean(scaled * hat, axis=1, keepdims=True))
            acc_ref[rows, :] = dh
            low = dh.astype(BF)
            dyb_ref[rows, :] = low
            do_ref[rows, :] = dot(low, wout_ref[...], NT).astype(BF)
            place_rows(a2t_ref, rows, o_ref[rows, :], order_ref)
        dgain_ref[...] = total
        copy(mixed_ref, mixed_out, 2).start()
        copy(acc_ref, dh_out, 3).start()
        copy(do_ref, do_out, 4).start()

    for tile_number in range(2):

        @pl.when(step == tail + tile_number)
        def _():
            half = width // 2
            grads = dyb_ref[:, tile_number * half : (tile_number + 1) * half]
            own_ref[...] = dot(a2t_ref[:side, :], grads, NN).astype(BF)
            send_ref[...] = dot(a2t_ref[side:, :], grads, NN).astype(BF)

    @pl.when(step == steps - 1)
    def _():
        copy(mixed_ref, mixed_out, 2).wait()
        copy(acc_ref, dh_out, 3).wait()
        copy(do_ref, do_out, 4).wait()


def feed_forward(order, inverse, start, count, skip, state, x, o, out_grad, factor, gain, out_pieces, pieces, down_pieces):
    length, width = out_grad.shape
    chunk = CHUNK
    first = state is None
    steps = count if first else count + 2
    last = count - 1
    rows = pl.BlockSpec((chunk, width), lambda i, *_: (start + jnp.minimum(i, last), 0))
    columns = pl.BlockSpec((width // 2, TILE), lambda i, *_: (0, i))
    whole = lambda *s: pl.BlockSpec(s, lambda i, *_: (0,) * len(s), pipeline_mode=pl.Buffered(1))
    anywhere = pl.BlockSpec(memory_space=pl.ANY)
    shape = jax.ShapeDtypeStruct
    (outs, out_places), (tiles, w_places), (downs, d_places) = out_pieces, pieces, down_pieces
    big = whole(length, width)
    full, low = pltpu.VMEM((length, width), F32), pltpu.VMEM((length, width), BF)
    scratch = [
        pltpu.VMEM((width, width), BF),
        pltpu.VMEM((width, TILE), BF),
        pltpu.VMEM((FF, width), BF),
        low,
        pltpu.VMEM((width, length), BF),
        low,
        pltpu.VMEM((length, chunk), BF),
        pltpu.VMEM((length, TILE), BF),
        pltpu.SemaphoreType.DMA((inverse.shape[0], 2)),
        pltpu.SemaphoreType.DMA((5,)),
    ]
    in_specs = [whole(*piece.shape[:2], width) for piece in outs]
    in_specs += [
        pl.BlockSpec((*piece.shape[:2], TILE), lambda i, *_: (0, 0, skip + jnp.minimum(i, last))) for piece in tiles
    ]
    in_specs += [anywhere] * len(downs)
    in_specs += [big, whole(length, 1), whole(1, width), big]
    operands = [*outs, *tiles, *downs, out_grad, factor, gain, o]
    halves_out = [shape((width // 2, steps * TILE), BF)] * 2
    aliases = {}
    if first:
        in_specs += [big]
        operands += [x]
        out_specs = [anywhere, big, big, columns, columns, rows]
        out_shape = [shape((length, width), F32)] * 3 + halves_out + [shape((FF, width), BF)]
        scratch = [full] + scratch
    else:
        in_specs += [big, anywhere, anywhere, anywhere]
        operands += list(state)
        out_specs = [anywhere, anywhere, anywhere, columns, columns, rows, whole(1, width)]
        out_shape = [shape((length, width), BF), shape((length, width), F32), shape((length, width), BF)]
        out_shape += halves_out + [shape((FF, width), BF), shape((1, width), F32)]
        scratch = [full, full, full, full, low, low] + scratch
        aliases = {len(operands) + 1: 5}
    return pl.pallas_call(
        functools.partial(feed_forward_kernel, first, start, count, (out_places, w_places, d_places)),
        grid_spec=pltpu.PrefetchScalarGridSpec(
            num_scalar_prefetch=2, grid=(steps,), in_specs=in_specs, out_specs=out_specs, scratch_shapes=scratch
        ),
        out_shape=out_shape,
        input_output_aliases=aliases,
        compiler_params=pltpu.CompilerParams(vmem_limit_bytes=63 * MIB),
        cost_estimate=cost(40),
        name="feed_forward",
    )(order, inverse, *operands)


def unproject_kernel(devices, order_ref, a1_ref, c_ref, dq_ref, dk_ref, dv_ref, wup_ref, dql_ref, own_ref, send_ref, *refs):
    gup_ref, a1t_ref, all_ref = refs if devices else (refs[0], refs[1], None)
    length, width = a1_ref.shape
    half = width // 2
    tile = min(256, length)
    for m in range(0, length, tile):
        place_rows(a1t_ref, pl.ds(m, tile), a1_ref[m : m + tile, :], order_ref)
    for head in range(LATENT_HEADS):
        latent = slice(head * LATENT_WIDTH, (head + 1) * LATENT_WIDTH)
        group = slice(head * GROUP_WIDTH, (head + 1) * GROUP_WIDTH)
        dq, dk, dv = dq_ref[:, group], dk_ref[:, group], dv_ref[:, group]
        dc = (dot(dk, wup_ref[latent, :GROUP_WIDTH], NT) + dot(dv, wup_ref[latent, GROUP_WIDTH:], NT)).astype(BF)
        mine = slice(QUERY_WIDTH + head * LATENT_WIDTH, QUERY_WIDTH + (head + 1) * LATENT_WIDTH)
        dql_ref[:, mine] = dc
        dql_ref[:, group] = dq
        for columns, grad in ((mine, dc), (group, dq)):
            own_ref[:, columns] = dot(a1t_ref[:half, :], grad, NN).astype(BF)
            send_ref[:, columns] = dot(a1t_ref[half:, :], grad, NN).astype(BF)
        turned = c_ref[:, latent].T
        gup_ref[latent, :GROUP_WIDTH] = dot(turned, dk, NN).astype(BF)
        gup_ref[latent, GROUP_WIDTH:] = dot(turned, dv, NN).astype(BF)
    if not devices:
        return
    rows, ups = width // devices, gup_ref.shape[0] // devices
    blocks = order_ref.shape[0]
    line = devices // blocks
    for block in range(blocks):
        for z in range(line):
            device = block * line + z
            for piece in range(gup_ref.shape[1] // TILE):
                start = pl.multiple_of(order_ref[block] * (line * rows) + (z * rows + piece * ups), ups)
                value = gup_ref[device * ups : (device + 1) * ups, piece * TILE : (piece + 1) * TILE]
                all_ref[pl.ds(start, ups), :] = value
    side = dql_ref.shape[1]
    own_ref[:, side:] = all_ref[:half, :]
    send_ref[:, side:] = all_ref[half:, :]


def unproject(devices, order, a1, c, dq, dk, dv, w_up):
    length, width = a1.shape
    latents = LATENT_HEADS * LATENT_WIDTH
    side = QUERY_WIDTH + latents
    operands = (a1, c, dq, dk, dv, w_up)
    both = side + TILE if devices else side
    outs = [(length, side), (width // 2, both), (width // 2, both)]
    scratch = [pltpu.VMEM((width, length), BF)]
    if devices:
        scratch = [pltpu.VMEM(w_up.shape, BF)] + scratch + [pltpu.VMEM((width, TILE), BF)]
    else:
        outs.append(w_up.shape)
    return pl.pallas_call(
        functools.partial(unproject_kernel, devices),
        grid_spec=pltpu.PrefetchScalarGridSpec(
            num_scalar_prefetch=1,
            grid=(1,),
            in_specs=[resident(*a.shape) for a in operands],
            out_specs=[resident(*s) for s in outs],
            scratch_shapes=scratch,
        ),
        out_shape=[jax.ShapeDtypeStruct(s, BF) for s in outs],
        compiler_params=pltpu.CompilerParams(vmem_limit_bytes=60 * MIB),
        cost_estimate=cost(20),
        name="unproject",
    )(order, *operands)


def input_grad_kernel(x_ref, dh_ref, dql_ref, gain_ref, win_ref, out_ref, dgain_ref):
    x = x_ref[...].astype(F32)
    inverse = lax.rsqrt(jnp.mean(x * x, axis=1, keepdims=True) + EPSILON_NORM)
    hat = x * inverse
    da1 = dot(dql_ref[...], win_ref[...], NT)
    part = jnp.sum(da1 * hat, axis=0, keepdims=True)
    scaled = da1 * gain_ref[...].astype(F32)
    out_ref[...] = (
        dh_ref[...] + inverse * (scaled - hat * jnp.mean(scaled * hat, axis=1, keepdims=True))
    ).astype(BF)

    @pl.when(pl.program_id(0) == 0)
    def _():
        dgain_ref[...] = part

    @pl.when(pl.program_id(0) > 0)
    def _():
        dgain_ref[...] += part


def input_grad(x, dh, dql, gain, w_in):
    length, width = x.shape
    tile = min(256, length)
    rows = lambda columns: pl.BlockSpec((tile, columns), lambda i: (i, 0))
    return pl.pallas_call(
        input_grad_kernel,
        grid=(length // tile,),
        in_specs=[rows(width), rows(width), rows(dql.shape[1]), resident(1, width), resident(*w_in.shape)],
        out_specs=[rows(width), resident(1, width)],
        out_shape=[jax.ShapeDtypeStruct((length, width), BF), jax.ShapeDtypeStruct((1, width), F32)],
        compiler_params=pltpu.CompilerParams(vmem_limit_bytes=60 * MIB),
        cost_estimate=cost(20),
        name="input_grad",
    )(x, dh, dql, gain, w_in)


class Ring:
    def __init__(self, data, line):
        self.cores = 2 if data % 2 == 0 else 1
        self.plane, self.line = data // self.cores, line
        place = lax.axis_index("dp")
        self.core, self.at, self.z = place % self.cores, place // self.cores, lax.axis_index("fsdp")

    def partner(self, index, shift, count):
        if count & (count - 1) == 0:
            return index ^ shift
        return (index + shift) % count

    def send_core(self, value):
        swap = [(i, i ^ 1) for i in range(self.plane * 2)]
        return lax.ppermute(value, "dp", swap)

    def send_plane(self, value, shift):
        pairs = [
            (p * self.cores + c, self.partner(p, shift, self.plane) * self.cores + c)
            for p in range(self.plane)
            for c in range(self.cores)
        ]
        return lax.ppermute(value, "dp", pairs)

    def send_line(self, value, shift):
        return lax.ppermute(value, "fsdp", [(i, (i + shift) % self.line) for i in range(self.line)])


def take(array, index, axis):
    return lax.dynamic_index_in_dim(array, index, axis, keepdims=False)


def core_blocks(ring, grad, core):
    rows = grad.shape[0] // (ring.plane * ring.cores * ring.line)
    return take(grad.reshape(ring.plane, ring.cores, ring.line, rows, grad.shape[1]), core, 1)


def total(parts):
    return sum(part.astype(F32) for part in parts)


def core_sends(ring, value):
    return [(ring.send_core, value)]


def plane_sends(ring, parts, relative):
    spot = lambda shift: shift if relative else ring.partner(ring.at, shift, ring.plane)
    block = lambda shift: total([take(part, spot(shift), 0) for part in parts]).astype(BF)
    sends = [
        (lambda value, shift=shift: ring.send_plane(value, shift), block(shift)) for shift in range(1, ring.plane)
    ]
    return block(0), sends


def line_sends(ring, grad, bit, axis=0):
    shape = grad.shape
    pairs = grad.reshape(*shape[:axis], shape[axis] // 2, 2, *shape[axis + 1 :])
    side = (ring.z >> bit) & 1
    swap = [(i, i ^ (1 << bit)) for i in range(ring.line)]
    give = take(pairs, 1 - side, axis + 1).astype(BF)
    return take(pairs, side, axis + 1), [(lambda value: lax.ppermute(value, "fsdp", swap), give)]


def beside(sends, kept, kernel=None, *inputs):
    inputs, gives, kept = together(inputs, [give for _, give in sends], kept)
    received = [send(give) for (send, _), give in zip(sends, gives)]
    return together(kernel(*inputs) if kernel else (), received, kept)


def line_rest(ring, grads, done):
    for bit in range(done, ring.line.bit_length() - 1):
        kept, sends = zip(*(line_sends(ring, grad, bit) for grad in grads))
        _, received, kept = beside([send for one in sends for send in one], kept)
        grads = [total(pair) for pair in zip(kept, received)]
    return [grad[0] for grad in grads]


def halves_order(ring):
    blocks = jnp.arange(ring.plane * ring.cores)
    plane, core = blocks // ring.cores, blocks % ring.cores
    if ring.plane & (ring.plane - 1) == 0:
        shift = plane ^ ring.at
    else:
        shift = (plane - ring.at) % ring.plane
    order = (((core - ring.core) % ring.cores) * ring.plane + shift).astype(jnp.int32)
    shift, core = blocks % ring.plane, blocks // ring.plane
    if ring.plane & (ring.plane - 1) == 0:
        plane = shift ^ ring.at
    else:
        plane = (shift + ring.at) % ring.plane
    inverse = (plane * ring.cores + (core + ring.core) % ring.cores).astype(jnp.int32)
    return order, inverse


class Gather:
    def __init__(self, ring, piece, by_columns=False):
        self.ring, self.by_columns = ring, by_columns
        self.block = piece[None]
        self.bits = list(range(ring.line.bit_length() - 1))[::-1]

    def line_sends(self):
        swap = [(i, i ^ (1 << self.bits[0])) for i in range(self.ring.line)]
        return [(lambda value: lax.ppermute(value, "fsdp", swap), self.block)]

    def line_receive(self, values):
        low = ((self.ring.z >> self.bits.pop(0)) & 1) == 0
        pair = [jnp.where(low, self.block, values[0]), jnp.where(low, values[0], self.block)]
        block = jnp.stack(pair, axis=1)
        self.block = block.reshape(-1, *block.shape[2:])
        if not self.bits:
            self.split()

    def split(self):
        line, rows, columns = self.block.shape
        count = self.ring.plane.bit_length() - 1
        if self.by_columns:
            cut = columns // 2
            halves = [self.block[..., :cut].reshape(1, -1, cut), self.block[..., cut:].reshape(1, -1, cut)]
            self.offsets = [(0, 0), (cut, 0)]
        else:
            whole = self.block.reshape(-1, columns)
            cut = whole.shape[0] // 2
            halves = [whole[None, :cut], whole[None, cut:]]
            self.offsets = [(0, 0), (0, cut)]
        self.halves = [([half], [[0]]) for half in halves]
        self.orders = [list(range(count)), list(range(count))[::-1]]

    def plane_sends(self):
        sends = []
        for (arrays, _), order in zip(self.halves, self.orders):
            value = jnp.concatenate(arrays, axis=0) if len(arrays) > 1 else arrays[0]
            sends.append((lambda value, bit=order[0]: self.ring.send_plane(value, 1 << bit), value))
        return sends

    def plane_receive(self, values):
        for (arrays, shifts), order, value in zip(self.halves, self.orders, values):
            bit = order.pop(0)
            shifts.append([shift ^ (1 << bit) for have in shifts for shift in have])
            arrays.append(value)

    def direct_sends(self):
        self.offsets = [(0, 0)]
        block = self.block.reshape(1, -1, self.block.shape[-1])
        self.halves = [([block], [[0]])]
        return [(lambda value, k=k: self.ring.send_plane(value, k), block) for k in range(1, self.ring.plane)]

    def direct_receive(self, values):
        for shift, value in enumerate(values, 1):
            self.halves[0][0].append(value)
            self.halves[0][1].append([shift])

    def arrays(self):
        return [array for arrays, _ in self.halves for array in arrays]

    def hold(self, arrays):
        arrays = list(arrays)
        for mine, _ in self.halves:
            for number in range(len(mine)):
                mine[number] = arrays.pop(0)

    def places(self, core):
        return [
            (column, [(core * self.ring.plane + shift, row) for shift in have])
            for (_, shifts), (column, row) in zip(self.halves, self.offsets)
            for have in shifts
        ]

    def pieces(self, other):
        if self.ring.cores == 1:
            return self.arrays(), self.places(0)
        return self.arrays() + list(other), self.places(0) + self.places(1)

    def stacked(self):
        blocks = [{}, {}]
        for found, (arrays, shifts) in zip(blocks, self.halves):
            for array, have in zip(arrays, shifts):
                found.update(zip(have, array))
        return jnp.stack([jnp.concatenate([found[k] for found in blocks], axis=0) for k in range(self.ring.plane)])


def natural(ring, mine, other):
    if ring.plane & (ring.plane - 1) == 0:
        shifts = [ring.at ^ at for at in range(ring.plane)]
    else:
        shifts = [(ring.at - at) % ring.plane for at in range(ring.plane)]
    blocks = []
    for shift in shifts:
        pair = [choose(shift, list(part)) for part in (mine, other)][: ring.cores]
        blocks += [choose((core - ring.core) % ring.cores, pair) for core in range(ring.cores)]
    return jnp.stack(blocks)


def choose(index, options):
    result = options[0]
    for number, option in enumerate(options[1:], 1):
        result = jnp.where(index == number, option, result)
    return result


def sum_all(ring, value):
    if ring.cores == 2:
        value = value + ring.send_core(value)
    for count, send in ((ring.plane, ring.send_plane), (ring.line, None)):
        if count & (count - 1):
            return lax.psum(value, AXES)
    shift = 1
    while shift < ring.plane:
        value = value + ring.send_plane(value, shift)
        shift *= 2
    shift = 1
    while shift < ring.line:
        swap = [(i, i ^ shift) for i in range(ring.line)]
        value = value + lax.ppermute(value, "fsdp", swap)
        shift *= 2
    return value


def adamw_kernel(message_ref, dgains_ref, a_ref, b_ref, c_ref, d_ref, *refs):
    masters, firsts, seconds, norm_ref, outs = refs[:6], refs[6:12], refs[12:18], refs[18], refs[19:]
    gains = message_ref[:-8, :]
    norm = jnp.sqrt(message_ref[-1:, :1] + jnp.sum(gains * gains, keepdims=True))
    norm_ref[...] = norm
    clip = jnp.minimum(1.0, MAX_NORM / (norm + 1e-06))

    def update(index, place, grad, rate, decay):
        grad = clip * grad
        master = masters[index][place]
        first_new = BETA_ONE * firsts[index][place] + (1.0 - BETA_ONE) * grad
        second_new = BETA_TWO * seconds[index][place] + (1.0 - BETA_TWO) * grad * grad
        first_hat = first_new / (1.0 - BETA_ONE**STEP)
        second_hat = second_new / (1.0 - BETA_TWO**STEP)
        outs[3 * index][place] = master - rate * (
            first_hat / (jnp.sqrt(second_hat) + EPSILON_ADAM) + decay * master
        )
        outs[3 * index + 1][place] = first_new
        outs[3 * index + 2][place] = second_new

    everything = (slice(None), slice(None))
    side = masters[0].shape[1]
    update(0, everything, c_ref[:, :side], RATE_MATRIX, DECAY_MATRIX)
    rows = masters[1].shape[0]
    for tile in range(masters[1].shape[1] // TILE):
        place = (slice(None), slice(tile * TILE, (tile + 1) * TILE))
        update(1, place, c_ref[tile * rows : (tile + 1) * rows, side:], RATE_MATRIX, DECAY_MATRIX)
    second = FF // CHUNK - FIRST_CHUNKS
    update(2, everything, b_ref[:, second * TILE :], RATE_OUTPUT, DECAY_MATRIX)
    for chunk in range(FF // CHUNK):
        ref, at = (a_ref, chunk) if chunk < FIRST_CHUNKS else (b_ref, chunk - FIRST_CHUNKS)
        for which in range(2):
            place = (slice(None), slice(which * FF + chunk * CHUNK, which * FF + (chunk + 1) * CHUNK))
            start = at * TILE + which * CHUNK
            update(3, place, ref[:, start : start + CHUNK], RATE_MATRIX, DECAY_MATRIX)
    update(4, everything, d_ref[...], RATE_MATRIX, DECAY_MATRIX)
    update(5, everything, dgains_ref[...], RATE_GAIN, 0.0)


def adamw(message, dgains, totals, masters, firsts, seconds):
    shape = jax.ShapeDtypeStruct
    outs = [shape((1, 1), F32)] + [shape(w.shape, F32) for w in masters for _ in range(3)]
    return pl.pallas_call(
        adamw_kernel,
        out_shape=outs,
        compiler_params=pltpu.CompilerParams(vmem_limit_bytes=60 * MIB),
        cost_estimate=cost(5),
        name="adamw",
    )(message, dgains, *totals, *masters, *firsts, *seconds)


def together(*values):
    return lax.optimization_barrier(values)


def shards(data, line, tokens, out_grad, domain_ids, domain_scale, *state):
    masters, moments = state[:6], state[6:]
    firsts, seconds = moments[0::2], moments[1::2]
    ring = Ring(data, line)
    devices = data * line
    length, width = tokens.shape
    p_in, p_up, p_out, p_gate, p_down, p_gains = (w.astype(BF) for w in masters)
    latents = LATENT_HEADS * LATENT_WIDTH
    rows = width // devices
    chunks = FF // CHUNK
    columns = lambda a: a.reshape(a.shape[0], -1, TILE).transpose(1, 0, 2).reshape(-1, TILE)

    tiles = p_gate.reshape(rows, 2, chunks, CHUNK).transpose(0, 2, 1, 3).reshape(rows, -1)
    half = FIRST_CHUNKS
    one = Gather(ring, jnp.concatenate([p_in, columns(p_up).reshape(rows, -1), lane_pad(p_gains, rows)], axis=1))
    two = Gather(ring, jnp.concatenate([p_out, tiles[:, : half * TILE]], axis=1))
    down = Gather(ring, p_down, True)
    three = Gather(ring, tiles[:, half * TILE :])
    order, inverse = halves_order(ring)

    def early(domain_ids):
        picked = domain_ids[:, None] == jnp.arange(NDOM)[None, :]
        factor = jnp.sum(jnp.where(picked, domain_scale[None, :], 0.0), axis=1, keepdims=True)
        return rotation_tables(length), factor

    first = True
    while len(one.bits) > 0:
        if first:
            (tables, factor), received, _ = beside(one.line_sends(), (), early, domain_ids)
        else:
            _, received, _ = beside(one.line_sends(), ())
        first = False
        one.line_receive(received)
    number = 0
    while len(down.bits) > 0 or len(one.orders[0]) > 0:
        sends = one.plane_sends() if len(one.orders[0]) > 0 else []
        split = len(sends)
        sends += down.line_sends() if len(down.bits) > 0 else []
        _, received, kept = beside(sends, one.arrays())
        one.hold(kept)
        if split:
            one.plane_receive(received[:split])
        if len(received) > split:
            down.line_receive(received[split:])
    one_block = one.stacked()
    sends = core_sends(ring, one_block) + down.plane_sends() + two.line_sends()
    _, received, (one_block, kept, tokens) = beside(sends, (one_block, down.arrays(), tokens))
    down.hold(kept)
    one_other = received[0]
    down.plane_receive(received[1:-1])
    two.line_receive(received[-1:])
    while len(down.orders[0]) > 0 or len(two.bits) > 0:
        sends = down.plane_sends() if len(down.orders[0]) > 0 else []
        split = len(sends)
        sends += two.line_sends() if len(two.bits) > 0 else []
        _, received, kept = beside(sends, down.arrays())
        down.hold(kept)
        if split:
            down.plane_receive(received[:split])
        if len(received) > split:
            two.line_receive(received[split:])
    aligned = rows % 32 == 0 and p_up.shape[0] % 16 == 0
    if aligned:
        run = lambda tokens: project(devices, inverse, tokens, tables, one_block, one_other)
    else:
        first = natural(ring, one_block, one_other).reshape(devices, rows, -1)
        w_in = first[:, :, : p_in.shape[1]].reshape(width, -1)
        w_up = first[:, :, p_in.shape[1] : p_in.shape[1] + p_up.size // rows]
        w_up = w_up.reshape(devices, 2 * GROUP_WIDTH // TILE, p_up.shape[0], TILE).transpose(0, 2, 1, 3).reshape(latents, -1)
        gains = first[:, :2, -LANES:][:, :, : p_gains.shape[1]].transpose(1, 0, 2).reshape(2, width).astype(F32)
        run = lambda tokens: (*project(0, inverse, tokens, tables, w_in, w_up, gains), w_in, w_up, gains)
    down_mine = down.arrays()
    down_sends = [send for array in down_mine for send in core_sends(ring, array)]
    cut = 2
    sends = two.plane_sends() + three.line_sends() + down_sends[:cut]
    (a1, q, k, v, c, w_in, w_up, gains), received, kept = beside(sends, (two.arrays(), down_mine), run, tokens)
    two.hold(kept[0])
    down.hold(kept[1])
    down_sends = [(send, array) for (send, _), array in zip(down_sends, kept[1])]
    two.plane_receive(received[:2])
    three.line_receive(received[2:3])
    down_other = list(received[3:])
    sends = two.plane_sends() if len(two.orders[0]) > 0 else []
    split = len(sends)
    sends += three.line_sends() if len(three.bits) > 0 else []
    middle = len(sends)
    sends += down_sends[cut : 2 * cut]
    (o, logs), received, kept = beside(sends, (two.arrays(), down.arrays()), attention, q, k, v)
    two.hold(kept[0])
    down.hold(kept[1])
    down_sends = [(send, array) for (send, _), array in zip(down_sends, kept[1])]
    if split:
        two.plane_receive(received[:split])
    if middle > split:
        three.line_receive(received[split:middle])
    down_other += list(received[middle:])
    while len(two.orders[0]) > 0:
        two.plane_receive(beside(two.plane_sends(), ())[1])
    while len(three.bits) > 0:
        three.line_receive(beside(three.line_sends(), ())[1])
    sends = down_sends[2 * cut :] + [send for array in two.arrays() for send in core_sends(ring, array)]
    split = len(down_sends[2 * cut :])
    _, received, (o, kept, kept_down, kept_other) = beside(sends, (o, two.arrays(), down.arrays(), down_other))
    two.hold(kept)
    down.hold(kept_down)
    down_pieces = down.pieces(list(kept_other) + list(received[:split]))
    two_pieces = two.pieces(received[split:])
    common = (tokens, o, out_grad, factor, gains[1:], two_pieces)
    run = lambda o: feed_forward(
        order, inverse, 0, half, width // TILE, None, tokens, o, out_grad, factor, gains[1:], two_pieces, two_pieces, down_pieces
    )
    (h, acc, da2, own_a, send_a, g_down), received, kept = beside(three.direct_sends(), three.arrays(), run, o)
    three.hold(kept)
    three.direct_receive(received)
    blocks = lambda a: a.reshape(ring.plane, ring.line, rows, -1)
    sends = core_sends(ring, blocks(send_a)) + [send for array in three.arrays() for send in core_sends(ring, array)]
    _, received, (h, own_a, kept) = beside(sends, (h, own_a, three.arrays()))
    three.hold(kept)
    three_pieces = three.pieces(received[1:])
    kept_a, sends = plane_sends(ring, [blocks(own_a), received[0]], True)
    state = (acc, da2, g_down)
    run = lambda h: feed_forward(
        order, inverse, half, chunks - half, 0, (h, *state), *common, three_pieces, down_pieces
    )
    out, received, kept_a = beside(sends, kept_a, run, h)
    mixed, dh, do, own_b, send_b, g_down, dgain_two = out

    def run(g_down, kept_a, *came_a):
        kept_a, send_a = line_sends(ring, total([kept_a, *came_a]), 0)
        return core_blocks(ring, g_down, 1 - ring.core), kept_a, send_a[0][1]

    out, came_b, (do, own_b) = beside(core_sends(ring, blocks(send_b)), (do, own_b), run, g_down, kept_a, *received)
    send_d, kept_a, give_a = out
    kept_b, send_b = plane_sends(ring, [blocks(own_b), *came_b], True)
    sends = send_b + core_sends(ring, send_d) + [(line_sends(ring, give_a, 0)[1][0][0], give_a)]
    run = lambda do: attention_back(40, 0, PAIRS, q, k, v, o, do, logs, tables)
    grads, received, (kept_a, kept_b, g_down) = beside(sends, (kept_a, kept_b, g_down), run, do)
    *came_b, came_d, came_a = received
    halves_d = [jnp.split(part, 2, axis=-1) for part in (core_blocks(ring, g_down, ring.core), came_d)]
    kept_d, send_d = plane_sends(ring, [part[0] for part in halves_d], False)
    kept_e, send_e = line_sends(ring, total([part[1] for part in halves_d]), 0, 1)
    kept_a, send_a = line_sends(ring, total([kept_a, came_a]), 1)

    def run(dq, dk, dv):
        dql, own, send, *g_up = unproject(devices if aligned else 0, order, a1, c, dq, dk, dv, w_up)
        if g_up:
            g_up = g_up[0].reshape(devices, -1, 2 * GROUP_WIDTH // TILE, TILE).transpose(0, 2, 1, 3).reshape(width, -1)
            spots = [jnp.stack([take(core_blocks(ring, g_up, core), ring.partner(ring.at, k, ring.plane), 0)
                                for k in range(ring.plane)]).reshape(width // 2, -1) for core in (ring.core, 1 - ring.core)]
            own, send = jnp.concatenate([own, spots[0]], axis=1), jnp.concatenate([send, spots[1]], axis=1)
        return dql, own, send

    kept = (kept_a, kept_b, kept_d, kept_e, came_b)
    out, received, kept = beside(send_d + send_a + send_e, kept, run, *grads)
    kept_a, kept_b, kept_d, kept_e, came_b = kept
    dql, own_c, send_c = out
    *came_d, came_a, came_e = received
    kept_b, send_b = line_sends(ring, total([kept_b, *came_b]), 0)
    kept_e, send_e = line_sends(ring, total([kept_e, came_e]), 1, 1)
    _, received, kept = beside(
        core_sends(ring, blocks(send_c)) + send_b + send_e, (dql, own_c, kept_a, came_a, kept_b, kept_d, came_d, kept_e)
    )
    dql, own_c, kept_a, came_a, kept_b, kept_d, came_d, kept_e = kept
    came_c, came_b, came_e = received
    kept_a = total([kept_a, came_a])
    kept_c, send_c = plane_sends(ring, [blocks(own_c), came_c], True)
    kept_b, send_b = line_sends(ring, total([kept_b, came_b]), 1)
    kept_d, send_d = line_sends(ring, total([kept_d, *came_d]), 0)
    run = lambda dql: input_grad(tokens, dh, dql, gains[:1], w_in)
    kept = (kept_b, kept_c, kept_d, kept_e, came_e)
    (given, dgain_one), received, kept = beside(send_c + send_d + send_b, kept, run, dql)
    kept_b, kept_c, kept_d, kept_e, came_e = kept
    *came_c, came_d, came_b = received
    kept_b = total([kept_b, came_b])
    sum_e = total([kept_e, came_e])
    for bit in range(2, ring.line.bit_length() - 1):
        kept_e, send_e = line_sends(ring, sum_e, bit, 1)
        sum_e = total([kept_e, beside(send_e, ())[1][0]])
    kept_c, send_c = line_sends(ring, total([kept_c, *came_c]), 0)
    kept_d, send_d = line_sends(ring, total([kept_d, came_d]), 1)
    kept_e, send_e = plane_sends(ring, [sum_e], False)
    _, received, (kept_c, kept_d, kept_e) = beside(send_c + send_d + send_e, (kept_c, kept_d, kept_e))
    came_c, came_d, *came_e = received
    sums = [kept_a, kept_b, total([kept_d, came_d])]
    total_a, total_b, total_d = line_rest(ring, sums, 2)
    (total_c,) = line_rest(ring, [total([kept_c, came_c])], 1)
    total_d = jnp.concatenate([total_d, total([kept_e, *came_e])[0]], axis=-1)

    squares = sum(jnp.sum(grad * grad) for grad in (total_a, total_b, total_c, total_d))
    dgains = jnp.concatenate([dgain_one, dgain_two], axis=0)
    message = jnp.concatenate(
        [dgains.reshape(-1, LANES), jnp.full((8, LANES), squares, F32)], axis=0
    )
    message = sum_all(ring, message)
    share = masters[5].shape[1]
    place = lax.axis_index("dp") * line + lax.axis_index("fsdp")
    dgains = lax.dynamic_slice_in_dim(message[:-8].reshape(2, width), place * share, share, 1)
    totals = (total_a, total_b, total_c, total_d)
    grad_norm, *results = adamw(message, dgains, totals, masters, firsts, seconds)
    return (mixed, given, grad_norm[0, 0], *results)


def lane_pad(gains, rows):
    return jnp.pad(gains, ((0, rows - gains.shape[0]), (0, LANES - gains.shape[1])))


def solution(mesh):
    data, line = mesh.shape["dp"], mesh.shape["fsdp"]
    rows, flat, columns = P(AXES, None), P(AXES), P(None, AXES)

    def run(*arrays):
        return shards(data, line, *arrays)

    return jax.shard_map(
        run,
        mesh=mesh,
        in_specs=(rows, rows, flat, P()) + (rows,) * 5 + (columns,) + (rows,) * 10 + (columns,) * 2,
        out_specs=(rows, rows, P()) + (rows,) * 15 + (columns,) * 3,
        check_vma=False,
    )
```

time: 474 us -> 452 us (0.954); the launches traced: 471 us -> 443 us
  local copies, waits for them, and re-layouts: 54.2 us -> 22.6 us
  starting transfers between devices: 48.3 us -> 73.8 us
  between operations: 20.5 us -> 4.66 us
  waiting for transfers between devices: 122 us -> 110 us
  Pallas kernels: 181 us -> 192 us
    ppermute x15 -> x18, waiting for transfers between devices: 26.9 us -> 72.8 us  [the longest x8 52.9 us: line_sends(): return [(lambda value: lax.ppermute(value, 'fsdp', swap), self.block)]]
    all_gather x1 -> x0, waiting for transfers between devices: 37.6 us -> none  [shards(): lax.all_gather(bundle, AXES, axis=0, tiled=True).reshape(devices, -1, TILE)]
    ppermute x17 -> x32, waiting for transfers between devices: 44.5 us -> 19.5 us  [send_plane(): return lax.ppermute(value, 'dp', pairs)]
    ppermute x17 -> x32, starting transfers between devices: 20.8 us -> 35 us  [send_plane(): return lax.ppermute(value, 'dp', pairs)]
    reshape x6 -> x3, local copies, waits for them, and re-layouts: 14.6 us -> 0.48 us  [the longest x2 0.47 us: shards(): p_gate.reshape(rows, 2, chunks, CHUNK).transpose(0, 2, 1, 3)]
    pallas_call x4 -> x5, Pallas kernels: 113 us -> 125 us  [the longest x2 90.2 us: feed_forward(): pl.pallas_call(functools.partial(feed_forward_kernel, first, start, count...]
    add x1 -> x12, other arithmetic: 0.52 us -> 11.3 us  [the longest x11 10.7 us: total(): return sum((part.astype(F32) for part in parts))]
    convert_element_type x8 -> x4, other arithmetic: 20.1 us -> 9.35 us  [plane_sends(): total([take(part, spot(shift), 0) for part in parts]).astype(BF)]
  transfers between devices with their start and end apart: 41 -> 74, of which waited for: 15 -> 30; matrix products, arithmetic and copies ran while one was open for 11% -> 5% of each run, Pallas kernels for 19% -> 42%
where the time goes in v3:
time: 452 us; the launch traced here: 443 us
  Pallas kernels  192 us (42%)
  waiting for transfers between devices  110 us (24%)
  starting transfers between devices  73.8 us (16%)
  other arithmetic  41.1 us (9%)
  local copies, waits for them, and re-layouts  22.6 us (5%)
  between operations  4.66 us (1%)
    pallas_call x2, Pallas kernels, feed_forward(): pl.pallas_call(functools.partial(feed_forward_kernel, first, start, count...  90.2 us
    ppermute x8, waiting for transfers between devices, line_sends(): return [(lambda value: lax.ppermute(value, 'fsdp', swap), self.block)]  52.9 us
    ppermute x32, starting transfers between devices, send_plane(): return lax.ppermute(value, 'dp', pairs)  35 us
    pallas_call x1, Pallas kernels, attention_back(): pl.pallas_call(attention_back_kernel, grid=(count,), in_specs=[spec] * 5...  32.5 us
    pallas_call x1, Pallas kernels, attention(): pl.pallas_call(attention_kernel, grid=(PAIRS,), in_specs=[spec] * 3, out_...  24.5 us
    ppermute x10, waiting for transfers between devices, line_sends(): lax.ppermute(value, 'fsdp', swap)  19.9 us
    ppermute x32, waiting for transfers between devices, send_plane(): return lax.ppermute(value, 'dp', pairs)  19.5 us
    ppermute x10, starting transfers between devices, line_sends(): lax.ppermute(value, 'fsdp', swap)  17.2 us
  transfers between devices with their start and end apart: 74, of which 30 were waited for; matrix products, arithmetic and copies ran while one was open for 5% of the time, Pallas kernels for 42%

profile of v3, /device:TPU:0, one launch (start us, length us, event | category | flops | bytes accessed | tf_op | source)
XLA Modules:
  0.0 443.4 jit_solution(9199333169196405777)
XLA Ops:
  3.3 4.1 collective-permute-start
  7.4 3.2 fusion.12
  10.7 3.3 collective-permute-done
  14.9 7.1 %collective-permute-done.1 = bf16[2,32,2176]{2,1,0:T(8,128)(2,1)S(1)} collective-permute-done((bf16[2,32,2176]{2,1,0:T(8,128)(2,1)S(1)}, bf16[2,32,2176]{2,1,0:T(8,128)(2,1)S(1)}, u32[]{:S(2)}, u32[]{:S(2)}) %collective-permute-start.1) | collective-permute-done | bytes 278560 | tf_op jit(solution)/shard_map/ppermute | solution.py:731
  25.0 3.3 collective-permute-start.4
  30.1 5.7 %collective-permute-done.4 = bf16[1,88,1024]{2,1,0:T(8,128)(2,1)S(1)} collective-permute-done((bf16[1,88,1024]{2,1,0:T(8,128)(2,1)S(1)}, bf16[1,88,1024]{2,1,0:T(8,128)(2,1)S(1)}, u32[]{:S(2)}, u32[]{:S(2)}) %collective-permute-start.4) | collective-permute-done | bytes 180256 | tf_op jit(solution)/shard_map/ppermute | solution.py:731
  37.9 8.1 %collective-permute-done.7 = bf16[2,88,1024]{2,1,0:T(8,128)(2,1)S(1)} collective-permute-done((bf16[2,88,1024]{2,1,0:T(8,128)(2,1)S(1)}, bf16[2,88,1024]{2,1,0:T(8,128)(2,1)S(1)}, u32[]{:S(2)}, u32[]{:S(2)}) %collective-permute-start.7) | collective-permute-done | bytes 360480 | tf_op jit(solution)/shard_map/ppermute | solution.py:731
  46.0 3.7 collective-permute-done.5
  53.3 15.8 %collective-permute-done.11 = bf16[1,32,4608]{2,1,0:T(8,128)(2,1)S(1)} collective-permute-done((bf16[1,32,4608]{2,1,0:T(8,128)(2,1)S(1)}, bf16[1,32,4608]{2,1,0:T(8,128)(2,1)S(1)}, u32[]{:S(2)}, u32[]{:S(2)}) %collective-permute-start.11) | collective-permute-done | bytes 294944 | tf_op jit(solution)/shard_map/ppermute | solution.py:731
  73.7 12.8 %collective-permute-done.14 = bf16[2,32,4608]{2,1,0:T(8,128)(2,1)} collective-permute-done((bf16[2,32,4608]{2,1,0:T(8,128)(2,1)}, bf16[2,32,4608]{2,1,0:T(8,128)(2,1)}, u32[]{:S(2)}, u32[]{:S(2)}) %collective-permute-start.14) | collective-permute-done | bytes 589856 | tf_op jit(solution)/shard_map/ppermute | solution.py:731
  92.8 13.6 %project.1 = (bf16[1024,1024]{1,0:T(8,128)(2,1)}, bf16[1024,1024]{1,0:T(8,128)(2,1)}, bf16[1024,1024]{1,0:T(8,128)(2,1)}, bf16[1024,1024]{1,0:T(8,128)(2,1)}, bf...) custom-call(s32[8]{0:T(128)} %get-tuple-element.928.refs_0_.inverse_ref, ...), custom_call_target="tpu_custom_call" | custom-call | flops 20000000000 | bytes 1048576 | tf_op jit(solution)/shard_map/project/pallas_call | solution.py:166
  111.5 2.7 collective-permute-start.22
  114.2 24.5 %attention.1 = (bf16[1024,1024]{1,0:T(8,128)(2,1)}, f32[8,2,1024]{2,1,0:T(2,128)}) custom-call(bf16[1024,1024]{1,0:T(8,128)(2,1)} %get-tuple-element.534.q_ref, bf16[1024,1024]{1,0:T(8,128)(2,1)} %get-tuple-element.535.k_ref, bf16[1024,1024]{1,0:T(8,128)(2,1)} %get-tuple-element.536.v_ref), custom_call_target="tpu_custom_call" | custom-call | flops 1000000000 | bytes 1048576 | tf_op jit(solution)/shard_map/attention/pallas_call | solution.py:218
  152.7 51.6 %feed_forward.2 = (f32[1024,1024]{1,0:T(8,128)}, f32[1024,1024]{1,0:T(8,128)}, f32[1024,1024]{1,0:T(8,128)}, bf16[512,3584]{1,0:T(8,128)(2,1)}, bf16[512,3584]{1,0:T(8,128)(2,1)}, /*index=5*/bf16[2816,1024]{1,0:T(8,128)(2,1)}) custom-call(s32[8]{0:T(128)} %get-tuple-element.929.order_ref, s32[8]{0:T(128)} %get-tuple-element.928.refs_0_.inverse_ref, ...), custom_call_target="tpu_custom_call" | custom-call | flops 40000000000 | bytes 1048576 | tf_op jit(solution)/shard_map/feed_forward/pallas_call | solution.py:514
  205.9 6.7 %collective-permute-done.37.refs_16_ = bf16[1,128,2048]{2,1,0:T(8,128)(2,1)S(1)} collective-permute-done((bf16[1,128,2048]{2,1,0:T(8,128)(2,1)}, bf16[1,128,2048]{2,1,0:T(8,128)(2,1)S(1)}, u32[]{:S(2)}, u32[]{:S(2)}) %collective-permute-start.37) | collective-permute-done | bytes 524320 | tf_op jit(solution)/shard_map/ppermute | solution.py:643
  214.2 2.4 fusion.47
  222.4 38.7 %feed_forward.3 = (bf16[1024,1024]{1,0:T(8,128)(2,1)}, f32[1024,1024]{1,0:T(8,128)}, bf16[1024,1024]{1,0:T(8,128)(2,1)}, bf16[512,3072]{1,0:T(8,128)(2,1)}, bf16...) custom-call(s32[8]{0:T(128)} %get-tuple-element.929.order_ref, ...), custom_call_target="tpu_custom_call", output_to_operand_aliasing={{5}: (41, {})} | custom-call | flops 40000000000 | bytes 1048576 | tf_op jit(solution)/shard_map/feed_forward/pallas_call | solution.py:514
  262.7 3.8 dynamic-slice_bitcast_fusion.1
  270.0 4.4 fusion.4
  279.8 32.5 %attention_back.1 = (bf16[1024,1024]{1,0:T(8,128)(2,1)}, bf16[1024,1024]{1,0:T(8,128)(2,1)}, bf16[1024,1024]{1,0:T(8,128)(2,1)}) custom-call(bf16[1024,1024]{1,0:T(8,128)(2,1)} %get-tuple-element.534.q_ref, bf16[1024,1024]{1,0:T(8,128)(2,1)} %get-tuple-element.535.k_ref, bf16[1024,1024]{1,0:T(8,128)(2,1)} %get-tuple-element.536.v_ref, ...), custom_call_target="tpu_custom_call" | custom-call | flops 40000000000 | bytes 1048576 | tf_op jit(solution)/shard_map/attention_back/pallas_call | solution.py:278
  312.6 3.2 dynamic-slice_bitcast_fusion
  326.6 15.4 %unproject.1 = (bf16[1024,1536]{1,0:T(8,128)(2,1)}, bf16[512,2048]{1,0:T(8,128)(2,1)}, bf16[512,2048]{1,0:T(8,128)(2,1)}) custom-call(s32[8]{0:T(128)} %get-tuple-element.929.order_ref, bf16[1024,1024]{1,0:T(8,128)(2,1)} %get-tuple-element.681.a1_ref, bf16[1024,512]{1,0:T(8,128)(2,1)} %get-tuple-element.682.c_ref, ...), custom_call_target="tpu_custom_call" | custom-call | flops 20000000000 | bytes 1048576 | tf_op jit(solution)/shard_map/unproject/pallas_call | solution.py:577
  350.6 16.1 %collective-permute-done.57 = bf16[4,1,88,512]{3,2,1,0:T(8,128)(2,1)S(1)} collective-permute-done((bf16[4,1,88,512]{3,2,1,0:T(8,128)(2,1)S(1)}, bf16[4,1,88,512]{3,2,1,0:T(8,128)(2,1)S(1)}, u32[]{:S(2)}, u32[]{:S(2)}) %collective-permute-start.57) | collective-permute-done | bytes 360480 | tf_op jit(solution)/shard_map/ppermute | solution.py:689
  375.0 3.4 collective-permute-start.62
  380.0 9.7 %input_grad.1 = (bf16[1024,1024]{1,0:T(8,128)(2,1)}, f32[1,1024]{1,0:T(1,128)}) custom-call(bf16[1024,1024]{1,0:T(8,128)(2,1)} %x_ref, f32[1024,1024]{1,0:T(8,128)} %get-tuple-element.680.dh_ref, bf16[1024,1536]{1,0:T(8,128)(2,1)} %get-tuple-element.787.dql_ref, f32[1,1024]{1,0:T(1,128)} %get-tuple-element.921.gain_ref, ...), custom_call_target="tpu_custom_call" | custom-call | flops 20000000000 | bytes 1048576 | tf_op jit(solution)/shard_map/input_grad/pallas_call | solution.py:617
  392.1 5.3 %collective-permute-done.59 = bf16[4,32,2048]{2,1,0:T(8,128)(2,1)} collective-permute-done((bf16[4,32,2048]{2,1,0:T(8,128)(2,1)S(1)}, bf16[4,32,2048]{2,1,0:T(8,128)(2,1)}, u32[]{:S(2)}, u32[]{:S(2)}) %collective-permute-start.59) | collective-permute-done | bytes 524320 | tf_op jit(solution)/shard_map/ppermute | solution.py:651
  400.5 3.1 collective-permute-start.63
  411.3 2.7 collective-permute-start.68
  422.0 2.9 collective-permute-done.70
  425.8 2.8 collective-permute-done.71
  432.3 2.6 collective-permute-start.73
  437.6 5.6 %adamw.1 = (f32[1,1]{1,0:T(1,128)}, f32[32,1536]{1,0:T(8,128)}, f32[32,1536]{1,0:T(8,128)}, f32[32,1536]{1,0:T(8,128)}, f32[16,1024]{1,0:T(8,128)}, /*index=5*/f...) custom-call(f32[24,128]{1,0:T(8,128)} %copy-done.24, ...), custom_call_target="tpu_custom_call" | custom-call | flops 5000000000 | bytes 1048576 | tf_op jit(solution)/shard_map/adamw/pallas_call | solution.py:888
  (324 shorter events, 117.8 us)
Async XLA Ops:
  50.9 18.2 %collective-permute-start.8 = (bf16[4,128,2176]{2,1,0:T(8,128)(2,1)S(1)}, bf16[4,128,2176]{2,1,0:T(8,128)(2,1)S(1)}, u32[]{:S(2)}, u32[]{:S(2)}) collective-permute-start(bf16[4,128,2176]{2,1,0:T(8,128)(2,1)S(1)} %pad_maximum_fusion.refs_2_), channel_id=1, source_target_pairs={{0,4},{4,0},{8,12},{12,8},{16,20},{20,16},{24,28},{28,24},{1,5},{5... | collective-permute-start | bytes 6684680 | tf_op jit(solution)/shard_map/ppermute | solution.py:643
  50.9 18.1 %collective-permute-start.10 = (bf16[1,352,512]{2,1,0:T(8,128)(2,1)S(1)}, bf16[1,352,512]{2,1,0:T(8,128)(2,1)S(1)}, u32[]{:S(2)}, u32[]{:S(2)}) collective-permute-start(bf16[1,352,512]{2,1,0:T(8,128)(2,1)S(1)} %bitcast.300), channel_id=1, source_target_pairs={{0,16},{4,20},{8,24},{12,28},{16,0},{20,4},{24,8},{28,12},{1,17},{... | collective-permute-start | bytes 1081352 | tf_op jit(solution)/shard_map/ppermute | solution.py:651
  70.5 17.2 %collective-permute-start.12 = (bf16[2,352,512]{2,1,0:T(8,128)(2,1)S(1)}, bf16[2,352,512]{2,1,0:T(8,128)(2,1)}, u32[]{:S(2)}, u32[]{:S(2)}) collective-permute-start(bf16[2,352,512]{2,1,0:T(8,128)(2,1)S(1)} %pad_maximum_fusion.4), channel_id=1, source_target_pairs={{0,16},{4,20},{8,24},{12,28},{16,0},{20,4},{24,8},{28,12},{1,17},{... | collective-permute-start | bytes 2162696 | tf_op jit(solution)/shard_map/ppermute | solution.py:651
  71.0 16.9 %collective-permute-start.13 = (bf16[2,352,512]{2,1,0:T(8,128)(2,1)S(1)}, bf16[2,352,512]{2,1,0:T(8,128)(2,1)}, u32[]{:S(2)}, u32[]{:S(2)}) collective-permute-start(bf16[2,352,512]{2,1,0:T(8,128)(2,1)S(1)} %pad_maximum_fusion.5), channel_id=1, source_target_pairs={{0,8},{4,12},{8,0},{12,4},{16,24},{20,28},{24,16},{28,20},{1,9},{5... | collective-permute-start | bytes 2162696 | tf_op jit(solution)/shard_map/ppermute | solution.py:651
  89.2 17.2 %collective-permute-start.15 = (bf16[1,64,4608]{2,1,0:T(8,128)(2,1)S(1)}, bf16[1,64,4608]{2,1,0:T(8,128)(2,1)S(1)}, u32[]{:S(2)}, u32[]{:S(2)}) collective-permute-start(bf16[1,64,4608]{2,1,0:T(8,128)(2,1)S(1)} %bitcast.287), channel_id=1, source_target_pairs={{0,8},{4,12},{8,0},{12,4},{16,24},{20,28},{24,16},{28,20},{1,9},{5... | collective-permute-start | bytes 1769480 | tf_op jit(solution)/shard_map/ppermute | solution.py:651
  109.9 28.8 %collective-permute-start.20 = (bf16[2,64,4608]{2,1,0:T(8,128)(2,1)}, bf16[2,64,4608]{2,1,0:T(8,128)(2,1)}, u32[]{:S(2)}, u32[]{:S(2)}) collective-permute-start(bf16[2,64,4608]{2,1,0:T(8,128)(2,1)} %pad_maximum_fusion.1), channel_id=1, source_target_pairs={{0,16},{4,20},{8,24},{12,28},{16,0},{20,4},{24,8},{28,12},{1,17},{... | collective-permute-start | bytes 3538952 | tf_op jit(solution)/shard_map/ppermute | solution.py:651
  110.4 28.3 %collective-permute-start.21 = (bf16[2,64,4608]{2,1,0:T(8,128)(2,1)S(1)}, bf16[2,64,4608]{2,1,0:T(8,128)(2,1)}, u32[]{:S(2)}, u32[]{:S(2)}) collective-permute-start(bf16[2,64,4608]{2,1,0:T(8,128)(2,1)S(1)} %pad_maximum_fusion.2), channel_id=1, source_target_pairs={{0,8},{4,12},{8,0},{12,4},{16,24},{20,28},{24,16},{28,20},{1,9},{5... | collective-permute-start | bytes 3538952 | tf_op jit(solution)/shard_map/ppermute | solution.py:651
  110.9 27.8 %collective-permute-start.23 = (bf16[2,352,512]{2,1,0:T(8,128)(2,1)}, bf16[2,352,512]{2,1,0:T(8,128)(2,1)}, u32[]{:S(2)}, u32[]{:S(2)}) collective-permute-start(bf16[2,352,512]{2,1,0:T(8,128)(2,1)} %collective-permute-done.12.refs_26_.refs_22_), channel_id=1, source_target_pairs={{0,4},{4,0},{8,12},{12,8},{16,20},{20,16},{24,28},{28,24},{1,5},{5... | collective-permute-start | bytes 2162696 | tf_op jit(solution)/shard_map/ppermute | solution.py:643
  111.0 27.8 %collective-permute-start.24 = (bf16[1,352,512]{2,1,0:T(8,128)(2,1)S(1)}, bf16[1,352,512]{2,1,0:T(8,128)(2,1)}, u32[]{:S(2)}, u32[]{:S(2)}) collective-permute-start(bf16[1,352,512]{2,1,0:T(8,128)(2,1)S(1)} %bitcast.302), channel_id=1, source_target_pairs={{0,4},{4,0},{8,12},{12,8},{16,20},{20,16},{24,28},{28,24},{1,5},{5... | collective-permute-start | bytes 1081352 | tf_op jit(solution)/shard_map/ppermute | solution.py:643
  111.5 27.2 %collective-permute-start.22 = (bf16[2,32,2048]{2,1,0:T(8,128)(2,1)S(1)}, bf16[2,32,2048]{2,1,0:T(8,128)(2,1)S(1)}, u32[]{:S(2)}, u32[]{:S(2)}) collective-permute-start(bf16[2,32,2048]{2,1,0:T(8,128)(2,1)S(1)} %maximum_bitcast_fusion.8), channel_id=1, source_target_pairs={{0,1},{1,0},{2,3},{3,2},{4,5},{5,4},{6,7},{7,6},{8,9},{9,8},{10,11... | collective-permute-start | bytes 786440 | tf_op jit(solution)/shard_map/ppermute | solution.py:731
  149.2 55.1 %collective-permute-start.33 = (bf16[1,128,2048]{2,1,0:T(8,128)(2,1)}, bf16[1,128,2048]{2,1,0:T(8,128)(2,1)S(1)}, u32[]{:S(2)}, u32[]{:S(2)}) collective-permute-start(bf16[1,128,2048]{2,1,0:T(8,128)(2,1)} %bitcast.48.refs_12_), channel_id=1, source_target_pairs={{0,8},{4,12},{8,0},{12,4},{16,24},{20,28},{24,16},{28,20},{1,9},{5... | collective-permute-start | bytes 1572872 | tf_op jit(solution)/shard_map/ppermute | solution.py:651
  150.7 53.6 %collective-permute-start.34 = (bf16[1,128,2048]{2,1,0:T(8,128)(2,1)}, bf16[1,128,2048]{2,1,0:T(8,128)(2,1)}, u32[]{:S(2)}, u32[]{:S(2)}) collective-permute-start(bf16[1,128,2048]{2,1,0:T(8,128)(2,1)} %bitcast.48.refs_12_), channel_id=1, source_target_pairs={{0,16},{4,20},{8,24},{12,28},{16,0},{20,4},{24,8},{28,12},{1,17},{... | collective-permute-start | bytes 1572872 | tf_op jit(solution)/shard_map/ppermute | solution.py:651
  152.2 52.1 %collective-permute-start.35 = (bf16[1,128,2048]{2,1,0:T(8,128)(2,1)}, bf16[1,128,2048]{2,1,0:T(8,128)(2,1)}, u32[]{:S(2)}, u32[]{:S(2)}) collective-permute-start(bf16[1,128,2048]{2,1,0:T(8,128)(2,1)} %bitcast.48.refs_12_), channel_id=1, source_target_pairs={{0,24},{4,28},{8,16},{12,20},{16,8},{20,12},{24,0},{28,4},{1,25},{... | collective-permute-start | bytes 1572872 | tf_op jit(solution)/shard_map/ppermute | solution.py:651
  218.7 42.3 %collective-permute-start.41 = (bf16[4,32,3584]{2,1,0:T(8,128)(2,1)}, bf16[4,32,3584]{2,1,0:T(8,128)(2,1)}, u32[]{:S(2)}, u32[]{:S(2)}) collective-permute-start(bf16[4,32,3584]{2,1,0:T(8,128)(2,1)} %get-tuple-element.675), channel_id=1, source_target_pairs={{0,8},{4,12},{8,0},{12,4},{16,24},{20,28},{24,16},{28,20},{1,9},{5... | collective-permute-start | bytes 2752520 | tf_op jit(solution)/shard_map/ppermute | solution.py:651
  220.4 42.3 %collective-permute-start.42 = (bf16[4,32,3584]{2,1,0:T(8,128)(2,1)}, bf16[4,32,3584]{2,1,0:T(8,128)(2,1)}, u32[]{:S(2)}, u32[]{:S(2)}) collective-permute-start(bf16[4,32,3584]{2,1,0:T(8,128)(2,1)} %get-tuple-element.676), channel_id=1, source_target_pairs={{0,16},{4,20},{8,24},{12,28},{16,0},{20,4},{24,8},{28,12},{1,17},{... | collective-permute-start | bytes 2752520 | tf_op jit(solution)/shard_map/ppermute | solution.py:651
  222.4 40.3 %collective-permute-start.43 = (bf16[4,32,3584]{2,1,0:T(8,128)(2,1)}, bf16[4,32,3584]{2,1,0:T(8,128)(2,1)}, u32[]{:S(2)}, u32[]{:S(2)}) collective-permute-start(bf16[4,32,3584]{2,1,0:T(8,128)(2,1)} %get-tuple-element.677), channel_id=1, source_target_pairs={{0,24},{4,28},{8,16},{12,20},{16,8},{20,12},{24,0},{28,4},{1,25},{... | collective-permute-start | bytes 2752520 | tf_op jit(solution)/shard_map/ppermute | solution.py:651
  274.3 38.3 %collective-permute-start.48 = (bf16[4,4,88,1024]{3,2,1,0:T(8,128)(2,1)}, bf16[4,4,88,1024]{3,2,1,0:T(8,128)(2,1)S(1)}, u32[]{:S(2)}, u32[]{:S(2)}) collective-permute-start(bf16[4,4,88,1024]{3,2,1,0:T(8,128)(2,1)} %dynamic-slice_bitcast_fusion.1), channel_id=1, source_target_pairs={{0,4},{4,0},{8,12},{12,8},{16,20},{20,16},{24,28},{28,24},{1,5},{5... | collective-permute-start | bytes 8650760 | tf_op jit(solution)/shard_map/ppermute | solution.py:643
  274.8 37.5 %collective-permute-start.45 = (bf16[4,32,3072]{2,1,0:T(8,128)(2,1)}, bf16[4,32,3072]{2,1,0:T(8,128)(2,1)}, u32[]{:S(2)}, u32[]{:S(2)}) collective-permute-start(bf16[4,32,3072]{2,1,0:T(8,128)(2,1)} %get-tuple-element.710), channel_id=1, source_target_pairs={{0,8},{4,12},{8,0},{12,4},{16,24},{20,28},{24,16},{28,20},{1,9},{5... | collective-permute-start | bytes 2359304 | tf_op jit(solution)/shard_map/ppermute | solution.py:651
  276.3 36.1 %collective-permute-start.46 = (bf16[4,32,3072]{2,1,0:T(8,128)(2,1)}, bf16[4,32,3072]{2,1,0:T(8,128)(2,1)}, u32[]{:S(2)}, u32[]{:S(2)}) collective-permute-start(bf16[4,32,3072]{2,1,0:T(8,128)(2,1)} %get-tuple-element.711), channel_id=1, source_target_pairs={{0,16},{4,20},{8,24},{12,28},{16,0},{20,4},{24,8},{28,12},{1,17},{... | collective-permute-start | bytes 2359304 | tf_op jit(solution)/shard_map/ppermute | solution.py:651
  276.9 35.8 %collective-permute-start.47 = (bf16[4,32,3072]{2,1,0:T(8,128)(2,1)}, bf16[4,32,3072]{2,1,0:T(8,128)(2,1)}, u32[]{:S(2)}, u32[]{:S(2)}) collective-permute-start(bf16[4,32,3072]{2,1,0:T(8,128)(2,1)} %get-tuple-element.712), channel_id=1, source_target_pairs={{0,24},{4,28},{8,16},{12,20},{16,8},{20,12},{24,0},{28,4},{1,25},{... | collective-permute-start | bytes 2359304 | tf_op jit(solution)/shard_map/ppermute | solution.py:651
  278.3 34.0 %collective-permute-start.49 = (bf16[2,32,3584]{2,1,0:T(8,128)(2,1)}, bf16[2,32,3584]{2,1,0:T(8,128)(2,1)}, u32[]{:S(2)}, u32[]{:S(2)}) collective-permute-start(bf16[2,32,3584]{2,1,0:T(8,128)(2,1)} %fusion.17), channel_id=1, source_target_pairs={{0,1},{1,0},{2,3},{3,2},{4,5},{5,4},{6,7},{7,6},{8,9},{9,8},{10,11... | collective-permute-start | bytes 1376264 | tf_op jit(solution)/shard_map/ppermute | solution.py:689
  320.9 22.3 %collective-permute-start.54 = (bf16[4,2,88,512]{3,2,1,0:T(8,128)(2,1)}, bf16[4,2,88,512]{3,2,1,0:T(8,128)(2,1)S(1)}, u32[]{:S(2)}, u32[]{:S(2)}) collective-permute-start(bf16[4,2,88,512]{3,2,1,0:T(8,128)(2,1)} %fusion.14), channel_id=1, source_target_pairs={{0,1},{1,0},{2,3},{3,2},{4,5},{5,4},{6,7},{7,6},{8,9},{9,8},{10,11... | collective-permute-start | bytes 2162696 | tf_op jit(solution)/shard_map/ppermute | solution.py:689
  321.7 20.3 %collective-permute-start.50 = (bf16[4,88,512]{2,1,0:T(8,128)(2,1)}, bf16[4,88,512]{2,1,0:T(8,128)(2,1)S(1)}, u32[]{:S(2)}, u32[]{:S(2)}) collective-permute-start(bf16[4,88,512]{2,1,0:T(8,128)(2,1)} %get-tuple-element.736), channel_id=1, source_target_pairs={{0,8},{4,12},{8,0},{12,4},{16,24},{20,28},{24,16},{28,20},{1,9},{5... | collective-permute-start | bytes 1081352 | tf_op jit(solution)/shard_map/ppermute | solution.py:651
  322.9 19.1 %collective-permute-start.51 = (bf16[4,88,512]{2,1,0:T(8,128)(2,1)}, bf16[4,88,512]{2,1,0:T(8,128)(2,1)S(1)}, u32[]{:S(2)}, u32[]{:S(2)}) collective-permute-start(bf16[4,88,512]{2,1,0:T(8,128)(2,1)} %get-tuple-element.737), channel_id=1, source_target_pairs={{0,16},{4,20},{8,24},{12,28},{16,0},{20,4},{24,8},{28,12},{1,17},{... | collective-permute-start | bytes 1081352 | tf_op jit(solution)/shard_map/ppermute | solution.py:651
  324.0 18.0 %collective-permute-start.52 = (bf16[4,88,512]{2,1,0:T(8,128)(2,1)}, bf16[4,88,512]{2,1,0:T(8,128)(2,1)}, u32[]{:S(2)}, u32[]{:S(2)}) collective-permute-start(bf16[4,88,512]{2,1,0:T(8,128)(2,1)} %get-tuple-element.738), channel_id=1, source_target_pairs={{0,24},{4,28},{8,16},{12,20},{16,8},{20,12},{24,0},{28,4},{1,25},{... | collective-permute-start | bytes 1081352 | tf_op jit(solution)/shard_map/ppermute | solution.py:651
  348.2 19.3 %collective-permute-start.55 = (bf16[4,4,32,2048]{3,2,1,0:T(8,128)(2,1)S(1)}, bf16[4,4,32,2048]{3,2,1,0:T(8,128)(2,1)S(1)}, u32[]{:S(2)}, u32[]{:S(2)}) collective-permute-start(bf16[4,4,32,2048]{3,2,1,0:T(8,128)(2,1)S(1)} %bitcast.318), channel_id=1, source_target_pairs={{0,4},{4,0},{8,12},{12,8},{16,20},{20,16},{24,28},{28,24},{1,5},{5... | collective-permute-start | bytes 6291464 | tf_op jit(solution)/shard_map/ppermute | solution.py:643
  348.2 19.3 %collective-permute-start.56 = (bf16[2,32,3072]{2,1,0:T(8,128)(2,1)S(1)}, bf16[2,32,3072]{2,1,0:T(8,128)(2,1)S(1)}, u32[]{:S(2)}, u32[]{:S(2)}) collective-permute-start(bf16[2,32,3072]{2,1,0:T(8,128)(2,1)S(1)} %fusion.18), channel_id=1, source_target_pairs={{0,1},{1,0},{2,3},{3,2},{4,5},{5,4},{6,7},{7,6},{8,9},{9,8},{10,11... | collective-permute-start | bytes 1179656 | tf_op jit(solution)/shard_map/ppermute | solution.py:689
  349.9 16.8 %collective-permute-start.57 = (bf16[4,1,88,512]{3,2,1,0:T(8,128)(2,1)S(1)}, bf16[4,1,88,512]{3,2,1,0:T(8,128)(2,1)S(1)}, u32[]{:S(2)}, u32[]{:S(2)}) collective-permute-start(bf16[4,1,88,512]{3,2,1,0:T(8,128)(2,1)S(1)} %dynamic-slice_convert_fusion), channel_id=1, source_target_pairs={{0,2},{1,3},{2,0},{3,1},{4,6},{5,7},{6,4},{7,5},{8,10},{9,11},{10,... | collective-permute-start | bytes 1081352 | tf_op jit(solution)/shard_map/ppermute | solution.py:689
  371.5 20.6 %collective-permute-start.58 = (bf16[4,32,2048]{2,1,0:T(8,128)(2,1)}, bf16[4,32,2048]{2,1,0:T(8,128)(2,1)}, u32[]{:S(2)}, u32[]{:S(2)}) collective-permute-start(bf16[4,32,2048]{2,1,0:T(8,128)(2,1)} %get-tuple-element.791), channel_id=1, source_target_pairs={{0,8},{4,12},{8,0},{12,4},{16,24},{20,28},{24,16},{28,20},{1,9},{5... | collective-permute-start | bytes 1572872 | tf_op jit(solution)/shard_map/ppermute | solution.py:651
  372.6 24.8 %collective-permute-start.59 = (bf16[4,32,2048]{2,1,0:T(8,128)(2,1)S(1)}, bf16[4,32,2048]{2,1,0:T(8,128)(2,1)}, u32[]{:S(2)}, u32[]{:S(2)}) collective-permute-start(bf16[4,32,2048]{2,1,0:T(8,128)(2,1)S(1)} %get-tuple-element.792), channel_id=1, source_target_pairs={{0,16},{4,20},{8,24},{12,28},{16,0},{20,4},{24,8},{28,12},{1,17},{... | collective-permute-start | bytes 1572872 | tf_op jit(solution)/shard_map/ppermute | solution.py:651
  373.3 24.1 %collective-permute-start.60 = (bf16[4,32,2048]{2,1,0:T(8,128)(2,1)S(1)}, bf16[4,32,2048]{2,1,0:T(8,128)(2,1)}, u32[]{:S(2)}, u32[]{:S(2)}) collective-permute-start(bf16[4,32,2048]{2,1,0:T(8,128)(2,1)S(1)} %get-tuple-element.793), channel_id=1, source_target_pairs={{0,24},{4,28},{8,16},{12,20},{16,8},{20,12},{24,0},{28,4},{1,25},{... | collective-permute-start | bytes 1572872 | tf_op jit(solution)/shard_map/ppermute | solution.py:651
  375.0 17.1 %collective-permute-start.62 = (bf16[1,32,3072]{2,1,0:T(8,128)(2,1)S(1)}, bf16[1,32,3072]{2,1,0:T(8,128)(2,1)S(1)}, u32[]{:S(2)}, u32[]{:S(2)}) collective-permute-start(bf16[1,32,3072]{2,1,0:T(8,128)(2,1)S(1)} %dynamic-slice_convert_fusion.2), channel_id=1, source_target_pairs={{0,2},{1,3},{2,0},{3,1},{4,6},{5,7},{6,4},{7,5},{8,10},{9,11},{10,... | collective-permute-start | bytes 589832 | tf_op jit(solution)/shard_map/ppermute | solution.py:689
  (86 other events, 850.8 us)
